TPU v7x, 32 devices: a whole 2x2x4 slice. The times are simulated.
32 devices in a mesh: dp: 2 (over y), seq: 16 (over z, x, core).
Axes of the slice: x: 2, y: 2, z: 4, core: 2. Of those that a mesh axis runs over, the one named last changes fastest.
Arguments:
- enc_input: bfloat16 [2, 6144, 768], P('dp', 'seq'), may hold values from -6 to 6
- dec_input: bfloat16 [2, 1536, 768], P('dp', 'seq'), may hold values from -6 to 6
- passage_ids: int32 [2, 6144], P('dp'), may hold values from 0 to 39, never falling along the last dimension, each value on 1 to 384 neighbouring positions
- target_lengths: int32 [2, 2], P('dp'), may hold values from 256 to 768, as said below
- cotangent: bfloat16 [2, 1536, 768], P('dp', 'seq'), may hold values from -6 to 6
- enc_gains: float32 [2, 768], replicated, may hold values from 0.5 to 1.5
- enc_qkv: float32 [3, 768, 768], P(None, 'seq', 'dp'), may hold values from -0.21875 to 0.21875
- enc_out: float32 [768, 768], P('seq', 'dp'), may hold values from -0.4375 to 0.4375
- rel_table: float32 [32, 12], replicated, may hold values from -2 to 2
- enc_up: float32 [768, 3072], P('seq', 'dp'), may hold values from -0.21875 to 0.21875
- enc_down: float32 [3072, 768], P('seq', 'dp'), may hold values from -0.109375 to 0.109375
- dec_gains: float32 [3, 768], replicated, may hold values from 0.5 to 1.5
- self_qkv: float32 [3, 768, 768], P(None, 'seq', 'dp'), may hold values from -0.21875 to 0.21875
- self_out: float32 [768, 768], P('seq', 'dp'), may hold values from -0.4375 to 0.4375
- cross_qkv: float32 [3, 768, 768], P(None, 'seq', 'dp'), may hold values from -0.21875 to 0.21875
- cross_out: float32 [768, 768], P('seq', 'dp'), may hold values from -0.625 to 0.625
- dec_up: float32 [768, 3072], P('seq', 'dp'), may hold values from -0.21875 to 0.21875
- dec_down: float32 [3072, 768], P('seq', 'dp'), may hold values from -0.109375 to 0.109375
Outputs:
- dec_output: bfloat16 [2, 1536, 768], P('dp', 'seq')
- enc_input_grad: float32 [2, 6144, 768], P('dp', 'seq')
- dec_input_grad: float32 [2, 1536, 768], P('dp', 'seq')
- enc_gains_grad: float32 [2, 768], replicated
- enc_qkv_grad: float32 [3, 768, 768], P(None, 'seq', 'dp')
- enc_out_grad: float32 [768, 768], P('seq', 'dp')
- rel_table_grad: float32 [32, 12], replicated
- enc_up_grad: float32 [768, 3072], P('seq', 'dp')
- enc_down_grad: float32 [3072, 768], P('seq', 'dp')
- dec_gains_grad: float32 [3, 768], replicated
- self_qkv_grad: float32 [3, 768, 768], P(None, 'seq', 'dp')
- self_out_grad: float32 [768, 768], P('seq', 'dp')
- cross_qkv_grad: float32 [3, 768, 768], P(None, 'seq', 'dp')
- cross_out_grad: float32 [768, 768], P('seq', 'dp')
- dec_up_grad: float32 [768, 3072], P('seq', 'dp')
- dec_down_grad: float32 [3072, 768], P('seq', 'dp')
Inputs may be any that keep to these rules, and one draw needn't show every extreme that they name: `passage_ids`: per index of dp, the ids number 2 * 20 passages in order along the tokens, each of 1 to 384 tokens with one of exactly 384; passage id // 20 is its query. `target_lengths`: multiples of 256; in each row exactly one query has length 768, the others less.
All inputs are finite; a program needn't handle non-finite values.
Results may differ from a plain program's by a relative error of at most 0.03.
Values may be sent and summed in bfloat16 or wider, within the bound.
A program may use at most 320 MiB of HBM per device.

v0:
```python
import jax
import jax.numpy as jnp
from jax import lax
from jax.sharding import PartitionSpec as P

D = 768
HEADS = 12
HD = 64
BUCKETS = 32
PASS = 384
PASS_N = 20
TGT = 768


EPSILON = 1e-06
PRECISE = lax.Precision.HIGHEST
LIMITS = (12, 16, 23, 32, 46, 64, 91)
NEGATIVE = -1e30


def with_halo(block, sides, width):
    for axis, dim in sides:
        count = lax.axis_size(axis)
        forward = [(i, i + 1) for i in range(count - 1)]
        backward = [(target, source) for source, target in forward]
        low = lax.ppermute(
            lax.slice_in_dim(block, block.shape[dim] - width, None, axis=dim), axis, forward
        )
        high = lax.ppermute(lax.slice_in_dim(block, 0, width, axis=dim), axis, backward)
        block = jnp.concatenate([low, block, high], axis=dim)
    return block


def passed_along(block, axis, distance):
    devices = range(lax.axis_size(axis))
    route = [(i - distance, i) for i in devices if i - distance in devices]
    return lax.ppermute(block, axis, route)


def shifted(block, axis, distance):
    devices = range(lax.axis_size(axis))
    route = [((i - distance) % len(devices), i) for i in devices]
    return lax.ppermute(block, axis, route)


def bucket_of(distance):
    forward_half = (distance > 0).astype(jnp.int32) * 16
    distance_abs = jnp.abs(distance)
    far_bucket = jnp.full(distance_abs.shape, 8, jnp.int32)
    for threshold in LIMITS:
        far_bucket = far_bucket + (distance_abs >= threshold).astype(jnp.int32)
    return forward_half + jnp.where(distance_abs < 8, distance_abs, far_bucket)


def norm_apply(values, gain_row):
    return (
        values * lax.rsqrt(jnp.mean(values * values, axis=-1, keepdims=True) + EPSILON) * gain_row
    )


def norm_back(values, gain_row, gradient):
    unused, pullback = jax.vjp(norm_apply, values, gain_row)
    return pullback(gradient)


def gelu_back(inner_act, gradient):
    unused, pullback = jax.vjp(jax.nn.gelu, inner_act)
    return pullback(gradient)[0]


def matmul(left_side, right_side):
    return jnp.dot(left_side, right_side, preferred_element_type=jnp.float32)


def grad_of(left_side, right_side):
    return lax.dot_general(
        left_side, right_side, (((0,), (0,)), ((), ())), preferred_element_type=jnp.float32
    )


def back_of(gradient, weight):
    return lax.dot_general(
        gradient, weight, (((1,), (1,)), ((), ())), preferred_element_type=jnp.float32
    )


def heads_of(values):
    return values.reshape(values.shape[0], HEADS, HD)


def toeplitz_table(row_count, key_span):
    period = row_count + key_span
    offsets = jnp.arange(period, dtype=jnp.int32)
    distance = jnp.where(offsets < key_span, offsets - PASS, offsets - period - PASS)
    onehot = (bucket_of(distance)[:, None] == jnp.arange(BUCKETS, dtype=jnp.int32)[None, :]).astype(
        jnp.float32
    )
    return (onehot, period)


def bias_matrix(table_part, onehot, row_count, key_span, period):
    line = jnp.einsum("tb,bh->ht", onehot, table_part, precision=PRECISE)
    flat = jnp.tile(line, (1, row_count))[:, : row_count * (period - 1)]
    return flat.reshape(line.shape[0], row_count, period - 1)[:, :, :key_span]


def bias_back(grad_bias, onehot, row_count, key_span, period):
    padded = jnp.pad(grad_bias, ((0, 0), (0, 0), (0, period - 1 - key_span)))
    flat = padded.reshape(padded.shape[0], row_count * (period - 1))
    flat = jnp.pad(flat, ((0, 0), (0, row_count)))
    line = jnp.sum(flat.reshape(flat.shape[0], row_count, period), axis=1)
    return jnp.einsum("tb,ht->bh", onehot, line, precision=PRECISE)


def place_blocks(own, fetch, group_size, group_rel):
    blocks = jnp.zeros((own.shape[0], group_size) + own.shape[1:], own.dtype)
    blocks = lax.dynamic_update_index_in_dim(blocks, own, group_rel, 1)
    for distance in range(1, group_size):
        piece = fetch(own, distance)
        target = jnp.maximum(group_rel - distance, 0)
        updated = lax.dynamic_update_index_in_dim(blocks, piece, target, 1)
        blocks = jnp.where(group_rel - distance >= 0, updated, blocks)
    return blocks.reshape(own.shape[0], group_size * own.shape[1], own.shape[2])


def attend_full(queries, key_rows, value_rows, allowed, bias_add):
    scores = (
        jnp.einsum("rhd,khd->hrk", queries, key_rows, preferred_element_type=jnp.float32) * 0.125
        + bias_add
    )
    scores = jnp.where(allowed[None], scores, NEGATIVE)
    peak_score = jnp.max(scores, axis=-1, keepdims=True)
    exp_scores = jnp.exp(scores - peak_score)
    totals = jnp.sum(exp_scores, axis=-1, keepdims=True)
    weights = (exp_scores / totals).astype(jnp.bfloat16)
    mixture = jnp.einsum("hrk,khd->rhd", weights, value_rows, preferred_element_type=jnp.float32)
    return (mixture, (peak_score + jnp.log(totals))[..., 0])


def attend_step(queries, key_rows, value_rows, allowed, running):
    peak_run, total_run, mix_run = running
    scores = (
        jnp.einsum("rhd,khd->hrk", queries, key_rows, preferred_element_type=jnp.float32) * 0.125
    )
    scores = jnp.where(allowed[None], scores, NEGATIVE)
    new_peak = jnp.maximum(peak_run, jnp.max(scores, axis=-1))
    rescale = jnp.exp(peak_run - new_peak)
    exp_scores = jnp.where(allowed[None], jnp.exp(scores - new_peak[..., None]), 0.0)
    total_run = total_run * rescale + jnp.sum(exp_scores, axis=-1)
    added = jnp.einsum(
        "hrk,khd->rhd",
        exp_scores.astype(jnp.bfloat16),
        value_rows,
        preferred_element_type=jnp.float32,
    )
    mix_run = mix_run * rescale.T[:, :, None] + added
    return (new_peak, total_run, mix_run)


def attend_back(queries, key_rows, value_rows, allowed, bias_add, logsum, grad_out, row_dot):
    scores = (
        jnp.einsum("rhd,khd->hrk", queries, key_rows, preferred_element_type=jnp.float32) * 0.125
        + bias_add
    )
    scores = jnp.where(allowed[None], scores, NEGATIVE)
    weights = jnp.exp(scores - logsum[..., None])
    grad_values = jnp.einsum(
        "hrk,rhd->khd", weights.astype(jnp.bfloat16), grad_out, preferred_element_type=jnp.float32
    )
    grad_weights = jnp.einsum(
        "rhd,khd->hrk", grad_out, value_rows, preferred_element_type=jnp.float32
    )
    grad_scores = weights * (grad_weights - row_dot[..., None])
    rounded = grad_scores.astype(jnp.bfloat16)
    grad_queries = (
        jnp.einsum("hrk,khd->rhd", rounded, key_rows, preferred_element_type=jnp.float32) * 0.125
    )
    grad_keys = (
        jnp.einsum("hrk,rhd->khd", rounded, queries, preferred_element_type=jnp.float32) * 0.125
    )
    return (grad_queries, grad_keys, grad_values, grad_scores)


def per_device(
    enc_input,
    dec_input,
    passage_ids,
    target_lengths,
    cotangent,
    enc_gains,
    enc_qkv,
    enc_out,
    rel_table,
    enc_up,
    enc_down,
    dec_gains,
    self_qkv,
    self_out,
    cross_qkv,
    cross_out,
    dec_up,
    dec_down,
):
    bf16 = jnp.bfloat16
    f32 = jnp.float32
    (
        enc_qkv_part,
        enc_out_part,
        enc_up_part,
        enc_down_part,
        self_qkv_part,
        self_out_part,
        cross_qkv_part,
        cross_out_part,
        dec_up_part,
        dec_down_part,
    ) = (
        lax.all_gather(enc_qkv.astype(bf16), "seq", axis=1, tiled=True),
        lax.all_gather(enc_out.astype(bf16), "seq", axis=0, tiled=True),
        lax.all_gather(enc_up.astype(bf16), "seq", axis=0, tiled=True),
        lax.all_gather(enc_down.astype(bf16), "seq", axis=0, tiled=True),
        lax.all_gather(self_qkv.astype(bf16), "seq", axis=1, tiled=True),
        lax.all_gather(self_out.astype(bf16), "seq", axis=0, tiled=True),
        lax.all_gather(cross_qkv.astype(bf16), "seq", axis=1, tiled=True),
        lax.all_gather(cross_out.astype(bf16), "seq", axis=0, tiled=True),
        lax.all_gather(dec_up.astype(bf16), "seq", axis=0, tiled=True),
        lax.all_gather(dec_down.astype(bf16), "seq", axis=0, tiled=True),
    )
    (
        enc_qkv_w,
        enc_out_w,
        enc_up_w,
        enc_down_w,
        self_qkv_w,
        self_out_w,
        cross_qkv_w,
        cross_out_w,
        dec_up_w,
        dec_down_w,
    ) = (
        lax.all_gather(enc_qkv_part, "dp", axis=2, tiled=True),
        lax.all_gather(enc_out_part, "dp", axis=1, tiled=True),
        lax.all_gather(enc_up_part, "dp", axis=1, tiled=True),
        lax.all_gather(enc_down_part, "dp", axis=1, tiled=True),
        lax.all_gather(self_qkv_part, "dp", axis=2, tiled=True),
        lax.all_gather(self_out_part, "dp", axis=1, tiled=True),
        lax.all_gather(cross_qkv_part, "dp", axis=2, tiled=True),
        lax.all_gather(cross_out_part, "dp", axis=1, tiled=True),
        lax.all_gather(dec_up_part, "dp", axis=1, tiled=True),
        lax.all_gather(dec_down_part, "dp", axis=1, tiled=True),
    )
    enc_gains_w = enc_gains.astype(bf16)
    dec_gains_w = dec_gains.astype(bf16)
    seq_index = lax.axis_index("seq")
    seq_count = lax.axis_size("seq")
    tokens = enc_input[0].astype(f32)
    row_count = tokens.shape[0]
    key_span = row_count + 2 * PASS
    passage = passage_ids[0]
    lengths = target_lengths[0]
    row_ids = lax.dynamic_slice_in_dim(passage, seq_index * row_count, row_count)
    key_ids = lax.dynamic_slice_in_dim(
        jnp.pad(passage, (PASS, PASS), constant_values=-1), seq_index * row_count, key_span
    )
    enc_allowed = row_ids[:, None] == key_ids[None, :]
    onehot, period = toeplitz_table(row_count, key_span)
    enc_gain_one = enc_gains_w[0].astype(f32)
    enc_gain_two = enc_gains_w[1].astype(f32)
    normed_one = norm_apply(tokens, enc_gain_one).astype(bf16)
    enc_proj = jnp.einsum("rd,cde->cre", normed_one, enc_qkv_w, preferred_element_type=f32).astype(
        bf16
    )
    enc_near = with_halo(enc_proj[1:], (("seq", 1),), PASS)
    enc_queries = heads_of(enc_proj[0])
    enc_keys = heads_of(enc_near[0])
    enc_values = heads_of(enc_near[1])
    mixtures = []
    logsums = []
    for head_first in range(0, HEADS, 4):
        head_part = slice(head_first, head_first + 4)
        bias_part = bias_matrix(rel_table[:, head_part], onehot, row_count, key_span, period)
        mixture, logsum = attend_full(
            enc_queries[:, head_part],
            enc_keys[:, head_part],
            enc_values[:, head_part],
            enc_allowed,
            bias_part,
        )
        mixtures.append(mixture)
        logsums.append(logsum)
    enc_mixture = jnp.concatenate(mixtures, axis=1)
    enc_logsum = jnp.concatenate(logsums, axis=0)
    enc_mixed_b = enc_mixture.reshape(row_count, D).astype(bf16)
    enc_hidden = tokens + matmul(enc_mixed_b, enc_out_w)
    normed_two = norm_apply(enc_hidden, enc_gain_two).astype(bf16)
    enc_inner = matmul(normed_two, enc_up_w)
    enc_active = jax.nn.gelu(enc_inner).astype(bf16)
    encoded = enc_hidden + matmul(enc_active, enc_down_w)
    encoded_b = encoded.astype(bf16)
    cross_kv = jnp.einsum(
        "rd,cde->cre", encoded_b, cross_qkv_w[1:], preferred_element_type=f32
    ).astype(bf16)
    cross_keys_h = heads_of(cross_kv[0])
    cross_values_h = heads_of(cross_kv[1])
    key_owner = row_ids // PASS_N
    dec_tokens = dec_input[0].astype(f32)
    dec_rows = dec_tokens.shape[0]
    dec_total = dec_rows * seq_count
    slots_all = jnp.arange(dec_total, dtype=jnp.int32)
    owner_all = slots_all // TGT
    place_all = slots_all % TGT
    query_range = jnp.arange(lengths.shape[0], dtype=jnp.int32)
    valid_all = jnp.any(
        (owner_all[:, None] == query_range[None, :]) & (place_all[:, None] < lengths[None, :]),
        axis=1,
    )
    my_place = lax.dynamic_slice_in_dim(place_all, seq_index * dec_rows, dec_rows)
    my_valid = lax.dynamic_slice_in_dim(valid_all, seq_index * dec_rows, dec_rows)
    valid_rows = my_valid.astype(f32)[:, None]
    group_size = TGT // dec_rows
    group_rel = seq_index % group_size
    key_first = seq_index // group_size * TGT
    group_place = lax.dynamic_slice_in_dim(place_all, key_first, TGT)
    group_valid = lax.dynamic_slice_in_dim(valid_all, key_first, TGT)
    self_allowed = (group_place[None, :] <= my_place[:, None]) & group_valid[None, :]
    dec_gain_one = dec_gains_w[0].astype(f32)
    dec_gain_two = dec_gains_w[1].astype(f32)
    dec_gain_three = dec_gains_w[2].astype(f32)
    dec_normed_one = norm_apply(dec_tokens, dec_gain_one).astype(bf16)
    self_proj = jnp.einsum(
        "rd,cde->cre", dec_normed_one, self_qkv_w, preferred_element_type=f32
    ).astype(bf16)

    def fetch_keys(piece, distance):
        return passed_along(piece, "seq", distance)

    self_keys = place_blocks(self_proj[1:], fetch_keys, group_size, group_rel)
    self_mix, self_logsum = attend_full(
        heads_of(self_proj[0]), heads_of(self_keys[0]), heads_of(self_keys[1]), self_allowed, 0.0
    )
    self_mix_b = self_mix.reshape(dec_rows, D).astype(bf16)
    dec_hidden = dec_tokens + matmul(self_mix_b, self_out_w)
    dec_normed_two = norm_apply(dec_hidden, dec_gain_two).astype(bf16)
    cross_queries = matmul(dec_normed_two, cross_qkv_w[0]).astype(bf16)

    def visiting_owner(turn_index):
        source = (seq_index - turn_index) % seq_count
        return (source * dec_rows + jnp.arange(dec_rows, dtype=jnp.int32)) // TGT

    def cross_forward(turn_index, carried):
        travel_q, peak_run, total_run, mix_run = carried
        allowed = visiting_owner(turn_index)[:, None] == key_owner[None, :]
        running = attend_step(
            heads_of(travel_q.astype(bf16)),
            cross_keys_h,
            cross_values_h,
            allowed,
            (peak_run, total_run, mix_run),
        )
        return shifted((travel_q, running[0], running[1], running[2]), "seq", 1)

    start_state = (
        cross_queries.astype(f32),
        jnp.full((HEADS, dec_rows), NEGATIVE, f32),
        jnp.zeros((HEADS, dec_rows), f32),
        jnp.zeros((dec_rows, HEADS, HD), f32),
    )
    unused, peak_home, total_home, mix_home = lax.fori_loop(
        0, seq_count, cross_forward, start_state
    )
    cross_mix = mix_home / total_home.T[:, :, None]
    cross_logsum = peak_home + jnp.log(total_home)
    cross_mix_b = cross_mix.reshape(dec_rows, D).astype(bf16)
    dec_hidden_two = dec_hidden + matmul(cross_mix_b, cross_out_w)
    dec_normed_three = norm_apply(dec_hidden_two, dec_gain_three).astype(bf16)
    dec_inner = matmul(dec_normed_three, dec_up_w)
    dec_active = jax.nn.gelu(dec_inner).astype(bf16)
    dec_final = dec_hidden_two + matmul(dec_active, dec_down_w)
    dec_output = (dec_final * valid_rows).astype(bf16)
    grad_final = cotangent[0].astype(f32) * valid_rows
    grad_final_b = grad_final.astype(bf16)
    grad_dec_down = grad_of(dec_active, grad_final_b)
    grad_dec_inner = gelu_back(dec_inner, back_of(grad_final_b, dec_down_w)).astype(bf16)
    grad_dec_up = grad_of(dec_normed_three, grad_dec_inner)
    grad_hidden_two, grad_gain_three = norm_back(
        dec_hidden_two, dec_gain_three, back_of(grad_dec_inner, dec_up_w)
    )
    grad_hidden_two = grad_hidden_two + grad_final
    grad_cross_b = grad_hidden_two.astype(bf16)
    grad_cross_out = grad_of(cross_mix_b, grad_cross_b)
    grad_cross_mix = heads_of(back_of(grad_cross_b, cross_out_w).astype(bf16))
    cross_dot = jnp.sum(grad_cross_mix.astype(f32) * cross_mix, axis=-1).T

    def cross_backward(turn_index, carried):
        travel, key_grad_run, value_grad_run = carried
        travel_q, travel_grad, travel_logsum, travel_dot, travel_dq = travel
        allowed = visiting_owner(turn_index)[:, None] == key_owner[None, :]
        grad_q, grad_k, grad_v, unused_scores = attend_back(
            heads_of(travel_q.astype(bf16)),
            cross_keys_h,
            cross_values_h,
            allowed,
            0.0,
            travel_logsum,
            travel_grad.astype(bf16),
            travel_dot,
        )
        moved = shifted(
            (travel_q, travel_grad, travel_logsum, travel_dot, travel_dq + grad_q), "seq", 1
        )
        return (moved, key_grad_run + grad_k, value_grad_run + grad_v)

    back_state = (
        (
            cross_queries.astype(f32),
            grad_cross_mix.astype(f32),
            cross_logsum,
            cross_dot,
            jnp.zeros((dec_rows, HEADS, HD), f32),
        ),
        jnp.zeros((row_count, HEADS, HD), f32),
        jnp.zeros((row_count, HEADS, HD), f32),
    )
    travel_home, cross_key_grad, cross_value_grad = lax.fori_loop(
        0, seq_count, cross_backward, back_state
    )
    grad_cross_q_b = travel_home[4].reshape(dec_rows, D).astype(bf16)
    grad_cross_qw = grad_of(dec_normed_two, grad_cross_q_b)
    grad_hidden, grad_gain_two = norm_back(
        dec_hidden, dec_gain_two, back_of(grad_cross_q_b, cross_qkv_w[0])
    )
    grad_hidden = grad_hidden + grad_hidden_two
    cross_kv_grad = jnp.stack(
        [cross_key_grad.reshape(row_count, D), cross_value_grad.reshape(row_count, D)]
    ).astype(bf16)
    grad_cross_kvw = jnp.einsum("rd,cre->cde", encoded_b, cross_kv_grad, preferred_element_type=f32)
    grad_encoded = jnp.einsum(
        "cre,cde->rd", cross_kv_grad, cross_qkv_w[1:], preferred_element_type=f32
    )
    grad_cross_qkv = jnp.concatenate([grad_cross_qw[None], grad_cross_kvw], axis=0)
    grad_self_b = grad_hidden.astype(bf16)
    grad_self_out = grad_of(self_mix_b, grad_self_b)
    grad_self_mix = heads_of(back_of(grad_self_b, self_out_w).astype(bf16))
    self_dot = jnp.sum(grad_self_mix.astype(f32) * self_mix, axis=-1).T
    self_gq, self_gk, self_gv, unused_self = attend_back(
        heads_of(self_proj[0]),
        heads_of(self_keys[0]),
        heads_of(self_keys[1]),
        self_allowed,
        0.0,
        self_logsum,
        grad_self_mix,
        self_dot,
    )
    blocks = jnp.stack([self_gk.reshape(TGT, D), self_gv.reshape(TGT, D)]).reshape(
        2, group_size, dec_rows, D
    )
    key_grads = lax.dynamic_index_in_dim(blocks, group_rel, 1, keepdims=False)
    for distance in range(1, group_size):
        downward = lax.dynamic_index_in_dim(
            blocks, jnp.maximum(group_rel - distance, 0), 1, keepdims=False
        )
        downward = jnp.where(group_rel - distance >= 0, downward, 0.0)
        key_grads = key_grads + passed_along(downward, "seq", -distance)
    self_grad_b = jnp.concatenate([self_gq.reshape(dec_rows, D)[None], key_grads], axis=0).astype(
        bf16
    )
    grad_self_qkv = jnp.einsum(
        "rd,cre->cde", dec_normed_one, self_grad_b, preferred_element_type=f32
    )
    grad_normed_one = jnp.einsum("cre,cde->rd", self_grad_b, self_qkv_w, preferred_element_type=f32)
    grad_dec_in, grad_gain_one = norm_back(dec_tokens, dec_gain_one, grad_normed_one)
    grad_dec_in = grad_dec_in + grad_hidden
    grad_dec_gains = jnp.stack([grad_gain_one, grad_gain_two, grad_gain_three])
    grad_encoded_b = grad_encoded.astype(bf16)
    grad_enc_down = grad_of(enc_active, grad_encoded_b)
    grad_enc_inner = gelu_back(enc_inner, back_of(grad_encoded_b, enc_down_w)).astype(bf16)
    grad_enc_up = grad_of(normed_two, grad_enc_inner)
    grad_enc_hidden, grad_enc_gain_two = norm_back(
        enc_hidden, enc_gain_two, back_of(grad_enc_inner, enc_up_w)
    )
    grad_enc_hidden = grad_enc_hidden + grad_encoded
    grad_attn_b = grad_enc_hidden.astype(bf16)
    grad_enc_out = grad_of(enc_mixed_b, grad_attn_b)
    grad_enc_mix = heads_of(back_of(grad_attn_b, enc_out_w).astype(bf16))
    enc_dot = jnp.sum(grad_enc_mix.astype(f32) * enc_mixture, axis=-1).T
    query_grads = []
    key_grad_parts = []
    value_grad_parts = []
    table_parts = []
    for head_first in range(0, HEADS, 4):
        head_part = slice(head_first, head_first + 4)
        bias_part = bias_matrix(rel_table[:, head_part], onehot, row_count, key_span, period)
        part_q, part_k, part_v, part_scores = attend_back(
            enc_queries[:, head_part],
            enc_keys[:, head_part],
            enc_values[:, head_part],
            enc_allowed,
            bias_part,
            enc_logsum[head_part],
            grad_enc_mix[:, head_part],
            enc_dot[head_part],
        )
        query_grads.append(part_q)
        key_grad_parts.append(part_k)
        value_grad_parts.append(part_v)
        table_parts.append(bias_back(part_scores, onehot, row_count, key_span, period))
    enc_grad_q = jnp.concatenate(query_grads, axis=1).reshape(row_count, D)
    near_grad = jnp.stack(
        [
            jnp.concatenate(key_grad_parts, axis=1).reshape(key_span, D),
            jnp.concatenate(value_grad_parts, axis=1).reshape(key_span, D),
        ]
    )
    from_higher = passed_along(near_grad[:, :PASS], "seq", -1)
    from_lower = passed_along(near_grad[:, key_span - PASS :], "seq", 1)
    local_kv = near_grad[:, PASS : PASS + row_count]
    local_kv = local_kv + from_higher
    local_kv = local_kv + from_lower
    enc_grad_b = jnp.concatenate([enc_grad_q[None], local_kv], axis=0).astype(bf16)
    grad_enc_qkv = jnp.einsum("rd,cre->cde", normed_one, enc_grad_b, preferred_element_type=f32)
    grad_enc_normed = jnp.einsum("cre,cde->rd", enc_grad_b, enc_qkv_w, preferred_element_type=f32)
    grad_enc_in, grad_enc_gain_one = norm_back(tokens, enc_gain_one, grad_enc_normed)
    grad_enc_in = grad_enc_in + grad_enc_hidden
    grad_enc_gains = jnp.stack([grad_enc_gain_one, grad_enc_gain_two])
    table_grad, enc_gains_total, dec_gains_total = lax.psum(
        (jnp.concatenate(table_parts, axis=1), grad_enc_gains, grad_dec_gains), ("dp", "seq")
    )
    (
        sum_enc_qkv,
        sum_enc_out,
        sum_enc_up,
        sum_enc_down,
        sum_self_qkv,
        sum_self_out,
        sum_cross_qkv,
        sum_cross_out,
        sum_dec_up,
        sum_dec_down,
    ) = (
        lax.psum_scatter(grad_enc_qkv, "seq", scatter_dimension=1, tiled=True),
        lax.psum_scatter(grad_enc_out, "seq", scatter_dimension=0, tiled=True),
        lax.psum_scatter(grad_enc_up, "seq", scatter_dimension=0, tiled=True),
        lax.psum_scatter(grad_enc_down, "seq", scatter_dimension=0, tiled=True),
        lax.psum_scatter(grad_self_qkv, "seq", scatter_dimension=1, tiled=True),
        lax.psum_scatter(grad_self_out, "seq", scatter_dimension=0, tiled=True),
        lax.psum_scatter(grad_cross_qkv, "seq", scatter_dimension=1, tiled=True),
        lax.psum_scatter(grad_cross_out, "seq", scatter_dimension=0, tiled=True),
        lax.psum_scatter(grad_dec_up, "seq", scatter_dimension=0, tiled=True),
        lax.psum_scatter(grad_dec_down, "seq", scatter_dimension=0, tiled=True),
    )
    shards = (
        lax.psum_scatter(sum_enc_qkv, "dp", scatter_dimension=2, tiled=True),
        lax.psum_scatter(sum_enc_out, "dp", scatter_dimension=1, tiled=True),
        lax.psum_scatter(sum_enc_up, "dp", scatter_dimension=1, tiled=True),
        lax.psum_scatter(sum_enc_down, "dp", scatter_dimension=1, tiled=True),
        lax.psum_scatter(sum_self_qkv, "dp", scatter_dimension=2, tiled=True),
        lax.psum_scatter(sum_self_out, "dp", scatter_dimension=1, tiled=True),
        lax.psum_scatter(sum_cross_qkv, "dp", scatter_dimension=2, tiled=True),
        lax.psum_scatter(sum_cross_out, "dp", scatter_dimension=1, tiled=True),
        lax.psum_scatter(sum_dec_up, "dp", scatter_dimension=1, tiled=True),
        lax.psum_scatter(sum_dec_down, "dp", scatter_dimension=1, tiled=True),
    )
    return (
        dec_output[None],
        grad_enc_in[None],
        grad_dec_in[None],
        enc_gains_total,
        shards[0],
        shards[1],
        table_grad,
        shards[2],
        shards[3],
        dec_gains_total,
        shards[4],
        shards[5],
        shards[6],
        shards[7],
        shards[8],
        shards[9],
    )


def solution(mesh):
    placed = (
        P("dp", "seq", None),
        P("dp", "seq", None),
        P("dp", None),
        P("dp", None),
        P("dp", "seq", None),
        P(),
        P(None, "seq", "dp"),
        P("seq", "dp"),
        P(),
        P("seq", "dp"),
        P("seq", "dp"),
        P(),
        P(None, "seq", "dp"),
        P("seq", "dp"),
        P(None, "seq", "dp"),
        P("seq", "dp"),
        P("seq", "dp"),
        P("seq", "dp"),
    )
    return jax.shard_map(
        per_device,
        mesh=mesh,
        in_specs=placed,
        out_specs=(
            P("dp", "seq", None),
            P("dp", "seq", None),
            P("dp", "seq", None),
            P(),
            P(None, "seq", "dp"),
            P("seq", "dp"),
            P(),
            P("seq", "dp"),
            P("seq", "dp"),
            P(),
            P(None, "seq", "dp"),
            P("seq", "dp"),
            P(None, "seq", "dp"),
            P("seq", "dp"),
            P("seq", "dp"),
            P("seq", "dp"),
        ),
        check_vma=False,
    )
```

profile of v0, /device:TPU:0, one launch (start us, length us, event | category | flops | bytes accessed | tf_op | source)
XLA Modules:
  0.0 2777.3 jit_solution(12151548325555645340)
XLA Ops:
  17.3 36.8 %all-gather.18.cloned.1.call-done = bf16[3,768,384]{2,1,0:T(8,128)(2,1)} async-done(((bf16[3,48,384]{2,1,0:T(8,128)(2,1)}), bf16[3,768,384]{2,1,0:T(8,128)(2,1)}) %all-gather.18.cloned.1.call-update) | async-done | bytes 1769488 | tf_op jit(solution)/shard_map/all_gather | solution.py:222
  54.1 42.2 %all-gather.28.cloned.1.call-done = bf16[3,768,384]{2,1,0:T(8,128)(2,1)} async-done(((bf16[3,48,384]{2,1,0:T(8,128)(2,1)}), bf16[3,768,384]{2,1,0:T(8,128)(2,1)}) %all-gather.28.cloned.1.call-update) | async-done | bytes 1769488 | tf_op jit(solution)/shard_map/all_gather | solution.py:218
  96.4 22.7 all_gather.62
  119.2 20.3 all-gather.24.cloned.1.call-done
  139.6 22.5 all_gather.68
  162.2 22.2 all-gather.34.cloned.1.call-done
  184.5 43.7 %all-gather.38.cloned.1.call-done = bf16[3072,384]{1,0:T(8,128)(2,1)} async-done(((bf16[192,384]{1,0:T(8,128)(2,1)}), bf16[3072,384]{1,0:T(8,128)(2,1)}) %all-gather.38.cloned.1.call-update) | async-done | bytes 2359312 | tf_op jit(solution)/shard_map/all_gather | solution.py:221
  228.3 22.4 all_gather.74
  251.9 21.1 all-gather.44.cloned.1.call-done
  587.7 57.6 %all-gather.40.cloned.1.call-done = bf16[3072,768]{1,0:T(8,128)(2,1)} async-done(((bf16[3072,384]{1,0:T(8,128)(2,1)}), bf16[3072,768]{1,0:T(8,128)(2,1)}) %all-gather.40.cloned.1.call-update) | async-done | bytes 4718608 | tf_op jit(solution)/shard_map/all_gather | solution.py:244
  654.2 197.3 %while.49 = (s32[]{:T(128)}, bf16[96,768]{0,1:T(8,128)(2,1)S(1)}, f32[12,96]{1,0:T(8,128)S(1)}, f32[12,96]{1,0:T(8,128)S(1)}, f32[96,12,64]{0,2,1:T(8,128)S(1)},...) while((s32[]{:T(128)}, bf16[96,768]{0,1:T(8,128)(2,1)S(1)}, ...), condition=%wide.region_16.17_spmd, body=%wide.region_13.16_spmd.sunk | while | flops 119185648 | bytes 9550510 | solution.py:368
  866.7 302.7 %while.50 = (s32[]{:T(128)}, bf16[96,768]{0,1:T(8,128)(2,1)}, bf16[96,12,64]{0,2,1:T(8,128)(2,1)}, f32[12,96]{1,0:T(8,128)S(1)}, f32[12,96]{1,0:T(8,128)S(1)}, /...) while((s32[]{:T(128)}, bf16[96,768]{0,1:T(8,128)(2,1)}, ...), condition=%wide.region_21.22_spmd.clone, body=%wide.region_20.21_spmd.clone.sunk | while | flops 287871872 | bytes 23439152 | solution.py:424
  1329.3 61.2 %collective-permute-done.21 = f32[2,96,768]{2,1,0:T(8,128)} collective-permute-done((f32[2,96,768]{2,1,0:T(8,128)}, f32[2,96,768]{2,1,0:T(8,128)}, u32[]{:S(2)}, u32[]{:S(2)}) %collective-permute-start.21) | collective-permute-done | bytes 589856 | tf_op jit(solution)/shard_map/ppermute | solution.py:37
  1390.5 26.7 collective-permute-done.23
  1496.0 442.2 %all-reduce.14.cloned.1.call-done = (f32[3,768,768]{2,0,1:T(4,128)}, f32[3,768,768]{2,0,1:T(4,128)}, f32[3,768,768]{2,0,1:T(4,128)}) async-done(((f32[3,768,768]{2,0,1:T(4,128)}, f32[3,768,768]{2,0,1:T(4,128)}, f32[3,768,768]{2,0,1:T(4,128)}), (f32[3,768,768]{2,0,1:T(4,128)}, f32[3,768,768]{2,0,1:T(4,128)}, f32[3,768,768]{2,0,1:T(4,128)})) %all-reduce.14.cloned.1.call-update) | async-done | bytes 21233680
  2024.8 46.4 %reduce-scatter.40.cloned.1.call-done = f32[48,768]{1,0:T(8,128)} async-done(((f32[768,768]{1,0:T(8,128)}), f32[48,768]{1,0:T(8,128)}) %reduce-scatter.40.cloned.1.call-update) | async-done | bytes 147472 | tf_op jit(solution)/shard_map/reduce_scatter | solution.py:548
  2071.2 66.2 %reduce-scatter.36.cloned.1.call-done = f32[48,768]{1,0:T(8,128)} async-done(((f32[768,768]{1,0:T(8,128)}), f32[48,768]{1,0:T(8,128)}) %reduce-scatter.36.cloned.1.call-update) | async-done | bytes 147472 | tf_op jit(solution)/shard_map/reduce_scatter | solution.py:546
  2137.5 114.4 %reduce-scatter.32.cloned.1.call-done = f32[192,768]{1,0:T(8,128)} async-done(((f32[3072,768]{1,0:T(8,128)}), f32[192,768]{1,0:T(8,128)}) %reduce-scatter.32.cloned.1.call-update) | async-done | bytes 589840 | tf_op jit(solution)/shard_map/reduce_scatter | solution.py:544
  2392.0 90.8 %reduce-scatter.48.cloned.1.call-done = f32[192,768]{1,0:T(8,128)} async-done(((f32[3072,768]{1,0:T(8,128)}), f32[192,768]{1,0:T(8,128)}) %reduce-scatter.48.cloned.1.call-update) | async-done | bytes 589840 | tf_op jit(solution)/shard_map/reduce_scatter | solution.py:550
  2489.6 109.0 %reduce-scatter.44.cloned.1.call-done = f32[48,3072]{1,0:T(8,128)} async-done(((f32[768,3072]{1,0:T(8,128)}), f32[48,3072]{1,0:T(8,128)}) %reduce-scatter.44.cloned.1.call-update) | async-done | bytes 589840 | tf_op jit(solution)/shard_map/reduce_scatter | solution.py:549
  2603.1 41.2 %all-reduce.10 = (f32[2,768]{1,0:T(2,128)}, f32[32,12]{0,1:T(8,128)}, f32[3,768]{1,0:T(4,128)}) all-reduce(f32[2,768]{1,0:T(2,128)S(1)} %pad_maximum_fusion.18, f32[32,12]{0,1:T(8,128)S(1)} %pad_maximum_fusion.17, f32[3,768]{1,0:T(4,128)S(1)} %pad_maximum_fusion.16), channel_id=1, replica_groups=mesh['dp'=2,'seq'=16] {'dp','seq'}, use_global_device_ids=true, to_apply=%region_30.31 | all-reduce | flops 4224 | bytes 33792 | tf_op jit(solution)/shard_map/psum | solution.py:526
  2698.0 18.2 reduce-scatter.34.cloned.1.call-done
  2734.2 18.2 reduce-scatter.50.cloned.1.call-done
  2752.4 18.1 reduce-scatter.46.cloned.1.call-done
  (1377 shorter events, 1392.3 us)
Async XLA Ops:
  16.5 424.3 %all-gather.48.cloned.1.call-start = ((), (), s32[]{:S(2)}) async-start(), calls=%async_computation.32 | async-start | bytes 2506752 | tf_op jit(solution)/shard_map/all_gather | solution.py:227
  17.2 423.7 %all-gather.20.cloned.1.call-start = ((), (), s32[]{:S(2)}) async-start(), calls=%async_computation.18 | async-start | bytes 5308416 | tf_op jit(solution)/shard_map/all_gather | solution.py:245
  96.3 419.4 %all-gather.22.cloned.1.call-start = ((), (), s32[]{:S(2)}) async-start(), calls=%async_computation.19 | async-start | bytes 1769472 | tf_op jit(solution)/shard_map/all_gather | solution.py:246
  139.5 421.6 %all-gather.32.cloned.1.call-start = ((), (), s32[]{:S(2)}) async-start(), calls=%async_computation.24 | async-start | bytes 1769472 | tf_op jit(solution)/shard_map/all_gather | solution.py:242
  184.4 460.9 %all-gather.40.cloned.1.call-start = ((), (), s32[]{:S(2)}) async-start(), calls=%async_computation.28 | async-start | bytes 7077888 | tf_op jit(solution)/shard_map/all_gather | solution.py:244
  228.2 623.4 %all-gather.42.cloned.1.call-start = ((), (), s32[]{:S(2)}) async-start(), calls=%async_computation.29 | async-start | bytes 1769472 | tf_op jit(solution)/shard_map/all_gather | solution.py:248
  250.7 602.8 %all-gather.46.cloned.1.call-start = ((), (), s32[]{:S(2)}) async-start(), calls=%async_computation.31 | async-start | bytes 7077888 | tf_op jit(solution)/shard_map/all_gather | solution.py:249
  273.0 583.9 %all-gather.50.cloned.1.call-start = ((), (), s32[]{:S(2)}) async-start(), calls=%async_computation.33 | async-start | bytes 7077888 | tf_op jit(solution)/shard_map/all_gather | solution.py:250
  440.8 1497.4 %all-reduce.14.cloned.1.call-start = ((), (), s32[]{:S(2)}) async-start(), calls=%async_computation.51 | async-start | bytes 56623104
  1455.7 568.4 %reduce-scatter.24.cloned.1.call-start = ((), (), s32[]{:S(2)}) async-start(), calls=%async_computation.34 | async-start | bytes 2506752 | tf_op jit(solution)/shard_map/reduce_scatter | solution.py:542
  1459.3 611.9 %reduce-scatter.40.cloned.1.call-start = ((), (), s32[]{:S(2)}) async-start(), calls=%async_computation.42 | async-start | bytes 2506752 | tf_op jit(solution)/shard_map/reduce_scatter | solution.py:548
  1461.3 676.2 %reduce-scatter.36.cloned.1.call-start = ((), (), s32[]{:S(2)}) async-start(), calls=%async_computation.40 | async-start | bytes 2506752 | tf_op jit(solution)/shard_map/reduce_scatter | solution.py:546
  1463.2 788.7 %reduce-scatter.32.cloned.1.call-start = ((), (), s32[]{:S(2)}) async-start(), calls=%async_computation.38 | async-start | bytes 10027008 | tf_op jit(solution)/shard_map/reduce_scatter | solution.py:544
  1472.5 910.8 %reduce-scatter.28.cloned.1.call-start = ((), (), s32[]{:S(2)}) async-start(), calls=%async_computation.36 | async-start | bytes 10027008 | tf_op jit(solution)/shard_map/reduce_scatter | solution.py:543
  1480.8 1002.1 %reduce-scatter.48.cloned.1.call-start = ((), (), s32[]{:S(2)}) async-start(), calls=%async_computation.46 | async-start | bytes 10027008 | tf_op jit(solution)/shard_map/reduce_scatter | solution.py:550
  1487.1 1111.6 %reduce-scatter.44.cloned.1.call-start = ((), (), s32[]{:S(2)}) async-start(), calls=%async_computation.44 | async-start | bytes 10027008 | tf_op jit(solution)/shard_map/reduce_scatter | solution.py:549
  1494.1 1151.5 %reduce-scatter.56.cloned.1.call-start = ((), (), s32[]{:S(2)}) async-start(), calls=%async_computation.50 | async-start | bytes 1179648
  1966.7 693.4 %reduce-scatter.54.cloned.1.call-start = ((), (), s32[]{:S(2)}) async-start(), calls=%async_computation.49 | async-start | bytes 1179648
  1995.0 679.5 %reduce-scatter.52.cloned.1.call-start = ((), (), s32[]{:S(2)}) async-start(), calls=%async_computation.48 | async-start | bytes 1179648
  2024.0 664.9 %reduce-scatter.26.cloned.1.call-start = ((), (), s32[]{:S(2)}) async-start(), calls=%async_computation.35 | async-start | bytes 221184 | tf_op jit(solution)/shard_map/reduce_scatter | solution.py:554
  2024.7 664.2 %reduce-scatter.42.cloned.1.call-start = ((), (), s32[]{:S(2)}) async-start(), calls=%async_computation.43 | async-start | bytes 221184 | tf_op jit(solution)/shard_map/reduce_scatter | solution.py:560
  2071.2 626.8 %reduce-scatter.38.cloned.1.call-start = ((), (), s32[]{:S(2)}) async-start(), calls=%async_computation.41 | async-start | bytes 221184 | tf_op jit(solution)/shard_map/reduce_scatter | solution.py:558
  2137.5 578.7 %reduce-scatter.34.cloned.1.call-start = ((), (), s32[]{:S(2)}) async-start(), calls=%async_computation.39 | async-start | bytes 884736 | tf_op jit(solution)/shard_map/reduce_scatter | solution.py:556
  2252.0 482.2 %reduce-scatter.30.cloned.1.call-start = ((), (), s32[]{:S(2)}) async-start(), calls=%async_computation.37 | async-start | bytes 884736 | tf_op jit(solution)/shard_map/reduce_scatter | solution.py:555
  (374 other events, 10474.1 us)
Sparse Core Ops, SparseCore 0:
  10.9 43.0 all-gather.17
  56.9 39.2 all-gather.27
  99.2 40.2 all-gather.23
  142.2 42.1 all-gather.33
  187.1 41.0 all-gather.37
  230.9 41.9 all-gather.43
  275.8 41.0 all-gather.47
  318.5 48.1 all-gather.19
  368.2 49.3 all-gather.29
  419.0 22.7 all-gather.21
  443.4 49.3 all-gather.25
  494.2 22.7 all-gather.31
  518.5 62.6 all-gather.35
  582.6 62.6 all-gather.39
  670.9 62.6 all-gather.45
  735.0 62.6 all-gather.49
  1455.8 482.4 all-reduce.13
  1942.5 63.0 reduce-scatter.23
  2009.1 61.9 reduce-scatter.39
  2075.4 62.0 reduce-scatter.35
  2141.6 110.3 reduce-scatter.31
  2256.6 111.1 reduce-scatter.27
  2371.7 111.0 reduce-scatter.47
  2487.5 111.0 reduce-scatter.43
  (11 shorter events, 167.3 us)
where the time goes:
time: 2790 us; the launch traced here: 2780 us
  waiting for transfers between devices  1540 us (55%)
  local copies, waits for them, and re-layouts  573 us (21%)
  matrix products  356 us (13%)
  blocking collectives  109 us (4%)
  starting transfers between devices  94.2 us (3%)
  other arithmetic  84.1 us (3%)
    unnamed x39, waiting for transfers between devices  443 us
    unnamed x365, local copies, waits for them, and re-layouts  287 us
    ppermute x144, waiting for transfers between devices, shifted(): return lax.ppermute(block, axis, route)  233 us
    reduce_scatter x1, waiting for transfers between devices, per_device(): lax.psum_scatter(grad_enc_down, 'seq', scatter_dimension=0, tiled=True)  114 us
    reduce_scatter x1, waiting for transfers between devices, per_device(): lax.psum_scatter(grad_dec_up, 'seq', scatter_dimension=0, tiled=True)  109 us
    ppermute x16, waiting for transfers between devices, passed_along(): return lax.ppermute(block, axis, route)  94 us
    reduce_scatter x1, waiting for transfers between devices, per_device(): lax.psum_scatter(grad_dec_down, 'seq', scatter_dimension=0, tiled=True)  90.8 us
    reduce_scatter x1, waiting for transfers between devices, per_device(): lax.psum_scatter(grad_self_out, 'seq', scatter_dimension=0, tiled=True)  66.2 us
  transfers between devices with their start and end apart: 197, of which 73 were waited for; matrix products, arithmetic and copies ran while one was open for 31% of the time, Pallas kernels for 0%

commit v1 on v0

v1 whole, which is shorter than its diff:
```python
import functools

import jax
import jax.numpy as jnp
from jax import lax
from jax.experimental import pallas as pl
from jax.experimental.pallas import tpu as pltpu
from jax.sharding import PartitionSpec as P

D = 768
HEADS = 12
HD = 64
FF = 3072
BUCKETS = 32
PASS = 384
PASS_N = 20
TGT = 768
STATS = 16
PAIR = 2 * HD
PAIRS = HEADS // 2

EPSILON = 1e-06
PRECISE = lax.Precision.HIGHEST
LIMITS = (12, 16, 23, 32, 46, 64, 91)
NEGATIVE = -1e30
FAR = 1 << 20
KEYS = 128
VMEM = 56 * 1024 * 1024
bf16 = jnp.bfloat16
f32 = jnp.float32


def bucket_of(distance):
    forward_half = (distance > 0).astype(jnp.int32) * 16
    distance_abs = jnp.abs(distance)
    far_bucket = jnp.full(distance_abs.shape, 8, jnp.int32)
    for threshold in LIMITS:
        far_bucket = far_bucket + (distance_abs >= threshold).astype(jnp.int32)
    return forward_half + jnp.where(distance_abs < 8, distance_abs, far_bucket)


def norm_apply(values, gain_row):
    return (
        values * lax.rsqrt(jnp.mean(values * values, axis=-1, keepdims=True) + EPSILON) * gain_row
    )


def norm_back(values, gain_row, gradient):
    unused, pullback = jax.vjp(norm_apply, values, gain_row)
    return pullback(gradient)


def gelu_back(inner_act, gradient):
    unused, pullback = jax.vjp(jax.nn.gelu, inner_act)
    return pullback(gradient)[0]


def matmul(left_side, right_side):
    return jnp.dot(left_side, right_side, preferred_element_type=f32)


def grad_of(left_side, right_side):
    return lax.dot_general(
        left_side, right_side, (((0,), (0,)), ((), ())), preferred_element_type=f32
    )


def back_of(gradient, weight):
    return lax.dot_general(
        gradient, weight, (((1,), (1,)), ((), ())), preferred_element_type=f32
    )


def head_mask(values, half):
    lanes = lax.broadcasted_iota(jnp.int32, values.shape, 1)
    keep = (lanes < HD) if half == 0 else (lanes >= HD)
    return jnp.where(keep, values, jnp.zeros_like(values))


def dot_nt(a, b):
    return lax.dot_general(a, b, (((1,), (1,)), ((), ())), preferred_element_type=f32)


def dot_tn(a, b):
    return lax.dot_general(a, b, (((0,), (0,)), ((), ())), preferred_element_type=f32)


def bias_slot(key_block, row_block):
    return jnp.clip(key_block - PASS // KEYS - row_block, -2, 2) + 2


def attend_kernel(causal, with_bias, spans_ref, q_ref, k_ref, v_ref, row_ref, key_ref, *rest):
    if with_bias:
        bias_ref, o_ref, stat_ref, acc_ref, peak_ref, total_ref = rest
    else:
        o_ref, stat_ref, acc_ref, peak_ref, total_ref = rest
    block = pl.program_id(0)
    acc_ref[...] = jnp.zeros_like(acc_ref)
    peak_ref[...] = jnp.full(peak_ref.shape, NEGATIVE, f32)
    total_ref[...] = jnp.zeros_like(total_ref)
    row_mark = row_ref[0]

    def body(key_block, unused):
        keys = pl.ds(pl.multiple_of(key_block * KEYS, KEYS), KEYS)
        key_mark = key_ref[keys, :]
        allowed = (key_mark <= row_mark) if causal else (key_mark == row_mark)
        if with_bias:
            biased = pl.ds(pl.multiple_of(bias_slot(key_block, block) * KEYS, KEYS), KEYS)
        for pair in range(PAIRS):
            lanes = slice(pair * PAIR, (pair + 1) * PAIR)
            k_pair = k_ref[keys, lanes]
            v_pair = v_ref[keys, lanes]
            q_pair = q_ref[:, lanes]
            for half in range(2):
                head = pair * 2 + half
                scores = dot_nt(k_pair, head_mask(q_pair, half)) * 0.125
                if with_bias:
                    scores = scores + bias_ref[head, biased, :]
                scores = jnp.where(allowed, scores, NEGATIVE)
                old = peak_ref[head : head + 1, :]
                peak = jnp.maximum(old, jnp.max(scores, axis=0, keepdims=True))
                rescale = jnp.exp(old - peak)
                weights = jnp.exp(scores - peak)
                peak_ref[head : head + 1, :] = peak
                total_ref[head : head + 1, :] = total_ref[
                    head : head + 1, :
                ] * rescale + jnp.sum(weights, axis=0, keepdims=True)
                mixed = dot_tn(v_pair, weights.astype(bf16))
                rows = slice(head * HD, (head + 1) * HD)
                acc_ref[rows, :] = (
                    acc_ref[rows, :] * rescale + mixed[half * HD : (half + 1) * HD, :]
                )
        return 0

    lax.fori_loop(spans_ref[2 * block], spans_ref[2 * block + 1], body, 0)
    total = total_ref[...]
    some = total > 0.0
    inverse = jnp.where(some, 1.0 / jnp.where(some, total, 1.0), 0.0)
    stat_ref[...] = jnp.where(
        some, peak_ref[...] + jnp.log(jnp.where(some, total, 1.0)), NEGATIVE
    )
    for pair in range(PAIRS):
        parts = []
        for half in range(2):
            head = pair * 2 + half
            rows = slice(head * HD, (head + 1) * HD)
            parts.append(acc_ref[rows, :] * inverse[head : head + 1, :])
        o_ref[:, pair * PAIR : (pair + 1) * PAIR] = (
            jnp.concatenate(parts, axis=0).T.astype(o_ref.dtype)
        )


def attend(q_src, q_col, kv_src, k_col, v_col, row_mark, key_mark, spans, bias, rows, causal):
    count = q_src.shape[0]
    blocks = count // rows
    span = kv_src.shape[0]
    specs = [
        pl.BlockSpec((rows, D), lambda i, s: (i, q_col)),
        pl.BlockSpec((span, D), lambda i, s: (0, k_col)),
        pl.BlockSpec((span, D), lambda i, s: (0, v_col)),
        pl.BlockSpec((1, 1, rows), lambda i, s: (i, 0, 0)),
        pl.BlockSpec((span, 1), lambda i, s: (0, 0)),
    ]
    operands = [q_src, kv_src, kv_src, row_mark.reshape(blocks, 1, rows), key_mark[:, None]]
    if bias is not None:
        specs.append(pl.BlockSpec(bias.shape, lambda i, s: (0, 0, 0)))
        operands.append(bias)
    return pl.pallas_call(
        functools.partial(attend_kernel, causal, bias is not None),
        grid_spec=pltpu.PrefetchScalarGridSpec(
            num_scalar_prefetch=1,
            grid=(blocks,),
            in_specs=specs,
            out_specs=[
                pl.BlockSpec((rows, D), lambda i, s: (i, 0)),
                pl.BlockSpec((STATS, rows), lambda i, s: (0, i)),
            ],
            scratch_shapes=[
                pltpu.VMEM((D, rows), f32),
                pltpu.VMEM((STATS, rows), f32),
                pltpu.VMEM((STATS, rows), f32),
            ],
        ),
        out_shape=[
            jax.ShapeDtypeStruct((count, D), bf16),
            jax.ShapeDtypeStruct((STATS, count), f32),
        ],
        compiler_params=pltpu.CompilerParams(vmem_limit_bytes=VMEM),
        cost_estimate=pl.CostEstimate(
            flops=4 * count * span * D // 3, bytes_accessed=8 * span * D, transcendentals=0
        ),
    )(spans, *operands)


def attend_back_kernel(
    causal,
    with_bias,
    spans_ref,
    q_ref,
    k_ref,
    v_ref,
    row_ref,
    key_ref,
    do_ref,
    stat_ref,
    dot_ref,
    *rest,
):
    if with_bias:
        bias_ref, dq_ref, dk_ref, dv_ref, dbias_ref, dqt_ref, dk_acc, dv_acc = rest
    else:
        dq_ref, dk_ref, dv_ref, dqt_ref, dk_acc, dv_acc = rest
    block = pl.program_id(0)

    @pl.when(block == 0)
    def start():
        dk_acc[...] = jnp.zeros_like(dk_acc)
        dv_acc[...] = jnp.zeros_like(dv_acc)
        if with_bias:
            dbias_ref[...] = jnp.zeros_like(dbias_ref)

    dqt_ref[...] = jnp.zeros_like(dqt_ref)
    row_mark = row_ref[0]

    def body(key_block, unused):
        keys = pl.ds(pl.multiple_of(key_block * KEYS, KEYS), KEYS)
        key_mark = key_ref[keys, :]
        allowed = (key_mark <= row_mark) if causal else (key_mark == row_mark)
        if with_bias:
            biased = pl.ds(pl.multiple_of(bias_slot(key_block, block) * KEYS, KEYS), KEYS)
        for pair in range(PAIRS):
            lanes = slice(pair * PAIR, (pair + 1) * PAIR)
            k_pair = k_ref[keys, lanes]
            v_pair = v_ref[keys, lanes]
            q_pair = q_ref[:, lanes]
            do_pair = do_ref[:, lanes]
            dk_add = None
            dv_add = None
            for half in range(2):
                head = pair * 2 + half
                q_half = head_mask(q_pair, half)
                do_half = head_mask(do_pair, half)
                scores = dot_nt(k_pair, q_half) * 0.125
                if with_bias:
                    scores = scores + bias_ref[head, biased, :]
                scores = jnp.where(allowed, scores, NEGATIVE)
                weights = jnp.exp(scores - stat_ref[head : head + 1, :])
                grad_weights = dot_nt(v_pair, do_half)
                grad_scores = weights * (grad_weights - dot_ref[head : head + 1, :])
                if with_bias:
                    dbias_ref[head, biased, :] += grad_scores
                rounded = grad_scores.astype(bf16)
                dv_part = jnp.dot(weights.astype(bf16), do_half, preferred_element_type=f32)
                dk_part = jnp.dot(rounded, q_half, preferred_element_type=f32)
                dv_add = dv_part if dv_add is None else dv_add + dv_part
                dk_add = dk_part if dk_add is None else dk_add + dk_part
                mixed = dot_tn(k_pair, rounded)
                rows = slice(head * HD, (head + 1) * HD)
                dqt_ref[rows, :] += mixed[half * HD : (half + 1) * HD, :]
            dk_acc[keys, lanes] += dk_add
            dv_acc[keys, lanes] += dv_add
        return 0

    lax.fori_loop(spans_ref[2 * block], spans_ref[2 * block + 1], body, 0)
    for pair in range(PAIRS):
        lanes = slice(pair * PAIR, (pair + 1) * PAIR)
        dq_ref[:, lanes] = (dqt_ref[lanes, :] * 0.125).T.astype(dq_ref.dtype)

    @pl.when(block == pl.num_programs(0) - 1)
    def finish():
        dk_ref[...] = (dk_acc[...] * 0.125).astype(dk_ref.dtype)
        dv_ref[...] = dv_acc[...].astype(dv_ref.dtype)


def attend_back(
    q_src, q_col, kv_src, k_col, v_col, row_mark, key_mark, spans, bias, rows, causal, do, stat, dot
):
    count = q_src.shape[0]
    blocks = count // rows
    span = kv_src.shape[0]
    specs = [
        pl.BlockSpec((rows, D), lambda i, s: (i, q_col)),
        pl.BlockSpec((span, D), lambda i, s: (0, k_col)),
        pl.BlockSpec((span, D), lambda i, s: (0, v_col)),
        pl.BlockSpec((1, 1, rows), lambda i, s: (i, 0, 0)),
        pl.BlockSpec((span, 1), lambda i, s: (0, 0)),
        pl.BlockSpec((rows, D), lambda i, s: (i, 0)),
        pl.BlockSpec((STATS, rows), lambda i, s: (0, i)),
        pl.BlockSpec((STATS, rows), lambda i, s: (0, i)),
    ]
    operands = [q_src, kv_src, kv_src, row_mark.reshape(blocks, 1, rows), key_mark[:, None]]
    operands += [do, stat, dot]
    out_specs = [
        pl.BlockSpec((rows, D), lambda i, s: (i, 0)),
        pl.BlockSpec((span, D), lambda i, s: (0, 0)),
        pl.BlockSpec((span, D), lambda i, s: (0, 0)),
    ]
    out_shape = [
        jax.ShapeDtypeStruct((count, D), bf16),
        jax.ShapeDtypeStruct((span, D), bf16),
        jax.ShapeDtypeStruct((span, D), bf16),
    ]
    if bias is not None:
        specs.append(pl.BlockSpec(bias.shape, lambda i, s: (0, 0, 0)))
        operands.append(bias)
        out_specs.append(pl.BlockSpec(bias.shape, lambda i, s: (0, 0, 0)))
        out_shape.append(jax.ShapeDtypeStruct(bias.shape, f32))
    return pl.pallas_call(
        functools.partial(attend_back_kernel, causal, bias is not None),
        grid_spec=pltpu.PrefetchScalarGridSpec(
            num_scalar_prefetch=1,
            grid=(blocks,),
            in_specs=specs,
            out_specs=out_specs,
            scratch_shapes=[
                pltpu.VMEM((D, rows), f32),
                pltpu.VMEM((span, D), f32),
                pltpu.VMEM((span, D), f32),
            ],
        ),
        out_shape=out_shape,
        compiler_params=pltpu.CompilerParams(vmem_limit_bytes=VMEM),
        cost_estimate=pl.CostEstimate(
            flops=10 * count * span * D // 3, bytes_accessed=16 * span * D, transcendentals=0
        ),
    )(spans, *operands)


CORE, ROW, LOW, HIGH, COLUMN = 1, 2, 4, 8, 16
ORDERS = ((COLUMN, ROW, LOW, HIGH), (ROW, COLUMN, LOW, HIGH), (LOW, HIGH, ROW, COLUMN))
LAGS = (0, 4, 9, 13, 16)
SMALL = 16


def reduce_plan(shapes):
    chunks = []
    for source, (rows, columns) in enumerate(shapes):
        if rows > 48:
            for first in range(0, rows, 96):
                chunks.append((source, first, 96, 0, columns // 2))
        elif columns == 3 * D:
            for first in range(0, columns, D):
                chunks.append((source, 0, rows, first, D // 2))
        else:
            chunks.append((source, 0, rows, 0, columns // 2))
    plan = []
    sizes = [0, 0, 0]
    for chunk in chunks:
        size = chunk[2] * chunk[4]
        shares = (sizes[0] / 0.39, sizes[1] / 0.39, sizes[2] / 0.22)
        order = shares.index(min(shares))
        sizes[order] += size
        plan.append(chunk + (ORDERS[order],))
    return plan


def stage_shapes(chunk):
    left = [HIGH, LOW, ROW]
    both = True
    held = [(tuple(left), both)]
    for axis in chunk[5]:
        if axis == COLUMN:
            both = False
        else:
            left.remove(axis)
        held.append((tuple(left), both))
    return held


def buffer_shape(chunk, held):
    left, both = held
    width = chunk[4] * (2 if both else 1)
    return (2,) * len(left) + (chunk[2], width)


def reduce_kernel(plan, count, *refs):
    sources = refs[:count]
    small_in = refs[count]
    outs = refs[count + 1 : 2 * count + 1]
    small_out = refs[2 * count + 1]
    scratch = list(refs[2 * count + 2 :])
    send_sem, recv_sem, own_sem, small_acc, small_recv = scratch[:5]
    scratch = scratch[5:]
    own = scratch[: len(plan)]
    held = [scratch[len(plan) + 5 * i : len(plan) + 5 * i + 5] for i in range(len(plan))]

    dp = lax.axis_index("dp")
    seq = lax.axis_index("seq")

    def bit_of(axis):
        return dp if axis == COLUMN else (seq // axis) % 2

    def partner(axis):
        if axis == COLUMN:
            return (1 - dp, seq)
        return (dp, seq + axis * (1 - 2 * bit_of(axis)))

    everyone = (CORE, ROW, LOW, HIGH, COLUMN)
    barrier = pltpu.get_barrier_semaphore()
    for axis in everyone:
        pl.semaphore_signal(
            barrier, inc=1, device_id=partner(axis), device_id_type=pl.DeviceIdType.MESH
        )
    pl.semaphore_wait(barrier, len(everyone))

    def remote(source, target, item, stage, axis):
        return pltpu.make_async_remote_copy(
            src_ref=source,
            dst_ref=target,
            send_sem=send_sem.at[item, stage],
            recv_sem=recv_sem.at[item, stage],
            device_id=partner(axis),
            device_id_type=pl.DeviceIdType.MESH,
        )

    def core_copy(item):
        source, row, rows, column, half, order = plan[item]
        block = sources[source].at[
            :, :, :, 1 - bit_of(CORE), pl.ds(row, rows), pl.ds(column, 2 * half)
        ]
        return remote(block, held[item][0], item, 0, CORE)

    def own_copy(item):
        source, row, rows, column, half, order = plan[item]
        block = sources[source].at[
            :, :, :, bit_of(CORE), pl.ds(row, rows), pl.ds(column, 2 * half)
        ]
        return pltpu.make_async_copy(block, own[item], own_sem.at[item])

    def view(item, stage, mine):
        chunk = plan[item]
        axis = chunk[5][stage - 1]
        left, both = stage_shapes(chunk)[stage - 1]
        bit = bit_of(axis) if mine else 1 - bit_of(axis)
        if axis == COLUMN:
            lanes = pl.ds(pl.multiple_of(bit * chunk[4], 128), chunk[4])
            return (len(left), None, lanes)
        return (left.index(axis), bit, slice(None))

    def stage_copy(item, stage):
        at, bit, lanes = view(item, stage, False)
        block = held[item][stage - 1]
        if bit is None:
            block = block.at[(slice(None),) * (at + 1) + (lanes,)]
        else:
            block = block.at[(slice(None),) * at + (bit,)]
        return remote(block, held[item][stage], item, stage, plan[item][5][stage - 1])

    def small_copy(stage):
        source = small_in if stage == 0 else small_acc.at[stage - 1]
        return remote(source, small_recv.at[stage], len(plan), stage, everyone[stage])

    def core_add(item):
        def body(i, unused):
            at = (i // 4, i // 2 % 2, i % 2)
            held[item][0][at] = held[item][0][at] + own[item][at]
            return 0

        lax.fori_loop(0, 8, body, 0)

    def stage_add(item, stage):
        chunk = plan[item]
        left, both = stage_shapes(chunk)[stage]
        at, bit, lanes = view(item, stage, True)
        target = held[item][stage]

        def body(i, unused):
            index = tuple(i // (1 << (len(left) - 1 - n)) % 2 for n in range(len(left)))
            if bit is None:
                kept = held[item][stage - 1][index + (slice(None), lanes)]
            else:
                kept = held[item][stage - 1][index[:at] + (bit,) + index[at:]]
            if stage == 4:
                out = outs[chunk[0]]
                first = chunk[3] // 2
                out[pl.ds(chunk[1], chunk[2]), pl.ds(first, chunk[4])] = kept.astype(
                    f32
                ) + target[...].astype(f32)
            else:
                target[index] = kept + target[index]
            return 0

        if left:
            lax.fori_loop(0, 1 << len(left), body, 0)
        else:
            body(0, 0)

    for item in range(len(plan)):
        core_copy(item).start()
        own_copy(item).start()
    small_copy(0).start()
    events = sorted(
        (item + LAGS[stage], stage, item) for item in range(len(plan)) for stage in range(5)
    )
    for unused, stage, item in events:
        if stage == 0:
            core_copy(item).wait_recv()
            own_copy(item).wait()
            core_add(item)
        else:
            stage_copy(item, stage).wait_recv()
            stage_add(item, stage)
        if stage < 4:
            stage_copy(item, stage + 1).start()
        if item == 0:
            small_copy(stage).wait()
            before = small_in[...] if stage == 0 else small_acc[stage - 1]
            summed = before + small_recv[stage]
            if stage < 4:
                small_acc[stage] = summed
                small_copy(stage + 1).start()
            else:
                small_out[...] = summed
    for item in range(len(plan)):
        core_copy(item).wait_send()
        for stage in range(1, 5):
            stage_copy(item, stage).wait_send()


def reduce_all(grads, small):
    shapes = [(grad.shape[0] // 16, grad.shape[1]) for grad in grads]
    plan = reduce_plan(shapes)
    scratch = [
        pltpu.SemaphoreType.DMA((len(plan) + 1, 5)),
        pltpu.SemaphoreType.DMA((len(plan) + 1, 5)),
        pltpu.SemaphoreType.DMA((len(plan),)),
        pltpu.VMEM((4, SMALL, D), f32),
        pltpu.VMEM((5, SMALL, D), f32),
    ]
    scratch += [pltpu.VMEM(buffer_shape(c, stage_shapes(c)[0]), bf16) for c in plan]
    for chunk in plan:
        shapes_held = stage_shapes(chunk)
        scratch += [pltpu.VMEM(buffer_shape(chunk, h), bf16) for h in shapes_held]
    operands = [
        grad.reshape(2, 2, 2, 2, rows, columns) for grad, (rows, columns) in zip(grads, shapes)
    ]
    space = pl.BlockSpec(memory_space=pl.ANY)
    near = pl.BlockSpec(memory_space=pltpu.VMEM)
    results = pl.pallas_call(
        functools.partial(reduce_kernel, plan, len(grads)),
        in_specs=[space] * len(grads) + [near],
        out_specs=[near] * (len(grads) + 1),
        out_shape=[jax.ShapeDtypeStruct((rows, columns // 2), f32) for rows, columns in shapes]
        + [jax.ShapeDtypeStruct((SMALL, D), f32)],
        scratch_shapes=scratch,
        compiler_params=pltpu.CompilerParams(
            collective_id=1, has_side_effects=True, vmem_limit_bytes=60 * 1024 * 1024
        ),
        name="reduce_all",
    )(*operands, small)
    return results[:-1], results[-1]


def reduce_plainly(grads):
    dp_count = lax.axis_size("dp")
    split = []
    for grad in grads:
        rows = lax.psum_scatter(grad, "seq", scatter_dimension=0, tiled=True)
        units = 3 if rows.shape[1] == 3 * D else 1
        rows = rows.reshape(rows.shape[0], units, dp_count, -1)
        split.append(rows.transpose(2, 0, 1, 3))
    flat = jnp.concatenate([rows.reshape(dp_count, -1) for rows in split], axis=1)
    flat = lax.psum_scatter(flat, "dp", scatter_dimension=0, tiled=False).astype(f32)
    sums = []
    first = 0
    for rows in split:
        size = rows.size // dp_count
        sums.append(flat[first : first + size].reshape(rows.shape[1], -1))
        first += size
    return sums


def per_head_dot(left_side, right_side):
    product = (left_side.astype(f32) * right_side.astype(f32)).reshape(-1, HEADS, HD)
    return jnp.pad(jnp.sum(product, axis=-1), ((0, 0), (0, STATS - HEADS))).T


def bias_bands():
    key_at = jnp.arange(5 * KEYS, dtype=jnp.int32)[:, None] - 2 * KEYS
    row_at = jnp.arange(KEYS, dtype=jnp.int32)[None, :]
    return bucket_of(key_at - row_at).reshape(-1)


def per_device(
    enc_input,
    dec_input,
    passage_ids,
    target_lengths,
    cotangent,
    enc_gains,
    enc_qkv,
    enc_out,
    rel_table,
    enc_up,
    enc_down,
    dec_gains,
    self_qkv,
    self_out,
    cross_qkv,
    cross_out,
    dec_up,
    dec_down,
):
    seq_index = lax.axis_index("seq")
    seq_count = lax.axis_size("seq")
    dp_count = lax.axis_size("dp")
    part = D // seq_count
    wide = D // dp_count

    masters = (enc_qkv, self_qkv, self_out, cross_qkv, enc_out, enc_up, enc_down)
    masters = masters + (cross_out, dec_up, dec_down)

    def pieces_of(master):
        if master.ndim == 3:
            return [master[c] for c in range(3)]
        if master.shape[1] > wide:
            return [master[:, c * wide : (c + 1) * wide] for c in range(master.shape[1] // wide)]
        return [master[c * part : (c + 1) * part] for c in range(master.shape[0] // part)]

    pieces = [piece.astype(bf16) for master in masters for piece in pieces_of(master)]
    packed = lax.all_gather(jnp.concatenate(pieces, axis=0), "dp", axis=0)
    packed = packed.reshape(dp_count, len(pieces), part, wide)

    def rows_of(first, count):
        return packed[:, first : first + count].transpose(2, 1, 0, 3).reshape(part, count * D)

    def rows_of_wide(first):
        return packed[:, first : first + 4].transpose(2, 0, 1, 3).reshape(part, FF)

    def rows_of_tall(first):
        return packed[:, first : first + 4].transpose(1, 2, 0, 3).reshape(4 * part, D)

    def whole(rows):
        return lax.all_gather(rows, "seq", axis=0, tiled=True)

    enc_qkv_w = whole(rows_of(0, 3))
    self_qkv_w = whole(rows_of(3, 3))
    self_out_w = whole(rows_of(6, 1))
    cross_qkv_w = whole(rows_of(7, 3))
    enc_out_w = whole(rows_of(10, 1))
    enc_up_w = whole(rows_of_wide(11))
    enc_down_w = whole(rows_of_tall(15))
    cross_out_w = whole(rows_of(19, 1))
    dec_up_w = whole(rows_of_wide(20))
    dec_down_w = whole(rows_of_tall(24))

    enc_gains_w = enc_gains.astype(bf16).astype(f32)
    dec_gains_w = dec_gains.astype(bf16).astype(f32)
    tokens = enc_input[0].astype(f32)
    row_count = tokens.shape[0]
    key_span = row_count + 2 * PASS
    passage = passage_ids[0]
    lengths = target_lengths[0]
    row_ids = lax.dynamic_slice_in_dim(passage, seq_index * row_count, row_count)
    key_ids = lax.dynamic_slice_in_dim(
        jnp.pad(passage, (PASS, PASS), constant_values=-1), seq_index * row_count, key_span
    )
    places = jnp.arange(key_span, dtype=jnp.int32)
    enc_blocks = row_ids.reshape(row_count // KEYS, KEYS)
    low_at = jnp.min(
        jnp.where(key_ids[None, :] == enc_blocks[:, :1], places[None, :], key_span), axis=1
    )
    high_at = jnp.max(
        jnp.where(key_ids[None, :] == enc_blocks[:, KEYS - 1 :], places[None, :], 0), axis=1
    )
    enc_spans = jnp.stack([low_at // KEYS, high_at // KEYS + 1], axis=1).reshape(-1)

    band_bucket = bias_bands()
    band_onehot = (
        jnp.arange(BUCKETS, dtype=jnp.int32)[:, None] == band_bucket[None, :]
    ).astype(f32)
    band = lax.dot_general(
        rel_table, band_onehot, (((0,), (0,)), ((), ())), precision=PRECISE,
        preferred_element_type=f32,
    ).reshape(HEADS, 5 * KEYS, KEYS)

    dec_tokens = dec_input[0].astype(f32)
    dec_rows = dec_tokens.shape[0]
    dec_total = dec_rows * seq_count
    slot_first = seq_index * dec_rows
    my_query = slot_first // TGT
    my_place = slot_first % TGT + jnp.arange(dec_rows, dtype=jnp.int32)
    my_length = lax.dynamic_index_in_dim(lengths, my_query, 0, keepdims=False)
    valid_rows = (my_place < my_length).astype(f32)[:, None]
    group_size = TGT // dec_rows
    groups = [
        list(range(first, first + group_size)) for first in range(0, seq_count, group_size)
    ]
    group_place = jnp.arange(TGT, dtype=jnp.int32)
    self_marks = jnp.where(group_place < my_length, group_place, FAR)
    self_spans = jnp.stack(
        [jnp.int32(0), (slot_first % TGT + dec_rows + KEYS - 1) // KEYS]
    ).astype(jnp.int32)

    dec_normed_one = norm_apply(dec_tokens, dec_gains_w[0]).astype(bf16)
    self_proj = matmul(dec_normed_one, self_qkv_w).astype(bf16)
    self_near = lax.all_gather(
        self_proj[:, D:], "seq", axis=0, tiled=True, axis_index_groups=groups
    )
    self_args = (self_proj, 0, self_near, 0, 1, my_place, self_marks, self_spans, None)
    self_mix_b, self_stat = attend(*self_args, dec_rows, True)
    dec_hidden = dec_tokens + matmul(self_mix_b, self_out_w)
    dec_normed_two = norm_apply(dec_hidden, dec_gains_w[1]).astype(bf16)
    cross_queries = matmul(dec_normed_two, cross_qkv_w[:, :D]).astype(bf16)
    all_queries = lax.all_gather(cross_queries, "seq", axis=0, tiled=True)

    normed_one = norm_apply(tokens, enc_gains_w[0]).astype(bf16)
    enc_proj = matmul(normed_one, enc_qkv_w).astype(bf16)
    forward = [(i, i + 1) for i in range(seq_count - 1)]
    backward = [(i + 1, i) for i in range(seq_count - 1)]
    own_kv = enc_proj[:, D:]
    enc_near = jnp.concatenate(
        [
            lax.ppermute(own_kv[row_count - PASS :], "seq", forward),
            own_kv,
            lax.ppermute(own_kv[:PASS], "seq", backward),
        ],
        axis=0,
    )
    enc_args = (enc_proj, 0, enc_near, 0, 1, row_ids, key_ids, enc_spans, band)
    enc_mixed_b, enc_stat = attend(*enc_args, KEYS, False)
    enc_hidden = tokens + matmul(enc_mixed_b, enc_out_w)
    normed_two = norm_apply(enc_hidden, enc_gains_w[1]).astype(bf16)
    enc_inner = matmul(normed_two, enc_up_w)
    enc_active = jax.nn.gelu(enc_inner).astype(bf16)
    encoded_b = (enc_hidden + matmul(enc_active, enc_down_w)).astype(bf16)
    cross_kv = matmul(encoded_b, cross_qkv_w[:, D:]).astype(bf16)

    key_owner = row_ids // PASS_N
    cross_rows = 256
    block_query = jnp.arange(dec_total // cross_rows, dtype=jnp.int32) * cross_rows // TGT
    own_first = jnp.sum(key_owner[None, :] < block_query[:, None], axis=1)
    own_last = jnp.sum(key_owner[None, :] <= block_query[:, None], axis=1)
    cross_spans = jnp.stack(
        [
            own_first // KEYS,
            jnp.where(own_last > own_first, (own_last + KEYS - 1) // KEYS, own_first // KEYS),
        ],
        axis=1,
    ).reshape(-1).astype(jnp.int32)
    slot_query = jnp.arange(dec_total, dtype=jnp.int32) // TGT
    cross_args = (all_queries, 0, cross_kv, 0, 1, slot_query, key_owner, cross_spans, None)
    part_mix, part_stat = attend(*cross_args, cross_rows, False)
    came_mix = lax.all_to_all(part_mix, "seq", 0, 0, tiled=True).reshape(seq_count, dec_rows, D)
    came_stat = lax.all_to_all(part_stat.T, "seq", 0, 0, tiled=True).reshape(
        seq_count, dec_rows, STATS
    )
    peak = jnp.max(came_stat, axis=0)
    shares = jnp.exp(came_stat - peak)
    total = jnp.sum(shares, axis=0)
    cross_stat = peak + jnp.log(total)
    shares = (shares / total)[:, :, :HEADS]
    cross_mix = jnp.sum(
        came_mix.astype(f32).reshape(seq_count, dec_rows, HEADS, HD) * shares[..., None], axis=0
    ).reshape(dec_rows, D)
    cross_mix_b = cross_mix.astype(bf16)
    dec_hidden_two = dec_hidden + matmul(cross_mix_b, cross_out_w)
    dec_normed_three = norm_apply(dec_hidden_two, dec_gains_w[2]).astype(bf16)
    dec_inner = matmul(dec_normed_three, dec_up_w)
    dec_active = jax.nn.gelu(dec_inner).astype(bf16)
    dec_final = dec_hidden_two + matmul(dec_active, dec_down_w)
    dec_output = (dec_final * valid_rows).astype(bf16)

    grad_final = cotangent[0].astype(f32) * valid_rows
    grad_final_b = grad_final.astype(bf16)
    grad_dec_down = grad_of(dec_active, grad_final_b)
    grad_dec_inner = gelu_back(dec_inner, back_of(grad_final_b, dec_down_w)).astype(bf16)
    grad_dec_up = grad_of(dec_normed_three, grad_dec_inner)
    grad_hidden_two, grad_gain_three = norm_back(
        dec_hidden_two, dec_gains_w[2], back_of(grad_dec_inner, dec_up_w)
    )
    grad_hidden_two = grad_hidden_two + grad_final
    grad_cross_b = grad_hidden_two.astype(bf16)
    grad_cross_out = grad_of(cross_mix_b, grad_cross_b)
    grad_cross_mix = back_of(grad_cross_b, cross_out_w).astype(bf16)
    cross_dot = per_head_dot(grad_cross_mix, cross_mix)
    all_grads = lax.all_gather(grad_cross_mix, "seq", axis=0, tiled=True)
    all_stats = lax.all_gather(
        jnp.concatenate([cross_stat, cross_dot.T], axis=1), "seq", axis=0, tiled=True
    ).T
    part_dq, cross_dk, cross_dv = attend_back(
        *cross_args, cross_rows, False, all_grads, all_stats[:STATS], all_stats[STATS:]
    )
    grad_cross_q_b = lax.psum_scatter(part_dq, "seq", scatter_dimension=0, tiled=True)
    grad_cross_qw = grad_of(dec_normed_two, grad_cross_q_b)
    grad_hidden, grad_gain_two = norm_back(
        dec_hidden, dec_gains_w[1], back_of(grad_cross_q_b, cross_qkv_w[:, :D])
    )
    grad_hidden = grad_hidden + grad_hidden_two
    cross_kv_grad = jnp.concatenate([cross_dk, cross_dv], axis=1)
    grad_cross_kvw = grad_of(encoded_b, cross_kv_grad)
    grad_encoded = back_of(cross_kv_grad, cross_qkv_w[:, D:])
    grad_cross_qkv = jnp.concatenate([grad_cross_qw, grad_cross_kvw], axis=1)
    grad_self_b = grad_hidden.astype(bf16)
    grad_self_out = grad_of(self_mix_b, grad_self_b)
    grad_self_mix = back_of(grad_self_b, self_out_w).astype(bf16)
    self_dot = per_head_dot(grad_self_mix, self_mix_b)
    self_dq, self_dk, self_dv = attend_back(
        *self_args, dec_rows, True, grad_self_mix, self_stat, self_dot
    )
    self_dkv = lax.psum_scatter(
        jnp.concatenate([self_dk, self_dv], axis=1),
        "seq",
        scatter_dimension=0,
        tiled=True,
        axis_index_groups=groups,
    )
    self_grad_b = jnp.concatenate([self_dq, self_dkv], axis=1)
    grad_self_qkv = grad_of(dec_normed_one, self_grad_b)
    grad_dec_in, grad_gain_one = norm_back(
        dec_tokens, dec_gains_w[0], back_of(self_grad_b, self_qkv_w)
    )
    grad_dec_in = grad_dec_in + grad_hidden
    grad_dec_gains = jnp.stack([grad_gain_one, grad_gain_two, grad_gain_three])

    grad_encoded_b = grad_encoded.astype(bf16)
    grad_enc_down = grad_of(enc_active, grad_encoded_b)
    grad_enc_inner = gelu_back(enc_inner, back_of(grad_encoded_b, enc_down_w)).astype(bf16)
    grad_enc_up = grad_of(normed_two, grad_enc_inner)
    grad_enc_hidden, grad_enc_gain_two = norm_back(
        enc_hidden, enc_gains_w[1], back_of(grad_enc_inner, enc_up_w)
    )
    grad_enc_hidden = grad_enc_hidden + grad_encoded
    grad_attn_b = grad_enc_hidden.astype(bf16)
    grad_enc_out = grad_of(enc_mixed_b, grad_attn_b)
    grad_enc_mix = back_of(grad_attn_b, enc_out_w).astype(bf16)
    enc_dot = per_head_dot(grad_enc_mix, enc_mixed_b)
    enc_dq, enc_dk, enc_dv, grad_band = attend_back(
        *enc_args, KEYS, False, grad_enc_mix, enc_stat, enc_dot
    )
    table_part = lax.dot_general(
        band_onehot,
        grad_band.reshape(HEADS, -1),
        (((1,), (1,)), ((), ())),
        precision=PRECISE,
        preferred_element_type=f32,
    )
    near_grad = jnp.concatenate([enc_dk, enc_dv], axis=1)
    from_higher = lax.ppermute(near_grad[:PASS], "seq", backward)
    from_lower = lax.ppermute(near_grad[key_span - PASS :], "seq", forward)
    own_grad = near_grad[PASS : PASS + row_count].astype(f32)
    own_grad = own_grad.at[row_count - PASS :].add(from_higher.astype(f32))
    own_grad = own_grad.at[:PASS].add(from_lower.astype(f32))
    enc_grad_b = jnp.concatenate([enc_dq, own_grad.astype(bf16)], axis=1)
    grad_enc_qkv = grad_of(normed_one, enc_grad_b)
    grad_enc_in, grad_enc_gain_one = norm_back(
        tokens, enc_gains_w[0], back_of(enc_grad_b, enc_qkv_w)
    )
    grad_enc_in = grad_enc_in + grad_enc_hidden
    grad_enc_gains = jnp.stack([grad_enc_gain_one, grad_enc_gain_two])
    grads = (
        grad_dec_down,
        grad_dec_up,
        grad_cross_out,
        grad_cross_qkv,
        grad_self_out,
        grad_self_qkv,
        grad_enc_down,
        grad_enc_up,
        grad_enc_out,
        grad_enc_qkv,
    )
    grads = [grad.astype(bf16) for grad in grads]
    gains_part = jnp.concatenate([grad_enc_gains, grad_dec_gains], axis=0)
    if dp_count == 2 and seq_count == 16:
        table_row = jnp.pad(table_part.reshape(1, -1), ((0, 0), (0, D - BUCKETS * HEADS)))
        small = jnp.concatenate([gains_part, table_row], axis=0)
        small = jnp.pad(small, ((0, SMALL - small.shape[0]), (0, 0)))
        sums, small = reduce_all(grads, small)
        gains_total = small[:5]
        table_grad = small[5, : BUCKETS * HEADS].reshape(BUCKETS, HEADS)
    else:
        gains_total, table_grad = lax.psum((gains_part, table_part), ("dp", "seq"))
        sums = reduce_plainly(grads)

    def threes(rows):
        return rows.reshape(part, 3, wide).transpose(1, 0, 2)

    return (
        dec_output[None],
        grad_enc_in[None],
        grad_dec_in[None],
        gains_total[:2],
        threes(sums[9]),
        sums[8],
        table_grad,
        sums[7],
        sums[6],
        gains_total[2:],
        threes(sums[5]),
        sums[4],
        threes(sums[3]),
        sums[2],
        sums[1],
        sums[0],
    )


def solution(mesh):
    rows = P("dp", "seq", None)
    three = P(None, "seq", "dp")
    two = P("seq", "dp")
    placed = (rows, rows, P("dp", None), P("dp", None), rows)
    placed = placed + (P(), three, two, P(), two, two, P(), three, two, three, two, two, two)
    return jax.shard_map(
        per_device,
        mesh=mesh,
        in_specs=placed,
        out_specs=(rows, rows, rows) + placed[5:],
        check_vma=False,
    )
```

time: 2790 us -> 1060 us (0.38)
  waiting for transfers between devices: 1540 us -> 487 us
  local copies, waits for them, and re-layouts: 573 us -> 69.1 us
  Pallas kernels: 0 us -> 284 us
  matrix products: 356 us -> 114 us
  starting transfers between devices: 94.2 us -> 15.6 us
  blocking collectives: 109 us -> 32 us
  other arithmetic: 84.1 us -> 33.3 us
    reduce_scatter x14 -> x2, waiting for transfers between devices: 509 us -> 14 us  [the longest x1 14 us: per_device(): lax.psum_scatter(jnp.concatenate([self_dk, self_dv], axis=1), 'seq', scat...]
    unnamed x39 -> x16, waiting for transfers between devices: 443 us -> 0.26 us
    ppermute x162 -> x4, waiting for transfers between devices: 327 us -> 0.01 us  [the longest x1 0.01 us: per_device(): lax.ppermute(own_kv[row_count - PASS:], 'seq', forward)]
    pallas_call x0 -> x7, Pallas kernels: none -> 284 us  [the longest x1 160 us: reduce_all(): pl.pallas_call(functools.partial(reduce_kernel, plan, len(grads)), in_spe...]
    unnamed x365 -> x260, local copies, waits for them, and re-layouts: 287 us -> 25.7 us
    dot_general x159 -> x13, matrix products: 298 us -> 45.5 us  [the longest x11 35.1 us: matmul(): return jnp.dot(left_side, right_side, preferred_element_type=f32)]
    all_gather x17 -> x14, waiting for transfers between devices: 262 us -> 419 us  [the longest x10 329 us: whole(): return lax.all_gather(rows, 'seq', axis=0, tiled=True)]
    ppermute x162 -> x4, starting transfers between devices: 92 us -> 10.5 us  [the longest x1 4.3 us: per_device(): lax.ppermute(own_kv[row_count - PASS:], 'seq', forward)]
  transfers between devices with their start and end apart: 197 -> 21, of which waited for: 73 -> 14; matrix products, arithmetic and copies ran while one was open for 31% -> 16% of each run, Pallas kernels for 0% -> 9%
where the time goes in v1:
time: 1060 us; the launch traced here: 1050 us
  waiting for transfers between devices  487 us (46%)
  Pallas kernels  284 us (27%)
  matrix products  114 us (11%)
  local copies, waits for them, and re-layouts  69.1 us (7%)
  other arithmetic  33.3 us (3%)
  blocking collectives  32 us (3%)
  between operations  15.8 us (1%)
  starting transfers between devices  15.6 us (1%)
    all_gather x10, waiting for transfers between devices, whole(): return lax.all_gather(rows, 'seq', axis=0, tiled=True)  329 us
    pallas_call x1, Pallas kernels, reduce_all(): pl.pallas_call(functools.partial(reduce_kernel, plan, len(grads)), in_spe...  160 us
    pallas_call x3, Pallas kernels, attend_back(): pl.pallas_call(functools.partial(attend_back_kernel, causal, bias is not...  70.7 us
    all_to_all x1, waiting for transfers between devices, per_device(): lax.all_to_all(part_mix, 'seq', 0, 0, tiled=True)  53.5 us
    pallas_call x3, Pallas kernels, attend(): pl.pallas_call(functools.partial(attend_kernel, causal, bias is not None)...  53 us
    dot_general x11, matrix products, grad_of(): lax.dot_general(left_side, right_side, (((0,), (0,)), ((), ())), preferre...  37.9 us
    all_gather x1, waiting for transfers between devices, per_device(): packed = lax.all_gather(jnp.concatenate(pieces, axis=0), 'dp', axis=0)  35.6 us
    dot_general x11, matrix products, matmul(): return jnp.dot(left_side, right_side, preferred_element_type=f32)  35.1 us
  transfers between devices with their start and end apart: 21, of which 14 were waited for; matrix products, arithmetic and copies ran while one was open for 16% of the time, Pallas kernels for 9%

profile of v1, /device:TPU:0, one launch (start us, length us, event | category | flops | bytes accessed | tf_op | source)
XLA Modules:
  0.0 1050.3 jit_solution(6417521401434447254)
XLA Ops:
  12.7 35.6 %all-gather.43.cloned.1.call-done = bf16[2688,384]{1,0:T(8,128)(2,1)} async-done(((bf16[1344,384]{1,0:T(8,128)(2,1)}), bf16[2688,384]{1,0:T(8,128)(2,1)}) %all-gather.43.cloned.1.call-update) | async-done | bytes 2064400 | tf_op jit(solution)/shard_map/all_gather | solution.py:621
  50.8 47.5 %all-gather.17.cloned.1.call-done = bf16[768,2304]{1,0:T(8,128)(2,1)} async-done(((bf16[48,2304]{1,0:T(8,128)(2,1)}), bf16[768,2304]{1,0:T(8,128)(2,1)}) %all-gather.17.cloned.1.call-update) | async-done | bytes 3538960 | tf_op jit(solution)/shard_map/all_gather | solution.py:634
  112.4 11.2 %all-gather.19.cloned.1.call-done.k_ref.v_ref = bf16[768,1536]{1,0:T(8,128)(2,1)} async-done(((bf16[96,1536]{1,0:T(8,128)(2,1)}), bf16[768,1536]{1,0:T(8,128)(2,1)}) %all-gather.19.cloned.1.call-update) | async-done | bytes 2359312 | tf_op jit(solution)/shard_map/all_gather | solution.py:697
  129.3 35.3 %all-gather.21.cloned.1.call-done = bf16[768,768]{1,0:T(8,128)(2,1)} async-done(((bf16[48,768]{1,0:T(8,128)(2,1)}), bf16[768,768]{1,0:T(8,128)(2,1)}) %all-gather.21.cloned.1.call-update) | async-done | bytes 1179664 | tf_op jit(solution)/shard_map/all_gather | solution.py:634
  166.5 47.0 %all-gather.23.cloned.1.call-done = bf16[768,2304]{1,0:T(8,128)(2,1)} async-done(((bf16[48,2304]{1,0:T(8,128)(2,1)}), bf16[768,2304]{1,0:T(8,128)(2,1)}) %all-gather.23.cloned.1.call-update) | async-done | bytes 3538960 | tf_op jit(solution)/shard_map/all_gather | solution.py:634
  222.6 39.8 %all-gather.27.cloned.1.call-done = bf16[768,2304]{1,0:T(8,128)(2,1)} async-done(((bf16[48,2304]{1,0:T(8,128)(2,1)}), bf16[768,2304]{1,0:T(8,128)(2,1)}) %all-gather.27.cloned.1.call-update) | async-done | bytes 3538960 | tf_op jit(solution)/shard_map/all_gather | solution.py:634
  294.8 31.8 %shard_map.308 = (bf16[384,768]{1,0:T(8,128)(2,1)}, f32[16,384]{1,0:T(8,128)}) custom-call(s32[6]{0:T(128)} %reshape.734.spans_ref, bf16[384,2304]{1,0:T(8,128)(2,1)} %copy-done.4, bf16[1152,1536]{1,0:T(8,128)(2,1)} %pad_maximum_fusion.k_ref.v_ref, bf16[1152,1536]{1,0:T(8,128)(2,1)} %pad_maximum_fusion.k_ref.v_ref, s32[3,1,128]{2,1,0:T(1,128)} %get-tuple-element.230.row_ref, ...), custom_call_target="tpu_custom_call" | custom-call | flops 452984832 | bytes 7077888 | tf_op jit(solution)/shard_map/pallas_call | solution.py:168
  328.8 35.9 %all-gather.31.cloned.1.call-done = bf16[768,3072]{1,0:T(8,128)(2,1)} async-done(((bf16[48,3072]{1,0:T(8,128)(2,1)}), bf16[768,3072]{1,0:T(8,128)(2,1)}) %all-gather.31.cloned.1.call-update) | async-done | bytes 4718608 | tf_op jit(solution)/shard_map/all_gather | solution.py:634
  371.3 48.0 %all-gather.33.cloned.1.call-done = bf16[3072,768]{1,0:T(8,128)(2,1)} async-done(((bf16[192,768]{1,0:T(8,128)(2,1)}), bf16[3072,768]{1,0:T(8,128)(2,1)}) %all-gather.33.cloned.1.call-update) | async-done | bytes 4718608 | tf_op jit(solution)/shard_map/all_gather | solution.py:634
  428.2 34.7 %all-gather.25.cloned.1.call-done.q_ref = bf16[1536,768]{1,0:T(8,128)(2,1)} async-done(((bf16[96,768]{1,0:T(8,128)(2,1)}), bf16[1536,768]{1,0:T(8,128)(2,1)}) %all-gather.25.cloned.1.call-update) | async-done | bytes 2359312 | tf_op jit(solution)/shard_map/all_gather | solution.py:705
  463.0 15.5 %shard_map.309 = (bf16[1536,768]{1,0:T(8,128)(2,1)}, f32[16,1536]{1,0:T(8,128)}) custom-call(s32[12]{0:T(128)} %reshape.731.spans_ref, bf16[1536,768]{1,0:T(8,128)(2,1)} %all-gather.25.cloned.1.call-done.q_ref, bf16[384,1536]{1,0:T(8,128)(2,1)} %convolution_convert_fusion.9.k_ref.v_ref, bf16[384,1536]{1,0:T(8,128)(2,1)} %convolution_convert_fusion.9.k_ref.v_ref, ...), custom_call_target="tpu_custom_call" | custom-call | flops 603979776 | bytes 2359296 | tf_op jit(solution)/shard_map/pallas_call | solution.py:168
  479.5 12.3 %all_to_all.18 = f32[16,96,16]{1,2,0:T(8,128)S(1)} all-to-all(f32[16,96,16]{1,2,0:T(8,128)S(1)} %copy.139), channel_id=1, replica_groups=mesh['dp'=2,'seq'=16] {'seq'}, dimensions={0} | all-to-all | bytes 196608 | tf_op jit(solution)/shard_map/all_to_all | solution.py:745
  498.2 53.5 %all-to-all-done = bf16[16,96,768]{2,1,0:T(8,128)(2,1)} async-done(((bf16[16,96,768]{2,1,0:T(8,128)(2,1)}), bf16[16,96,768]{2,1,0:T(8,128)(2,1)}, u32[]{:S(2)}, u32[]{:S(2)}) %all-to-all-start) | async-done | bytes 2359328 | tf_op jit(solution)/shard_map/all_to_all | solution.py:744
  559.3 24.8 %all-gather.37.cloned.1.call-done = bf16[768,3072]{1,0:T(8,128)(2,1)} async-done(((bf16[48,3072]{1,0:T(8,128)(2,1)}), bf16[768,3072]{1,0:T(8,128)(2,1)}) %all-gather.37.cloned.1.call-update) | async-done | bytes 4718608 | tf_op jit(solution)/shard_map/all_gather | solution.py:634
  587.4 50.9 %all-gather.39.cloned.1.call-done = bf16[3072,768]{1,0:T(8,128)(2,1)} async-done(((bf16[192,768]{1,0:T(8,128)(2,1)}), bf16[3072,768]{1,0:T(8,128)(2,1)}) %all-gather.39.cloned.1.call-update) | async-done | bytes 4718608 | tf_op jit(solution)/shard_map/all_gather | solution.py:634
  647.1 19.8 %all-gather.1 = f32[16,96,32]{1,2,0:T(8,128)S(1)} all-gather(f32[1,96,32]{1,2,0:T(8,128)S(1)} %fusion.75), channel_id=1, replica_groups=mesh['dp'=2,'seq'=16] {'seq'}, dimensions={0}, use_global_device_ids=true | all-gather | bytes 208896 | tf_op jit(solution)/shard_map/all_gather | solution.py:778
  679.0 8.2 all-gather.41.cloned.1.call-done.do_ref
  687.1 30.6 %shard_map.310 = (bf16[1536,768]{1,0:T(8,128)(2,1)}, bf16[384,768]{1,0:T(8,128)(2,1)}, bf16[384,768]{1,0:T(8,128)(2,1)}) custom-call(s32[12]{0:T(128)} %reshape.731.spans_ref, bf16[1536,768]{1,0:T(8,128)(2,1)} %all-gather.25.cloned.1.call-done.q_ref, bf16[384,1536]{1,0:T(8,128)(2,1)} %convolution_convert_fusion.9.k_ref.v_ref, ...), custom_call_target="tpu_custom_call" | custom-call | flops 1509949440 | bytes 4718592 | tf_op jit(solution)/shard_map/pallas_call | solution.py:308
  722.3 8.3 fusion.11
  741.5 33.2 %shard_map.311 = (bf16[384,768]{1,0:T(8,128)(2,1)}, bf16[1152,768]{1,0:T(8,128)(2,1)}, bf16[1152,768]{1,0:T(8,128)(2,1)}, f32[12,640,128]{2,1,0:T(8,128)}) custom-call(s32[6]{0:T(128)} %reshape.734.spans_ref, bf16[384,2304]{1,0:T(8,128)(2,1)} %copy-done.4, bf16[1152,1536]{1,0:T(8,128)(2,1)} %pad_maximum_fusion.k_ref.v_ref, ...), custom_call_target="tpu_custom_call" | custom-call | flops 1132462080 | bytes 14155776 | tf_op jit(solution)/shard_map/pallas_call | solution.py:308
  801.5 6.9 shard_map.312
  825.6 7.5 convolution_convert_fusion.2
  848.9 14.0 %reduce-scatter.5.cloned.1.call-done = bf16[96,1536]{1,0:T(8,128)(2,1)} async-done(((bf16[768,1536]{1,0:T(8,128)(2,1)}), bf16[96,1536]{1,0:T(8,128)(2,1)}) %reduce-scatter.5.cloned.1.call-update) | async-done | bytes 294928 | tf_op jit(solution)/shard_map/reduce_scatter | solution.py:801
  869.1 160.3 %reduce_all.1 = (f32[192,384]{1,0:T(8,128)}, f32[48,1536]{1,0:T(8,128)}, f32[48,384]{1,0:T(8,128)}, f32[48,1152]{1,0:T(8,128)}, f32[48,384]{1,0:T(8,128)}, /*ind...) custom-call(bf16[2,2,2,2,192,768]{5,4,3,2,1,0:T(8,128)(2,1)} %bitcas, ...), custom_call_target="tpu_custom_call" | custom-call | tf_op jit(solution)/shard_map/reduce_all/pallas_call | solution.py:539
  (452 shorter events, 221.9 us)
Async XLA Ops:
  7.2 273.8 %copy-start = (f32[32,12]{0,1:T(8,128)S(1)}, f32[32,12]{0,1:T(8,128)}, u32[]{:S(2)}) copy-start(f32[32,12]{0,1:T(8,128)} %param.34) | copy-start | bytes 4612
  7.2 41.0 %all-gather.43.cloned.1.call-start = ((), (), s32[]{:S(2)}) async-start(), calls=%async_computation.19 | async-start | bytes 3096576 | tf_op jit(solution)/shard_map/all_gather | solution.py:621
  12.7 85.7 %all-gather.17.cloned.1.call-start = ((), (), s32[]{:S(2)}) async-start(), calls=%async_computation.4 | async-start | bytes 3760128 | tf_op jit(solution)/shard_map/all_gather | solution.py:634
  50.5 73.0 %all-gather.19.cloned.1.call-start = ((), (), s32[]{:S(2)}) async-start(), calls=%async_computation.5 | async-start | bytes 2654208 | tf_op jit(solution)/shard_map/all_gather | solution.py:697
  50.6 162.9 %copy-start.55 = (f32[768]{0:T(1024)}, f32[768]{0:T(1024)S(1)}, u32[]{:S(2)}) copy-start(f32[768]{0:T(1024)S(1)} %get-tuple-element.201) | copy-start | bytes 9220
  102.1 62.5 %all-gather.21.cloned.1.call-start = ((), (), s32[]{:S(2)}) async-start(), calls=%async_computation.6 | async-start | bytes 1253376 | tf_op jit(solution)/shard_map/all_gather | solution.py:634
  102.9 110.6 %all-gather.23.cloned.1.call-start = ((), (), s32[]{:S(2)}) async-start(), calls=%async_computation.7 | async-start | bytes 3760128 | tf_op jit(solution)/shard_map/all_gather | solution.py:634
  104.0 158.4 %all-gather.27.cloned.1.call-start = ((), (), s32[]{:S(2)}) async-start(), calls=%async_computation.9 | async-start | bytes 3760128 | tf_op jit(solution)/shard_map/all_gather | solution.py:634
  105.1 221.5 %all-gather.29.cloned.1.call-start = ((), (), s32[]{:S(2)}) async-start(), calls=%async_computation.10 | async-start | bytes 1253376 | tf_op jit(solution)/shard_map/all_gather | solution.py:634
  105.9 258.8 %all-gather.31.cloned.1.call-start = ((), (), s32[]{:S(2)}) async-start(), calls=%async_computation.11 | async-start | bytes 5013504 | tf_op jit(solution)/shard_map/all_gather | solution.py:634
  107.8 311.5 %all-gather.33.cloned.1.call-start = ((), (), s32[]{:S(2)}) async-start(), calls=%async_computation.12 | async-start | bytes 5013504 | tf_op jit(solution)/shard_map/all_gather | solution.py:634
  109.0 354.0 %all-gather.25.cloned.1.call-start = ((), (), s32[]{:S(2)}) async-start(), calls=%async_computation.8 | async-start | bytes 2506752 | tf_op jit(solution)/shard_map/all_gather | solution.py:705
  215.9 341.6 %all-gather.35.cloned.1.call-start = ((), (), s32[]{:S(2)}) async-start(), calls=%async_computation.13 | async-start | bytes 1253376 | tf_op jit(solution)/shard_map/all_gather | solution.py:634
  216.7 367.4 %all-gather.37.cloned.1.call-start = ((), (), s32[]{:S(2)}) async-start(), calls=%async_computation.14 | async-start | bytes 5013504 | tf_op jit(solution)/shard_map/all_gather | solution.py:634
  217.9 420.5 %all-gather.39.cloned.1.call-start = ((), (), s32[]{:S(2)}) async-start(), calls=%async_computation.15 | async-start | bytes 5013504 | tf_op jit(solution)/shard_map/all_gather | solution.py:634
  266.2 25.1 %collective-permute-start.1 = (bf16[384,1536]{1,0:T(8,128)(2,1)S(1)}, bf16[384,1536]{1,0:T(8,128)(2,1)}, u32[]{:S(2)}, u32[]{:S(2)}) collective-permute-start(bf16[384,1536]{1,0:T(8,128)(2,1)S(1)} %slice.311), channel_id=1, source_target_pairs={{1,0},{2,1},{3,2},{4,3},{5,4},{6,5},{7,6},{8,7},{9,8},{10,9},{11,1... | collective-permute-start | bytes 3538952 | tf_op jit(solution)/shard_map/ppermute | solution.py:716
  267.5 23.8 %collective-permute-start = (bf16[384,1536]{1,0:T(8,128)(2,1)S(1)}, bf16[384,1536]{1,0:T(8,128)(2,1)}, u32[]{:S(2)}, u32[]{:S(2)}) collective-permute-start(bf16[384,1536]{1,0:T(8,128)(2,1)S(1)} %slice.311), channel_id=1, source_target_pairs={{0,1},{1,2},{2,3},{3,4},{4,5},{5,6},{6,7},{7,8},{8,9},{9,10},{10,1... | collective-permute-start | bytes 3538952 | tf_op jit(solution)/shard_map/ppermute | solution.py:714
  491.8 60.0 %all-to-all-start = ((bf16[16,96,768]{2,1,0:T(8,128)(2,1)}), bf16[16,96,768]{2,1,0:T(8,128)(2,1)}, u32[]{:S(2)}, u32[]{:S(2)}) async-start(bf16[16,96,768]{2,1,0:T(8,128)(2,1)} %bitcast.274), calls=%async_computation | async-start | bytes 4718592 | tf_op jit(solution)/shard_map/all_to_all | solution.py:744
  496.2 190.9 %all-gather.41.cloned.1.call-start = ((), (), s32[]{:S(2)}) async-start(), calls=%async_computation.16 | async-start | bytes 2506752 | tf_op jit(solution)/shard_map/all_gather | solution.py:777
  645.8 148.4 %reduce-scatter.3.cloned.1.call-start = ((), (), s32[]{:S(2)}) async-start(), calls=%async_computation.17 | async-start | bytes 2506752 | tf_op jit(solution)/shard_map/reduce_scatter | solution.py:784
  718.9 144.1 %reduce-scatter.5.cloned.1.call-start = ((), (), s32[]{:S(2)}) async-start(), calls=%async_computation.18 | async-start | bytes 2654208 | tf_op jit(solution)/shard_map/reduce_scatter | solution.py:801
  779.7 53.4 %collective-permute-start.3 = (bf16[384,1536]{1,0:T(8,128)(2,1)}, bf16[384,1536]{1,0:T(8,128)(2,1)}, u32[]{:S(2)}, u32[]{:S(2)}) collective-permute-start(bf16[384,1536]{1,0:T(8,128)(2,1)} %get-tuple-element.217), channel_id=1, source_target_pairs={{0,1},{1,2},{2,3},{3,4},{4,5},{5,6},{6,7},{7,8},{8,9},{9,10},{10,1... | collective-permute-start | bytes 3538952 | tf_op jit(solution)/shard_map/ppermute | solution.py:840
  783.0 50.1 %collective-permute-start.2 = (bf16[384,1536]{1,0:T(8,128)(2,1)}, bf16[384,1536]{1,0:T(8,128)(2,1)}, u32[]{:S(2)}, u32[]{:S(2)}) collective-permute-start(bf16[384,1536]{1,0:T(8,128)(2,1)} %get-tuple-element.216), channel_id=1, source_target_pairs={{1,0},{2,1},{3,2},{4,3},{5,4},{6,5},{7,6},{8,7},{9,8},{10,9},{11,1... | collective-permute-start | bytes 3538952 | tf_op jit(solution)/shard_map/ppermute | solution.py:839
  869.1 163.7 %copy-start.92 = (f32[96]{0:T(128)S(1)}, f32[96]{0:T(128)}, u32[]{:S(2)}) copy-start(f32[96]{0:T(128)} %copy-done.91) | copy-start | bytes 1156
  (102 other events, 1210.6 us)
Sparse Core Ops, SparseCore 0:
  12.8 35.4 all-gather.42
  51.1 47.1 all-gather.16
  102.2 21.2 all-gather.18
  126.2 38.3 all-gather.20
  167.3 46.1 all-gather.22
  216.2 46.1 all-gather.26
  265.3 44.1 all-gather.28
  312.3 52.3 all-gather.30
  367.5 51.7 all-gather.32
  422.1 40.8 all-gather.24
  465.8 50.0 all-gather.34
  518.6 65.4 all-gather.36
  587.0 51.3 all-gather.38
  645.9 41.1 all-gather.40
  719.0 67.1 reduce-scatter.2
  811.9 51.0 reduce-scatter.4

commit v2 on v1

--- a/solution.py
+++ b/solution.py
@@ -330,28 +330,227 @@
 ORDERS = ((COLUMN, ROW, LOW, HIGH), (ROW, COLUMN, LOW, HIGH), (LOW, HIGH, ROW, COLUMN))
 LAGS = (0, 4, 9, 13, 16)
 SMALL = 16
-
-
-def reduce_plan(shapes):
+EVERYONE = (CORE, ROW, LOW, HIGH, COLUMN)
+
+
+SPREAD = (
+    (HIGH, LOW, ROW, COLUMN),
+    (HIGH, LOW, COLUMN, ROW),
+    (COLUMN, ROW, HIGH, LOW),
+    (ROW, COLUMN, HIGH, LOW),
+)
+SPREAD_SHARES = (0.39, 0.39, 0.11, 0.11)
+SPREAD_LAGS = (-6, 0, 4, 8, 14)
+
+
+def chunks_of(shapes):
     chunks = []
     for source, (rows, columns) in enumerate(shapes):
         if rows > 48:
             for first in range(0, rows, 96):
                 chunks.append((source, first, 96, 0, columns // 2))
-        elif columns == 3 * D:
+        elif columns in (2 * D, 3 * D):
             for first in range(0, columns, D):
                 chunks.append((source, 0, rows, first, D // 2))
         else:
             chunks.append((source, 0, rows, 0, columns // 2))
+    return chunks
+
+
+def ordered(chunks, orders, shares):
     plan = []
-    sizes = [0, 0, 0]
+    sizes = [0] * len(orders)
     for chunk in chunks:
-        size = chunk[2] * chunk[4]
-        shares = (sizes[0] / 0.39, sizes[1] / 0.39, sizes[2] / 0.22)
-        order = shares.index(min(shares))
-        sizes[order] += size
-        plan.append(chunk + (ORDERS[order],))
+        loads = [size / share for size, share in zip(sizes, shares)]
+        order = loads.index(min(loads))
+        sizes[order] += chunk[2] * chunk[4]
+        plan.append(chunk + (orders[order],))
     return plan
+
+
+def position():
+    dp = lax.axis_index("dp")
+    seq = lax.axis_index("seq")
+
+    def bit_of(axis):
+        return dp if axis == COLUMN else (seq // axis) % 2
+
+    def partner(axis):
+        if axis == COLUMN:
+            return (1 - dp, seq)
+        return (dp, seq + axis * (1 - 2 * bit_of(axis)))
+
+    return bit_of, partner
+
+
+def meet(partner):
+    barrier = pltpu.get_barrier_semaphore()
+    for axis in EVERYONE:
+        pl.semaphore_signal(
+            barrier, inc=1, device_id=partner(axis), device_id_type=pl.DeviceIdType.MESH
+        )
+    pl.semaphore_wait(barrier, len(EVERYONE))
+
+
+def spread_kernel(plan, count, late, *refs):
+    shards = refs[:count]
+    late_shards = refs[count : count + late]
+    refs = refs[count + late :]
+    wholes = refs[:count]
+    late_rows = refs[count : count + late]
+    send_sem, recv_sem, own_sem = refs[count + late :]
+    bit_of, partner = position()
+    meet(partner)
+
+    def region(item, known, other=None):
+        source, row, rows, column, half, order = plan[item]
+
+        def bit(axis):
+            return 1 - bit_of(axis) if axis == other else bit_of(axis)
+
+        at = [slice(None) if axis in known else bit(axis) for axis in (HIGH, LOW, ROW, CORE)]
+        if COLUMN in known or len(order) == 3:
+            lanes = pl.ds(column, 2 * half)
+        else:
+            lanes = pl.ds(pl.multiple_of(column + bit(COLUMN) * half, 128), half)
+        return wholes[source].at[tuple(at) + (pl.ds(row, rows), lanes)]
+
+    def own_part(item):
+        source, row, rows, column, half, order = plan[item]
+        if len(order) == 3:
+            return shards[source].at[pl.ds(row, rows), pl.ds(column, 2 * half)]
+        return shards[source].at[pl.ds(row, rows), pl.ds(column // 2, half)]
+
+    def own_copy(item):
+        return pltpu.make_async_copy(own_part(item), region(item, ()), own_sem.at[item])
+
+    def remote(source, target, item, place, axis):
+        return pltpu.make_async_remote_copy(
+            src_ref=source,
+            dst_ref=target,
+            send_sem=send_sem.at[item, place],
+            recv_sem=recv_sem.at[item, place],
+            device_id=partner(axis),
+            device_id_type=pl.DeviceIdType.MESH,
+        )
+
+    def stage_copy(item, stage):
+        order = plan[item][5]
+        held = region(item, order[:stage])
+        return remote(own_part(item) if stage == 0 else held, held, item, stage, order[stage])
+
+    def core_copy(item, stage):
+        order = plan[item][5]
+        if stage == 0:
+            return remote(own_part(item), region(item, ()), item, 4, CORE)
+        held = region(item, order[: stage - 1], order[stage - 1])
+        return remote(held, held, item, 4 + stage, CORE)
+
+    def late_part(item):
+        half = late_shards[item].shape[1]
+        lanes = pl.ds(pl.multiple_of(bit_of(COLUMN) * half, 128), half)
+        return late_rows[item].at[:, lanes]
+
+    def late_own(item):
+        return pltpu.make_async_copy(
+            late_shards[item], late_part(item), own_sem.at[len(plan) + item]
+        )
+
+    def late_copy(item):
+        return remote(late_shards[item], late_part(item), len(plan) + item, 0, COLUMN)
+
+    for item in range(late):
+        late_own(item).start()
+        late_copy(item).start()
+    events = sorted(
+        (item + SPREAD_LAGS[stage + 1], stage, item)
+        for item in range(len(plan))
+        for stage in range(-1, len(plan[item][5]))
+    )
+    for unused, stage, item in events:
+        if stage < 0:
+            stage_copy(item, 0).start()
+            own_copy(item).start()
+            core_copy(item, 0).start()
+            continue
+        if stage == 0:
+            own_copy(item).wait()
+        stage_copy(item, stage).wait_recv()
+        if stage + 1 < len(plan[item][5]):
+            stage_copy(item, stage + 1).start()
+        core_copy(item, stage + 1).start()
+    for item in range(len(plan)):
+        for stage in range(len(plan[item][5])):
+            stage_copy(item, stage).wait_send()
+            core_copy(item, stage).wait()
+        core_copy(item, len(plan[item][5])).wait()
+    for item in range(late):
+        late_own(item).wait()
+        late_copy(item).wait()
+
+
+def spread(shards, late, rows, collective_id):
+    shapes = [(shard.shape[0], 2 * shard.shape[1]) for shard in shards]
+    late_shapes = [(shard.shape[0], 2 * shard.shape[1]) for shard in late]
+    marks = len(late)
+    plan = ordered(chunks_of(shapes), SPREAD, SPREAD_SHARES)
+    if rows is not None:
+        count, columns = rows.shape
+        for half, order in enumerate(SHARE):
+            first = half * columns // 2
+            plan.insert(half, (len(shards), 0, count, first, columns // 4, order))
+        shards = shards + [rows]
+        shapes.append(rows.shape)
+    space = pl.BlockSpec(memory_space=pl.ANY)
+    results = pl.pallas_call(
+        functools.partial(spread_kernel, plan, len(shards), len(late)),
+        in_specs=[space] * (len(shards) + len(late)),
+        out_specs=[space] * (len(shards) + len(late)),
+        out_shape=[
+            jax.ShapeDtypeStruct((2, 2, 2, 2, rows, columns), bf16) for rows, columns in shapes
+        ]
+        + [jax.ShapeDtypeStruct(shape, bf16) for shape in late_shapes],
+        scratch_shapes=[
+            pltpu.SemaphoreType.DMA((len(plan) + marks, 9)),
+            pltpu.SemaphoreType.DMA((len(plan) + marks, 9)),
+            pltpu.SemaphoreType.DMA((len(plan) + marks,)),
+        ],
+        compiler_params=pltpu.CompilerParams(
+            collective_id=collective_id, has_side_effects=True, vmem_limit_bytes=16 * 1024 * 1024
+        ),
+        cost_estimate=pl.CostEstimate(
+            flops=40 * 10**9 * sum(shape[0] for shape in shapes) // 100,
+            bytes_accessed=0,
+            transcendentals=0,
+        ),
+        name="spread",
+    )(*shards, *late)
+    return [
+        result.reshape(16 * rows, columns) for result, (rows, columns) in zip(results, shapes)
+    ], results[len(shards) :]
+
+
+def spread_plainly(shards, late):
+    early = len(shards)
+    shards = shards + late
+    dp_count = lax.axis_size("dp")
+    flat = jnp.concatenate([shard.reshape(-1) for shard in shards])
+    flat = lax.all_gather(flat, "dp", axis=0)
+    wholes = []
+    first = 0
+    for shard in shards:
+        rows = shard.shape[0]
+        units = shard.shape[1] * dp_count // D if shard.shape[1] * dp_count < FF else 1
+        block = flat[:, first : first + shard.size].reshape(dp_count, rows, units, -1)
+        first += shard.size
+        block = block.transpose(1, 2, 0, 3).reshape(rows, -1)
+        wholes.append(block)
+    whole = [lax.all_gather(block, "seq", axis=0, tiled=True) for block in wholes[:early]]
+    return whole, wholes[early:]
+
+
+def reduce_plan(shapes):
+    return ordered(chunks_of(shapes), ORDERS, (0.39, 0.39, 0.22))
 
 
 def stage_shapes(chunk):
@@ -373,35 +572,23 @@
     return (2,) * len(left) + (chunk[2], width)
 
 
-def reduce_kernel(plan, count, *refs):
+def reduce_kernel(plan, count, late, *refs):
     sources = refs[:count]
-    small_in = refs[count]
-    outs = refs[count + 1 : 2 * count + 1]
-    small_out = refs[2 * count + 1]
-    scratch = list(refs[2 * count + 2 :])
+    late_rows = refs[count : count + late]
+    small_in = refs[count + late]
+    refs = refs[count + late + 1 :]
+    outs = refs[:count]
+    late_outs = refs[count : count + late]
+    small_out = refs[count + late]
+    scratch = list(refs[count + late + 1 :])
     send_sem, recv_sem, own_sem, small_acc, small_recv = scratch[:5]
-    scratch = scratch[5:]
+    late_recv = scratch[5 : 5 + late]
+    scratch = scratch[5 + late :]
     own = scratch[: len(plan)]
     held = [scratch[len(plan) + 5 * i : len(plan) + 5 * i + 5] for i in range(len(plan))]
 
-    dp = lax.axis_index("dp")
-    seq = lax.axis_index("seq")
-
-    def bit_of(axis):
-        return dp if axis == COLUMN else (seq // axis) % 2
-
-    def partner(axis):
-        if axis == COLUMN:
-            return (1 - dp, seq)
-        return (dp, seq + axis * (1 - 2 * bit_of(axis)))
-
-    everyone = (CORE, ROW, LOW, HIGH, COLUMN)
-    barrier = pltpu.get_barrier_semaphore()
-    for axis in everyone:
-        pl.semaphore_signal(
-            barrier, inc=1, device_id=partner(axis), device_id_type=pl.DeviceIdType.MESH
-        )
-    pl.semaphore_wait(barrier, len(everyone))
+    bit_of, partner = position()
+    meet(partner)
 
     def remote(source, target, item, stage, axis):
         return pltpu.make_async_remote_copy(
@@ -448,7 +635,7 @@
 
     def small_copy(stage):
         source = small_in if stage == 0 else small_acc.at[stage - 1]
-        return remote(source, small_recv.at[stage], len(plan), stage, everyone[stage])
+        return remote(source, small_recv.at[stage], len(plan), stage, EVERYONE[stage])
 
     def core_add(item):
         def body(i, unused):
@@ -485,10 +672,21 @@
         else:
             body(0, 0)
 
+    def late_lanes(item, mine):
+        half = late_recv[item].shape[1]
+        bit = bit_of(COLUMN) if mine else 1 - bit_of(COLUMN)
+        return pl.ds(pl.multiple_of(bit * half, 128), half)
+
+    def late_copy(item):
+        block = late_rows[item].at[:, late_lanes(item, False)]
+        return remote(block, late_recv[item], len(plan) + 1 + item, 0, COLUMN)
+
     for item in range(len(plan)):
         core_copy(item).start()
         own_copy(item).start()
     small_copy(0).start()
+    for item in range(late):
+        late_copy(item).start()
     events = sorted(
         (item + LAGS[stage], stage, item) for item in range(len(plan)) for stage in range(5)
     )
@@ -511,22 +709,29 @@
                 small_copy(stage + 1).start()
             else:
                 small_out[...] = summed
+    for item in range(late):
+        late_copy(item).wait()
+        late_outs[item][...] = late_rows[item][:, late_lanes(item, True)].astype(
+            f32
+        ) + late_recv[item][...].astype(f32)
     for item in range(len(plan)):
         core_copy(item).wait_send()
         for stage in range(1, 5):
             stage_copy(item, stage).wait_send()
 
 
-def reduce_all(grads, small):
+def reduce_all(grads, late, small):
     shapes = [(grad.shape[0] // 16, grad.shape[1]) for grad in grads]
     plan = reduce_plan(shapes)
     scratch = [
-        pltpu.SemaphoreType.DMA((len(plan) + 1, 5)),
-        pltpu.SemaphoreType.DMA((len(plan) + 1, 5)),
+        pltpu.SemaphoreType.DMA((len(plan) + 1 + len(late), 5)),
+        pltpu.SemaphoreType.DMA((len(plan) + 1 + len(late), 5)),
         pltpu.SemaphoreType.DMA((len(plan),)),
         pltpu.VMEM((4, SMALL, D), f32),
         pltpu.VMEM((5, SMALL, D), f32),
     ]
+    late_shapes = [(rows.shape[0], rows.shape[1] // 2) for rows in late]
+    scratch += [pltpu.VMEM(shape, bf16) for shape in late_shapes]
     scratch += [pltpu.VMEM(buffer_shape(c, stage_shapes(c)[0]), bf16) for c in plan]
     for chunk in plan:
         shapes_held = stage_shapes(chunk)
@@ -537,26 +742,282 @@
     space = pl.BlockSpec(memory_space=pl.ANY)
     near = pl.BlockSpec(memory_space=pltpu.VMEM)
     results = pl.pallas_call(
-        functools.partial(reduce_kernel, plan, len(grads)),
-        in_specs=[space] * len(grads) + [near],
-        out_specs=[near] * (len(grads) + 1),
+        functools.partial(reduce_kernel, plan, len(grads), len(late)),
+        in_specs=[space] * len(grads) + [near] * (len(late) + 1),
+        out_specs=[near] * (len(grads) + len(late) + 1),
         out_shape=[jax.ShapeDtypeStruct((rows, columns // 2), f32) for rows, columns in shapes]
+        + [jax.ShapeDtypeStruct(shape, f32) for shape in late_shapes]
         + [jax.ShapeDtypeStruct((SMALL, D), f32)],
         scratch_shapes=scratch,
         compiler_params=pltpu.CompilerParams(
             collective_id=1, has_side_effects=True, vmem_limit_bytes=60 * 1024 * 1024
         ),
         name="reduce_all",
-    )(*operands, small)
-    return results[:-1], results[-1]
-
-
-def reduce_plainly(grads):
+    )(*operands, *late, small)
+    return results[: len(grads)], results[len(grads) : -1], results[-1]
+
+
+MERGE = ((CORE, ROW, LOW, HIGH), (CORE, LOW, HIGH, ROW))
+SHARE = ((HIGH, LOW, ROW), (ROW, HIGH, LOW))
+SLOT_AXES = (HIGH, LOW, ROW, CORE)
+HALF = D // 2
+HALF_HEADS = HEADS // 2
+HALF_STATS = STATS // 2
+
+
+def spread_heads(weights):
+    head_at = lax.broadcasted_iota(jnp.int32, (HALF_STATS, HALF), 0)
+    column_at = lax.broadcasted_iota(jnp.int32, (HALF_STATS, HALF), 1)
+    chosen = (column_at // HD == head_at).astype(f32)
+    return lax.dot_general(
+        weights, chosen, (((0,), (0,)), ((), ())), precision=PRECISE, preferred_element_type=f32
+    )
+
+
+def merge_kernel(mix_ref, stat_ref, out_ref, out_stat_ref, send_sem, recv_sem, *held):
+    bit_of, partner = position()
+    meet(partner)
+
+    def came(item, stage):
+        return held[8 * item + 2 * stage], held[8 * item + 2 * stage + 1]
+
+    def left_of(item, stage):
+        return [axis for axis in SLOT_AXES if axis not in MERGE[item][:stage]]
+
+    def before(item, stage):
+        if stage == 0:
+            return mix_ref, stat_ref
+        return came(item, stage - 1)
+
+    def copies(item, stage):
+        axis = MERGE[item][stage]
+        at = (slice(None),) * left_of(item, stage).index(axis) + (1 - bit_of(axis),)
+        pairs = zip(before(item, stage), came(item, stage))
+        made = []
+        for kind, (source, target) in enumerate(pairs):
+            block = source.at[at]
+            if stage == 0:
+                rest = (slice(None),) * (4 - len(at))
+                lanes = (slice(None), pl.ds(item * HALF, HALF)) if kind == 0 else (item,)
+                block = source.at[at + rest + lanes]
+            made.append(
+                pltpu.make_async_remote_copy(
+                    src_ref=block,
+                    dst_ref=target,
+                    send_sem=send_sem.at[item, stage, kind],
+                    recv_sem=recv_sem.at[item, stage, kind],
+                    device_id=partner(axis),
+                    device_id_type=pl.DeviceIdType.MESH,
+                )
+            )
+        return made
+
+    def merge(item, stage):
+        axis = MERGE[item][stage]
+        place = left_of(item, stage).index(axis)
+        left = left_of(item, stage + 1)
+        mine = before(item, stage)
+        theirs = came(item, stage)
+
+        def body(i, unused):
+            index = tuple(i // (1 << (len(left) - 1 - n)) % 2 for n in range(len(left)))
+            at = index[:place] + (bit_of(axis),) + index[place:]
+            if stage == 0:
+                mix = mine[0][at + (slice(None), slice(item * HALF, (item + 1) * HALF))]
+                stat = mine[1][at + (item,)]
+            else:
+                mix = mine[0][at]
+                stat = mine[1][at]
+            other = theirs[0][index].astype(f32)
+            other_stat = theirs[1][index]
+            peak = jnp.maximum(stat, other_stat)
+            share = jnp.exp(stat - peak)
+            other_share = jnp.exp(other_stat - peak)
+            total = share + other_share
+            weight = spread_heads(share / total)
+            merged = other + weight * (mix.astype(f32) - other)
+            if stage == 3:
+                out_ref[:, item * HALF : (item + 1) * HALF] = merged
+                out_stat_ref[item] = peak + jnp.log(total)
+            else:
+                theirs[0][index] = merged.astype(bf16)
+                theirs[1][index] = peak + jnp.log(total)
+            return 0
+
+        if left:
+            lax.fori_loop(0, 1 << len(left), body, 0)
+        else:
+            body(0, 0)
+
+    for item in range(2):
+        for copy in copies(item, 0):
+            copy.start()
+    for stage in range(4):
+        for item in range(2):
+            for copy in copies(item, stage):
+                copy.wait_recv()
+            merge(item, stage)
+            if stage < 3:
+                for copy in copies(item, stage + 1):
+                    copy.start()
+    for stage in range(4):
+        for item in range(2):
+            for copy in copies(item, stage):
+                copy.wait_send()
+
+
+def merge_all(mix, stat):
+    rows = mix.shape[0] // 16
+    near = pl.BlockSpec(memory_space=pltpu.VMEM)
+    scratch = [pltpu.SemaphoreType.DMA((2, 4, 2)), pltpu.SemaphoreType.DMA((2, 4, 2))]
+    for item in range(2):
+        for stage in range(4):
+            lead = (2,) * (3 - stage)
+            scratch.append(pltpu.VMEM(lead + (rows, HALF), bf16))
+            scratch.append(pltpu.VMEM(lead + (HALF_STATS, rows), f32))
+    return pl.pallas_call(
+        merge_kernel,
+        in_specs=[near] * 2,
+        out_specs=[near] * 2,
+        out_shape=[
+            jax.ShapeDtypeStruct((rows, D), f32),
+            jax.ShapeDtypeStruct((2, HALF_STATS, rows), f32),
+        ],
+        scratch_shapes=scratch,
+        compiler_params=pltpu.CompilerParams(
+            collective_id=4, has_side_effects=True, vmem_limit_bytes=32 * 1024 * 1024
+        ),
+        name="merge_all",
+    )(mix.reshape(2, 2, 2, 2, rows, D), stat.reshape(2, 2, 2, 2, 2, HALF_STATS, rows))
+
+
+def share_kernel(orders, axes, kinds, *refs):
+    sources = refs[:kinds]
+    outs = refs[kinds : 2 * kinds]
+    send_sem, recv_sem, own_sem = refs[2 * kinds :]
+    bit_of, partner = position()
+    meet(partner)
+    depth = len(orders[0])
+
+    def slice_of(kind, item):
+        if kind == 1:
+            return (item,)
+        half = sources[0].shape[1] // 2
+        return (slice(None), pl.ds(item * half, half))
+
+    def part(item):
+        return [sources[kind].at[slice_of(kind, item)] for kind in range(kinds)]
+
+    def region(item, known, other=None):
+        at = []
+        for axis in axes:
+            if axis in known:
+                at.append(slice(None))
+            else:
+                at.append(1 - bit_of(axis) if axis == other else bit_of(axis))
+        return [outs[kind].at[tuple(at) + slice_of(kind, item)] for kind in range(kinds)]
+
+    def remote(sources, targets, item, place, axis):
+        return [
+            pltpu.make_async_remote_copy(
+                src_ref=source,
+                dst_ref=target,
+                send_sem=send_sem.at[item, place, kind],
+                recv_sem=recv_sem.at[item, place, kind],
+                device_id=partner(axis),
+                device_id_type=pl.DeviceIdType.MESH,
+            )
+            for kind, (source, target) in enumerate(zip(sources, targets))
+        ]
+
+    def stage_copies(item, stage):
+        held = region(item, orders[item][:stage])
+        return remote(part(item) if stage == 0 else held, held, item, stage, orders[item][stage])
+
+    def core_copies(item, stage):
+        if stage == 0:
+            return remote(part(item), region(item, ()), item, depth, CORE)
+        held = region(item, orders[item][: stage - 1], orders[item][stage - 1])
+        return remote(held, held, item, depth + stage, CORE)
+
+    def own_copies(item):
+        return [
+            pltpu.make_async_copy(source, target, own_sem.at[item, kind])
+            for kind, (source, target) in enumerate(zip(part(item), region(item, ())))
+        ]
+
+    for item in range(2):
+        for copy in stage_copies(item, 0) + core_copies(item, 0) + own_copies(item):
+            copy.start()
+    for stage in range(depth):
+        for item in range(2):
+            if stage == 0:
+                for copy in own_copies(item):
+                    copy.wait()
+            for copy in stage_copies(item, stage):
+                copy.wait_recv()
+            if stage + 1 < depth:
+                for copy in stage_copies(item, stage + 1):
+                    copy.start()
+            for copy in core_copies(item, stage + 1):
+                copy.start()
+    for item in range(2):
+        for stage in range(depth):
+            for copy in stage_copies(item, stage):
+                copy.wait_send()
+        for stage in range(depth + 1):
+            for copy in core_copies(item, stage):
+                copy.wait()
+
+
+def share_all(arrays, orders, collective_id):
+    kinds = len(arrays)
+    near = pl.BlockSpec(memory_space=pltpu.VMEM)
+    axes = tuple(axis for axis in SLOT_AXES if axis == CORE or axis in orders[0])
+    sems = pltpu.SemaphoreType.DMA((2, 2 * len(orders[0]) + 1, 2))
+    lead = (2,) * len(axes)
+    outs = pl.pallas_call(
+        functools.partial(share_kernel, orders, axes, kinds),
+        in_specs=[near] * kinds,
+        out_specs=[near] * kinds,
+        out_shape=[jax.ShapeDtypeStruct(lead + array.shape, array.dtype) for array in arrays],
+        scratch_shapes=[sems, sems, pltpu.SemaphoreType.DMA((2, 2))],
+        compiler_params=pltpu.CompilerParams(
+            collective_id=collective_id, has_side_effects=True, vmem_limit_bytes=32 * 1024 * 1024
+        ),
+        name="share_all",
+    )(*arrays)
+    return [out.reshape((1 << len(axes),) + array.shape) for out, array in zip(outs, arrays)]
+
+
+def halves_of(stat):
+    pad = ((0, 0), (0, HALF_STATS - HALF_HEADS), (0, 0))
+    return jnp.pad(stat[:HEADS].reshape(2, HALF_HEADS, -1), pad)
+
+
+def heads_from(halves):
+    stat = halves[..., :HALF_HEADS, :].reshape(halves.shape[:-3] + (HEADS, -1))
+    return jnp.pad(stat, ((0, 0),) * (stat.ndim - 2) + ((0, STATS - HEADS), (0, 0)))
+
+
+def merge_plainly(came_mix, came_stat, rows):
+    came_stat = came_stat.reshape(-1, rows, STATS)
+    peak = jnp.max(came_stat, axis=0)
+    shares = jnp.exp(came_stat - peak)
+    total = jnp.sum(shares, axis=0)
+    shares = (shares / total)[:, :, :HEADS]
+    came_mix = came_mix.astype(f32).reshape(-1, rows, HEADS, HD)
+    mix = jnp.sum(came_mix * shares[..., None], axis=0).reshape(rows, D)
+    return mix, (peak + jnp.log(total)).T
+
+
+def reduce_plainly(grads, late):
     dp_count = lax.axis_size("dp")
     split = []
-    for grad in grads:
-        rows = lax.psum_scatter(grad, "seq", scatter_dimension=0, tiled=True)
-        units = 3 if rows.shape[1] == 3 * D else 1
+    early = len(grads)
+    grads = [lax.psum_scatter(grad, "seq", scatter_dimension=0, tiled=True) for grad in grads]
+    for rows in grads + late:
+        units = rows.shape[1] // D if rows.shape[1] < FF else 1
         rows = rows.reshape(rows.shape[0], units, dp_count, -1)
         split.append(rows.transpose(2, 0, 1, 3))
     flat = jnp.concatenate([rows.reshape(dp_count, -1) for rows in split], axis=1)
@@ -567,7 +1028,7 @@
         size = rows.size // dp_count
         sums.append(flat[first : first + size].reshape(rows.shape[1], -1))
         first += size
-    return sums
+    return sums[:early], sums[early:]
 
 
 def per_head_dot(left_side, right_side):
@@ -607,42 +1068,27 @@
     part = D // seq_count
     wide = D // dp_count
 
-    masters = (enc_qkv, self_qkv, self_out, cross_qkv, enc_out, enc_up, enc_down)
-    masters = masters + (cross_out, dec_up, dec_down)
-
-    def pieces_of(master):
-        if master.ndim == 3:
-            return [master[c] for c in range(3)]
-        if master.shape[1] > wide:
-            return [master[:, c * wide : (c + 1) * wide] for c in range(master.shape[1] // wide)]
-        return [master[c * part : (c + 1) * part] for c in range(master.shape[0] // part)]
-
-    pieces = [piece.astype(bf16) for master in masters for piece in pieces_of(master)]
-    packed = lax.all_gather(jnp.concatenate(pieces, axis=0), "dp", axis=0)
-    packed = packed.reshape(dp_count, len(pieces), part, wide)
-
-    def rows_of(first, count):
-        return packed[:, first : first + count].transpose(2, 1, 0, 3).reshape(part, count * D)
-
-    def rows_of_wide(first):
-        return packed[:, first : first + 4].transpose(2, 0, 1, 3).reshape(part, FF)
-
-    def rows_of_tall(first):
-        return packed[:, first : first + 4].transpose(1, 2, 0, 3).reshape(4 * part, D)
-
-    def whole(rows):
-        return lax.all_gather(rows, "seq", axis=0, tiled=True)
-
-    enc_qkv_w = whole(rows_of(0, 3))
-    self_qkv_w = whole(rows_of(3, 3))
-    self_out_w = whole(rows_of(6, 1))
-    cross_qkv_w = whole(rows_of(7, 3))
-    enc_out_w = whole(rows_of(10, 1))
-    enc_up_w = whole(rows_of_wide(11))
-    enc_down_w = whole(rows_of_tall(15))
-    cross_out_w = whole(rows_of(19, 1))
-    dec_up_w = whole(rows_of_wide(20))
-    dec_down_w = whole(rows_of_tall(24))
+    def flat(master):
+        shard = master.astype(bf16)
+        if shard.ndim == 3:
+            shard = shard.transpose(1, 0, 2).reshape(part, -1)
+        return shard
+
+    here = dp_count == 2 and seq_count == 16
+
+    def gathered(masters, late, rows, collective_id):
+        shards = [flat(master) for master in masters]
+        late = [flat(master) for master in late]
+        if here:
+            return spread(shards, late, rows, collective_id)
+        weights, late = spread_plainly(shards, late)
+        if rows is not None:
+            weights.append(lax.all_gather(rows, "seq", axis=0, tiled=True))
+        return weights, late
+
+    (self_qkv_w, enc_qkv_w, self_out_w, cross_q_w), unused = gathered(
+        (self_qkv, enc_qkv, self_out, cross_qkv[0]), (), None, 2
+    )
 
     enc_gains_w = enc_gains.astype(bf16).astype(f32)
     dec_gains_w = dec_gains.astype(bf16).astype(f32)
@@ -694,18 +1140,31 @@
 
     dec_normed_one = norm_apply(dec_tokens, dec_gains_w[0]).astype(bf16)
     self_proj = matmul(dec_normed_one, self_qkv_w).astype(bf16)
-    self_near = lax.all_gather(
-        self_proj[:, D:], "seq", axis=0, tiled=True, axis_index_groups=groups
-    )
+    if here:
+        (self_near,) = share_all((self_proj[:, D:],), ((LOW, ROW), (ROW, LOW)), 6)
+        self_near = self_near.reshape(TGT, 2 * D)
+    else:
+        self_near = lax.all_gather(
+            self_proj[:, D:], "seq", axis=0, tiled=True, axis_index_groups=groups
+        )
     self_args = (self_proj, 0, self_near, 0, 1, my_place, self_marks, self_spans, None)
     self_mix_b, self_stat = attend(*self_args, dec_rows, True)
     dec_hidden = dec_tokens + matmul(self_mix_b, self_out_w)
     dec_normed_two = norm_apply(dec_hidden, dec_gains_w[1]).astype(bf16)
-    cross_queries = matmul(dec_normed_two, cross_qkv_w[:, :D]).astype(bf16)
-    all_queries = lax.all_gather(cross_queries, "seq", axis=0, tiled=True)
+    cross_queries = matmul(dec_normed_two, cross_q_w).astype(bf16)
 
     normed_one = norm_apply(tokens, enc_gains_w[0]).astype(bf16)
     enc_proj = matmul(normed_one, enc_qkv_w).astype(bf16)
+    cross_queries, enc_proj = lax.optimization_barrier((cross_queries, enc_proj))
+    (enc_out_w, cross_kv_w, enc_up_w, enc_down_w, cross_out_w, all_queries), late_rows = gathered(
+        (enc_out, cross_qkv[1:], enc_up, enc_down, cross_out),
+        (dec_up, dec_down),
+        cross_queries,
+        3,
+    )
+    dec_up_w, dec_down_w = [
+        lax.all_gather(rows, "seq", axis=0, tiled=True) for rows in late_rows
+    ]
     forward = [(i, i + 1) for i in range(seq_count - 1)]
     backward = [(i + 1, i) for i in range(seq_count - 1)]
     own_kv = enc_proj[:, D:]
@@ -724,7 +1183,7 @@
     enc_inner = matmul(normed_two, enc_up_w)
     enc_active = jax.nn.gelu(enc_inner).astype(bf16)
     encoded_b = (enc_hidden + matmul(enc_active, enc_down_w)).astype(bf16)
-    cross_kv = matmul(encoded_b, cross_qkv_w[:, D:]).astype(bf16)
+    cross_kv = matmul(encoded_b, cross_kv_w).astype(bf16)
 
     key_owner = row_ids // PASS_N
     cross_rows = 256
@@ -741,18 +1200,14 @@
     slot_query = jnp.arange(dec_total, dtype=jnp.int32) // TGT
     cross_args = (all_queries, 0, cross_kv, 0, 1, slot_query, key_owner, cross_spans, None)
     part_mix, part_stat = attend(*cross_args, cross_rows, False)
-    came_mix = lax.all_to_all(part_mix, "seq", 0, 0, tiled=True).reshape(seq_count, dec_rows, D)
-    came_stat = lax.all_to_all(part_stat.T, "seq", 0, 0, tiled=True).reshape(
-        seq_count, dec_rows, STATS
-    )
-    peak = jnp.max(came_stat, axis=0)
-    shares = jnp.exp(came_stat - peak)
-    total = jnp.sum(shares, axis=0)
-    cross_stat = peak + jnp.log(total)
-    shares = (shares / total)[:, :, :HEADS]
-    cross_mix = jnp.sum(
-        came_mix.astype(f32).reshape(seq_count, dec_rows, HEADS, HD) * shares[..., None], axis=0
-    ).reshape(dec_rows, D)
+    if here:
+        stat_slots = halves_of(part_stat).reshape(2, HALF_STATS, seq_count, dec_rows)
+        cross_mix, cross_stat = merge_all(part_mix, stat_slots.transpose(2, 0, 1, 3))
+        cross_stat = heads_from(cross_stat)
+    else:
+        came_mix = lax.all_to_all(part_mix, "seq", 0, 0, tiled=True)
+        came_stat = lax.all_to_all(part_stat.T, "seq", 0, 0, tiled=True)
+        cross_mix, cross_stat = merge_plainly(came_mix, came_stat, dec_rows)
     cross_mix_b = cross_mix.astype(bf16)
     dec_hidden_two = dec_hidden + matmul(cross_mix_b, cross_out_w)
     dec_normed_three = norm_apply(dec_hidden_two, dec_gains_w[2]).astype(bf16)
@@ -772,25 +1227,37 @@
     grad_hidden_two = grad_hidden_two + grad_final
     grad_cross_b = grad_hidden_two.astype(bf16)
     grad_cross_out = grad_of(cross_mix_b, grad_cross_b)
+    late = [
+        lax.psum_scatter(grad.astype(bf16), "seq", scatter_dimension=0, tiled=True)
+        for grad in (grad_dec_up, grad_dec_down)
+    ]
     grad_cross_mix = back_of(grad_cross_b, cross_out_w).astype(bf16)
     cross_dot = per_head_dot(grad_cross_mix, cross_mix)
-    all_grads = lax.all_gather(grad_cross_mix, "seq", axis=0, tiled=True)
-    all_stats = lax.all_gather(
-        jnp.concatenate([cross_stat, cross_dot.T], axis=1), "seq", axis=0, tiled=True
-    ).T
+    if here:
+        both = jnp.concatenate([halves_of(cross_stat), halves_of(cross_dot)], axis=1)
+        all_grads, all_stats = share_all((grad_cross_mix, both), SHARE, 5)
+        all_grads = all_grads.reshape(dec_total, D)
+        all_stats = all_stats.reshape(seq_count, 2, 2, HALF_STATS, dec_rows)
+        all_stats = heads_from(all_stats.transpose(2, 0, 1, 3, 4)).transpose(0, 2, 1, 3)
+        all_stats = all_stats.reshape(2 * STATS, dec_total)
+    else:
+        all_grads = lax.all_gather(grad_cross_mix, "seq", axis=0, tiled=True)
+        all_stats = lax.all_gather(
+            jnp.concatenate([cross_stat, cross_dot], axis=0).T, "seq", axis=0, tiled=True
+        ).T
     part_dq, cross_dk, cross_dv = attend_back(
         *cross_args, cross_rows, False, all_grads, all_stats[:STATS], all_stats[STATS:]
     )
-    grad_cross_q_b = lax.psum_scatter(part_dq, "seq", scatter_dimension=0, tiled=True)
+    came_dq = lax.all_to_all(part_dq, "seq", 0, 0, tiled=True).reshape(seq_count, dec_rows, D)
+    grad_cross_q_b = jnp.sum(came_dq.astype(f32), axis=0).astype(bf16)
     grad_cross_qw = grad_of(dec_normed_two, grad_cross_q_b)
     grad_hidden, grad_gain_two = norm_back(
-        dec_hidden, dec_gains_w[1], back_of(grad_cross_q_b, cross_qkv_w[:, :D])
+        dec_hidden, dec_gains_w[1], back_of(grad_cross_q_b, cross_q_w)
     )
     grad_hidden = grad_hidden + grad_hidden_two
     cross_kv_grad = jnp.concatenate([cross_dk, cross_dv], axis=1)
     grad_cross_kvw = grad_of(encoded_b, cross_kv_grad)
-    grad_encoded = back_of(cross_kv_grad, cross_qkv_w[:, D:])
-    grad_cross_qkv = jnp.concatenate([grad_cross_qw, grad_cross_kvw], axis=1)
+    grad_encoded = back_of(cross_kv_grad, cross_kv_w)
     grad_self_b = grad_hidden.astype(bf16)
     grad_self_out = grad_of(self_mix_b, grad_self_b)
     grad_self_mix = back_of(grad_self_b, self_out_w).astype(bf16)
@@ -798,13 +1265,15 @@
     self_dq, self_dk, self_dv = attend_back(
         *self_args, dec_rows, True, grad_self_mix, self_stat, self_dot
     )
-    self_dkv = lax.psum_scatter(
+    came_dkv = lax.all_to_all(
         jnp.concatenate([self_dk, self_dv], axis=1),
         "seq",
-        scatter_dimension=0,
+        0,
+        0,
         tiled=True,
         axis_index_groups=groups,
-    )
+    ).reshape(group_size, dec_rows, 2 * D)
+    self_dkv = jnp.sum(came_dkv.astype(f32), axis=0).astype(bf16)
     self_grad_b = jnp.concatenate([self_dq, self_dkv], axis=1)
     grad_self_qkv = grad_of(dec_normed_one, self_grad_b)
     grad_dec_in, grad_gain_one = norm_back(
@@ -849,10 +1318,9 @@
     grad_enc_in = grad_enc_in + grad_enc_hidden
     grad_enc_gains = jnp.stack([grad_enc_gain_one, grad_enc_gain_two])
     grads = (
-        grad_dec_down,
-        grad_dec_up,
         grad_cross_out,
-        grad_cross_qkv,
+        grad_cross_kvw,
+        grad_cross_qw,
         grad_self_out,
         grad_self_qkv,
         grad_enc_down,
@@ -862,37 +1330,37 @@
     )
     grads = [grad.astype(bf16) for grad in grads]
     gains_part = jnp.concatenate([grad_enc_gains, grad_dec_gains], axis=0)
-    if dp_count == 2 and seq_count == 16:
+    if here:
         table_row = jnp.pad(table_part.reshape(1, -1), ((0, 0), (0, D - BUCKETS * HEADS)))
         small = jnp.concatenate([gains_part, table_row], axis=0)
         small = jnp.pad(small, ((0, SMALL - small.shape[0]), (0, 0)))
-        sums, small = reduce_all(grads, small)
+        sums, late, small = reduce_all(grads, late, small)
         gains_total = small[:5]
         table_grad = small[5, : BUCKETS * HEADS].reshape(BUCKETS, HEADS)
     else:
         gains_total, table_grad = lax.psum((gains_part, table_part), ("dp", "seq"))
-        sums = reduce_plainly(grads)
+        sums, late = reduce_plainly(grads, late)
 
     def threes(rows):
-        return rows.reshape(part, 3, wide).transpose(1, 0, 2)
+        return rows.reshape(part, -1, wide).transpose(1, 0, 2)
 
     return (
         dec_output[None],
         grad_enc_in[None],
         grad_dec_in[None],
         gains_total[:2],
-        threes(sums[9]),
-        sums[8],
+        threes(sums[8]),
+        sums[7],
         table_grad,
-        sums[7],
         sums[6],
+        sums[5],
         gains_total[2:],
-        threes(sums[5]),
-        sums[4],
-        threes(sums[3]),
-        sums[2],
-        sums[1],
+        threes(sums[4]),
+        sums[3],
+        jnp.concatenate([sums[2][None], threes(sums[1])], axis=0),
         sums[0],
+        late[0],
+        late[1],
     )
 
 

time: 1060 us -> 779 us (0.73)
  waiting for transfers between devices: 487 us -> 14.5 us
  Pallas kernels: 284 us -> 486 us
  starting transfers between devices: 15.6 us -> 48.6 us
  blocking collectives: 32 us -> 0 us
    all_gather x14 -> x2, waiting for transfers between devices: 419 us -> 0.02 us  [per_device(): lax.all_gather(rows, 'seq', axis=0, tiled=True)]
    pallas_call x1 -> x6, Pallas kernels: 160 us -> 372 us  [the longest x2 148 us: spread(): pl.pallas_call(functools.partial(spread_kernel, plan, len(shards), len(la...]
    all_to_all x1 -> x2, waiting for transfers between devices: 53.5 us -> 6.9 us  [the longest x1 6.89 us: per_device(): lax.all_to_all(jnp.concatenate([self_dk, self_dv], axis=1), 'seq', 0, 0,...]
    all_to_all x1 -> x2, starting transfers between devices: 4.46 us -> 35.5 us  [the longest x1 27.1 us: per_device(): lax.all_to_all(jnp.concatenate([self_dk, self_dv], axis=1), 'seq', 0, 0,...]
    all_gather x1 -> x0, blocking collectives: 19.8 us -> none  [per_device(): lax.all_gather(jnp.concatenate([cross_stat, cross_dot.T], axis=1), 'seq',...]
    unnamed x260 -> x268, local copies, waits for them, and re-layouts: 25.7 us -> 39.5 us
    all_to_all x1 -> x0, blocking collectives: 12.3 us -> none  [per_device(): lax.all_to_all(part_stat.T, 'seq', 0, 0, tiled=True)]
    dot_general x11, matrix products: 35.1 us -> 23.3 us  [matmul(): return jnp.dot(left_side, right_side, preferred_element_type=f32)]
  transfers between devices with their start and end apart: 21 -> 10, of which waited for: 14 -> 2; matrix products, arithmetic and copies ran while one was open for 16% -> 19% of each run, Pallas kernels for 9% -> 26%
where the time goes in v2:
time: 779 us; the launch traced here: 772 us
  Pallas kernels  486 us (62%)
  matrix products  106 us (14%)
  local copies, waits for them, and re-layouts  68.9 us (9%)
  starting transfers between devices  48.6 us (6%)
  other arithmetic  32 us (4%)
  between operations  15.7 us (2%)
  waiting for transfers between devices  14.5 us (2%)
    pallas_call x2, Pallas kernels, spread(): pl.pallas_call(functools.partial(spread_kernel, plan, len(shards), len(la...  148 us
    pallas_call x1, Pallas kernels, reduce_all(): pl.pallas_call(functools.partial(reduce_kernel, plan, len(grads), len(lat...  111 us
    pallas_call x1, Pallas kernels, merge_all(): pl.pallas_call(merge_kernel, in_specs=[near] * 2, out_specs=[near] * 2, o...  65.8 us
    pallas_call x3, Pallas kernels, attend_back(): pl.pallas_call(functools.partial(attend_back_kernel, causal, bias is not...  65.7 us
    pallas_call x3, Pallas kernels, attend(): pl.pallas_call(functools.partial(attend_kernel, causal, bias is not None)...  48.5 us
    pallas_call x2, Pallas kernels, share_all(): pl.pallas_call(functools.partial(share_kernel, orders, axes, kinds), in_s...  47.5 us
    unnamed x268, local copies, waits for them, and re-layouts  39.5 us
    dot_general x11, matrix products, grad_of(): lax.dot_general(left_side, right_side, (((0,), (0,)), ((), ())), preferre...  37.1 us
  transfers between devices with their start and end apart: 10, of which 2 were waited for; matrix products, arithmetic and copies ran while one was open for 19% of the time, Pallas kernels for 26%

profile of v2, /device:TPU:0, one launch (start us, length us, event | category | flops | bytes accessed | tf_op | source)
XLA Modules:
  0.0 771.6 jit_solution(2685980958019709129)
XLA Ops:
  10.7 49.3 %spread.2 = (bf16[2,2,2,2,48,2304]{5,4,3,2,1,0:T(8,128)(2,1)S(1)}, bf16[2,2,2,2,48,2304]{5,4,3,2,1,0:T(8,128)(2,1)S(1)}, bf16[2,2,2,2,48,768]{5,4,3,2,1,0:T(8,128)(2,1)S(1)}, bf16[2,2,2,2,48,768]{5,4,3,2,1,0:T(8,128)(2,1)S(1)}) custom-call(bf16[48,1152]{1,0:T(8,128)(2,1)S(1)} %bitcast.290, bf16[48,1152]{1,0:T(8,128)(2,1)S(1)} %bitcast.291, ...), custom_call_target="tpu_custom_call" | custom-call | flops 76800000000 | tf_op jit(solution)/shard_map/spread/pallas_call | solution.py:505
  63.6 18.9 %share_all.2 = bf16[2,2,2,96,1536]{4,3,2,1,0:T(8,128)(2,1)S(1)} custom-call(bf16[96,1536]{1,0:T(8,128)(2,1)S(1)} %slice.139.refs_0_), custom_call_target="tpu_custom_call" | custom-call | tf_op jit(solution)/shard_map/share_all/pallas_call | solution.py:979
  87.6 6.2 shard_map.307
  100.6 98.4 %spread.3 = (bf16[2,2,2,2,48,768]{5,4,3,2,1,0:T(8,128)(2,1)S(1)}, bf16[2,2,2,2,48,1536]{5,4,3,2,1,0:T(8,128)(2,1)S(1)}, bf16[2,2,2,2,48,3072]{5,4,3,2,1,0:T(8,12...) custom-call(bf16[48,384]{1,0:T(8,128)(2,1)S(1)} %convert_element_typ, ...), custom_call_target="tpu_custom_call" | custom-call | flops 192000000000 | tf_op jit(solution)/shard_map/spread/pallas_call | solution.py:505
  209.7 4.6 collective-permute-start
  239.8 26.9 %shard_map.308 = (bf16[384,768]{1,0:T(8,128)(2,1)}, f32[16,384]{1,0:T(8,128)}) custom-call(s32[6]{0:T(128)} %reshape.774.spans_ref, bf16[384,2304]{1,0:T(8,128)(2,1)} %convolution_convert_fusion.6.q_ref, bf16[1152,1536]{1,0:T(8,128)(2,1)} %pad_maximum_fusion.k_ref.v_ref, bf16[1152,1536]{1,0:T(8,128)(2,1)} %pad_maximum_fusion.k_ref.v_ref, ...), custom_call_target="tpu_custom_call" | custom-call | flops 452984832 | bytes 7077888 | tf_op jit(solution)/shard_map/pallas_call | solution.py:168
  276.3 15.4 %shard_map.309 = (bf16[1536,768]{1,0:T(8,128)(2,1)}, f32[16,1536]{1,0:T(8,128)}) custom-call(s32[12]{0:T(128)} %reshape.768.spans_ref, bf16[1536,768]{1,0:T(8,128)(2,1)} %bitcast.276, bf16[384,1536]{1,0:T(8,128)(2,1)} %convolution_convert_fusion.9.k_ref.v_ref, bf16[384,1536]{1,0:T(8,128)(2,1)} %convolution_convert_fusion.9.k_ref.v_ref, ...), custom_call_target="tpu_custom_call" | custom-call | flops 603979776 | bytes 2359296 | tf_op jit(solution)/shard_map/pallas_call | solution.py:168
  294.5 65.8 %merge_all.1 = (f32[96,768]{1,0:T(8,128)S(1)}, f32[2,8,96]{2,1,0:T(8,128)S(1)}) custom-call(bf16[2,2,2,2,96,768]{5,4,3,2,1,0:T(8,128)(2,1)S(1)} %bitcast.286, f32[2,2,2,2,2,8,96]{6,5,4,3,2,1,0:T(8,128)S(1)} %bitcast.288), custom_call_target="tpu_custom_call" | custom-call | tf_op jit(solution)/shard_map/merge_all/pallas_call | solution.py:878
  375.0 4.7 multiply_reduce_fusion.3
  382.3 28.6 %share_all.3 = (bf16[2,2,2,2,96,768]{5,4,3,2,1,0:T(8,128)(2,1)S(1)}, f32[2,2,2,2,2,16,96]{6,5,4,3,2,1,0:T(8,128)S(1)}) custom-call(bf16[96,768]{1,0:T(8,128)(2,1)S(1)} %get-tuple-element.252.refs_0_, f32[2,16,96]{2,1,0:T(8,128)S(1)} %select_maximum_fusion.refs_1_), custom_call_target="tpu_custom_call" | custom-call | tf_op jit(solution)/shard_map/share_all/pallas_call | solution.py:979
  414.1 30.4 %shard_map.310 = (bf16[1536,768]{1,0:T(8,128)(2,1)}, bf16[384,768]{1,0:T(8,128)(2,1)}, bf16[384,768]{1,0:T(8,128)(2,1)}) custom-call(s32[12]{0:T(128)} %reshape.768.spans_ref, bf16[1536,768]{1,0:T(8,128)(2,1)} %bitcast.277, bf16[384,1536]{1,0:T(8,128)(2,1)} %convolution_convert_fusion.9.k_ref.v_ref, bf16[384,1536]{1,0:T(8,128)(2,1)} %convolution_convert_fusion.9.k_ref.v_ref, ...), custom_call_target="tpu_custom_call" | custom-call | flops 1509949440 | bytes 4718592 | tf_op jit(solution)/shard_map/pallas_call | solution.py:308
  444.5 8.4 %all-to-all-start = ((bf16[16,96,768]{2,1,0:T(8,128)(2,1)}), bf16[16,96,768]{2,1,0:T(8,128)(2,1)}, u32[]{:S(2)}, u32[]{:S(2)}) async-start(bf16[16,96,768]{2,1,0:T(8,128)(2,1)} %bitcast.321), calls=%async_computation | async-start | bytes 4718592 | tf_op jit(solution)/shard_map/all_to_all | solution.py:1251
  456.2 8.8 %fusion.10 = bf16[384,3072]{1,0:T(8,128)(2,1)S(1)} fusion(f32[384,3072]{1,0:T(8,128)} %copy-done.115, bf16[3072,768]{1,0:T(8,128)(2,1)} %bitcast.299, f32[384,768]{1,0:T(8,128)S(1)} %fusion.110), kind=kOutput, calls=%fused_computation.19 | convolution fusion | flops 1835827200 | bytes 12976128 | tf_op jit(solution)/shard_map/dot_general | solution.py:69
  473.1 28.4 %shard_map.311 = (bf16[384,768]{1,0:T(8,128)(2,1)}, bf16[1152,768]{1,0:T(8,128)(2,1)}, bf16[1152,768]{1,0:T(8,128)(2,1)}, f32[12,640,128]{2,1,0:T(8,128)}) custom-call(s32[6]{0:T(128)} %reshape.774.spans_ref, bf16[384,2304]{1,0:T(8,128)(2,1)} %convolution_convert_fusion.6.q_ref, bf16[1152,1536]{1,0:T(8,128)(2,1)} %pad_maximum_fusion.k_ref.v_ref, ...), custom_call_target="tpu_custom_call" | custom-call | flops 1132462080 | bytes 14155776 | tf_op jit(solution)/shard_map/pallas_call | solution.py:308
  506.6 5.8 collective-permute-start.3
  514.2 5.3 copy.111
  524.1 8.2 %fusion = f32[32,12]{1,0:T(8,128)} fusion(f32[12,81920]{1,0:T(8,128)} %bitcast.308, s32[81920]{0:T(1024)S(1)} %copy-done.43), kind=kOutput, calls=%fused_computation.1 | convolution fusion | flops 380108800 | bytes 4261376 | tf_op jit(solution)/shard_map/dot_general | solution.py:1300
  535.1 4.5 convolution_convert_fusion.3
  545.3 7.0 shard_map.312
  555.6 27.1 %all-to-all-start.1 = ((bf16[8,96,1536]{2,1,0:T(8,128)(2,1)}), bf16[8,96,1536]{2,1,0:T(8,128)(2,1)}, u32[]{:S(2)}, u32[]{:S(2)}) async-start(bf16[8,96,1536]{2,1,0:T(8,128)(2,1)} %bitcast.312), calls=%async_computation.1 | async-start | bytes 4718592 | tf_op jit(solution)/shard_map/all_to_all | solution.py:1268
  592.3 7.8 %convolution_convert_fusion.4 = bf16[3072,768]{1,0:T(8,128)(2,1)} fusion(f32[384,768]{1,0:T(8,128)S(1)} %copy-done.51, f32[384,3072]{1,0:T(8,128)} %copy-done.115), kind=kOutput, calls=%fused_computation.11 | convolution fusion | flops 1825210368 | bytes 10616832 | tf_op jit(solution)/shard_map/dot_general | solution.py:63
  614.6 6.9 all-to-all-done.1
  633.6 6.8 reduce-scatter.5.cloned.1.call-done.refs_10_
  640.5 111.0 %reduce_all.1 = (f32[48,384]{1,0:T(8,128)}, f32[48,768]{1,0:T(8,128)}, f32[48,384]{1,0:T(8,128)}, f32[48,384]{1,0:T(8,128)}, f32[48,1152]{1,0:T(8,128)}, /*index...) custom-call(bf16[2,2,2,2,48,768]{5,4,3,2,1,0:T(8,128)(2,1)} %bitcast, ...), custom_call_target="tpu_custom_call" | custom-call | tf_op jit(solution)/shard_map/reduce_all/pallas_call | solution.py:744
  (428 shorter events, 170.9 us)
Async XLA Ops:
  7.2 217.0 %copy-start = (f32[32,12]{0,1:T(8,128)S(1)}, f32[32,12]{0,1:T(8,128)}, u32[]{:S(2)}) copy-start(f32[32,12]{0,1:T(8,128)} %param.34) | copy-start | bytes 4612
  7.2 353.5 %all-gather.3.cloned.1.call-start = ((), (), s32[]{:S(2)}) async-start(), calls=%async_computation.4 | async-start | bytes 5013504 | tf_op jit(solution)/shard_map/all_gather | solution.py:1166
  10.5 51.2 %copy-start.68 = (f32[768]{0:T(1024)}, f32[768]{0:T(1024)S(1)}, u32[]{:S(2)}) copy-start(f32[768]{0:T(1024)S(1)} %get-tuple-element.224) | copy-start | bytes 9220
  10.5 89.0 %copy-start.70 = (f32[768]{0:T(1024)}, f32[768]{0:T(1024)S(1)}, u32[]{:S(2)}) copy-start(f32[768]{0:T(1024)S(1)} %get-tuple-element.223) | copy-start | bytes 9220
  10.7 49.3 %copy-start.107 = (f32[96]{0:T(128)}, f32[96]{0:T(128)S(1)}, u32[]{:S(2)}) copy-start(f32[96]{0:T(128)S(1)} %fusion.57) | copy-start | bytes 1156
  10.7 51.1 %copy-start.91 = (f32[96]{0:T(128)}, f32[96]{0:T(128)S(1)}, u32[]{:S(2)}) copy-start(f32[96]{0:T(128)S(1)} %fusion.97) | copy-start | bytes 1156
  61.7 32.1 %copy-start.7 = (bf16[2,2,2,2,48,768]{5,4,3,2,1,0:T(8,128)(2,1)}, bf16[2,2,2,2,48,768]{5,4,3,2,1,0:T(8,128)(2,1)S(1)}, u32[]{:S(2)}) copy-start(bf16[2,2,2,2,48,768]{5,4,3,2,1,0:T(8,128)(2,1)S(1)} %get-tuple-element.104) | copy-start | bytes 3538948
  61.7 37.8 %copy-start.5 = (bf16[2,2,2,2,48,768]{5,4,3,2,1,0:T(8,128)(2,1)}, bf16[2,2,2,2,48,768]{5,4,3,2,1,0:T(8,128)(2,1)S(1)}, u32[]{:S(2)}) copy-start(bf16[2,2,2,2,48,768]{5,4,3,2,1,0:T(8,128)(2,1)S(1)} %get-tuple-element.105) | copy-start | bytes 3538948
  206.2 159.2 %all-gather.5.cloned.1.call-start = ((), (), s32[]{:S(2)}) async-start(), calls=%async_computation.5 | async-start | bytes 5013504 | tf_op jit(solution)/shard_map/all_gather | solution.py:1166
  207.0 426.7 %reduce-scatter.3.cloned.1.call-start = ((), (), s32[]{:S(2)}) async-start(), calls=%async_computation.6 | async-start | bytes 5013504 | tf_op jit(solution)/shard_map/reduce_scatter | solution.py:1231
  208.4 27.9 %collective-permute-start.1 = (bf16[384,1536]{1,0:T(8,128)(2,1)S(1)}, bf16[384,1536]{1,0:T(8,128)(2,1)}, u32[]{:S(2)}, u32[]{:S(2)}) collective-permute-start(bf16[384,1536]{1,0:T(8,128)(2,1)S(1)} %slice.121), channel_id=1, source_target_pairs={{1,0},{2,1},{3,2},{4,3},{5,4},{6,5},{7,6},{8,7},{9,8},{10,9},{11,1... | collective-permute-start | bytes 3538952 | tf_op jit(solution)/shard_map/ppermute | solution.py:1175
  209.7 26.6 %collective-permute-start = (bf16[384,1536]{1,0:T(8,128)(2,1)S(1)}, bf16[384,1536]{1,0:T(8,128)(2,1)}, u32[]{:S(2)}, u32[]{:S(2)}) collective-permute-start(bf16[384,1536]{1,0:T(8,128)(2,1)S(1)} %slice.121), channel_id=1, source_target_pairs={{0,1},{1,2},{2,3},{3,4},{4,5},{5,6},{6,7},{7,8},{8,9},{9,10},{10,1... | collective-permute-start | bytes 3538952 | tf_op jit(solution)/shard_map/ppermute | solution.py:1173
  234.0 131.4 %copy-start.103 = (f32[96]{0:T(128)}, f32[96]{0:T(128)S(1)}, u32[]{:S(2)}) copy-start(f32[96]{0:T(128)S(1)} %compare_convert_fusion) | copy-start | bytes 1156
  236.3 32.4 %slice-start = ((s8[4718592]{0:T(1024)(128)(4,1)}), s8[4194304]{0:T(1024)(128)(4,1)S(1)}, s32[]{:S(2)}) async-start(s8[4718592]{0:T(1024)(128)(4,1)} %bitcast.293), calls=%async_computation.8 | async-start | bytes 8388608
  239.8 28.9 %slice-start.1 = ((s8[4718592]{0:T(1024)(128)(4,1)}), s8[524288]{0:T(1024)(128)(4,1)S(1)}, s32[]{:S(2)}) async-start(s8[4718592]{0:T(1024)(128)(4,1)} %bitcast.293), calls=%async_computation.9 | async-start | bytes 1048576
  239.8 28.9 %copy-start.84 = (f32[768]{0:T(1024)S(1)}, f32[768]{0:T(1024)}, u32[]{:S(2)}) copy-start(f32[768]{0:T(1024)} %get-tuple-element.227) | copy-start | bytes 9220
  294.5 65.8 %copy-start.20 = (f32[96,768]{1,0:T(8,128)S(1)}, f32[96,768]{1,0:T(8,128)}, u32[]{:S(2)}) copy-start(f32[96,768]{1,0:T(8,128)} %copy-done.19) | copy-start | bytes 884740
  444.5 95.1 %all-to-all-start = ((bf16[16,96,768]{2,1,0:T(8,128)(2,1)}), bf16[16,96,768]{2,1,0:T(8,128)(2,1)}, u32[]{:S(2)}, u32[]{:S(2)}) async-start(bf16[16,96,768]{2,1,0:T(8,128)(2,1)} %bitcast.321), calls=%async_computation | async-start | bytes 4718592 | tf_op jit(solution)/shard_map/all_to_all | solution.py:1251
  452.8 187.6 %reduce-scatter.5.cloned.1.call-start = ((), (), s32[]{:S(2)}) async-start(), calls=%async_computation.7 | async-start | bytes 5013504 | tf_op jit(solution)/shard_map/reduce_scatter | solution.py:1231
  506.6 93.5 %collective-permute-start.3 = (bf16[384,1536]{1,0:T(8,128)(2,1)}, bf16[384,1536]{1,0:T(8,128)(2,1)}, u32[]{:S(2)}, u32[]{:S(2)}) collective-permute-start(bf16[384,1536]{1,0:T(8,128)(2,1)} %get-tuple-element.237), channel_id=1, source_target_pairs={{0,1},{1,2},{2,3},{3,4},{4,5},{5,6},{6,7},{7,8},{8,9},{9,10},{10,1... | collective-permute-start | bytes 3538952 | tf_op jit(solution)/shard_map/ppermute | solution.py:1309
  512.4 87.7 %collective-permute-start.2 = (bf16[384,1536]{1,0:T(8,128)(2,1)}, bf16[384,1536]{1,0:T(8,128)(2,1)}, u32[]{:S(2)}, u32[]{:S(2)}) collective-permute-start(bf16[384,1536]{1,0:T(8,128)(2,1)} %get-tuple-element.236), channel_id=1, source_target_pairs={{1,0},{2,1},{3,2},{4,3},{5,4},{6,5},{7,6},{8,7},{9,8},{10,9},{11,1... | collective-permute-start | bytes 3538952 | tf_op jit(solution)/shard_map/ppermute | solution.py:1308
  555.6 65.9 %all-to-all-start.1 = ((bf16[8,96,1536]{2,1,0:T(8,128)(2,1)}), bf16[8,96,1536]{2,1,0:T(8,128)(2,1)}, u32[]{:S(2)}, u32[]{:S(2)}) async-start(bf16[8,96,1536]{2,1,0:T(8,128)(2,1)} %bitcast.312), calls=%async_computation.1 | async-start | bytes 4718592 | tf_op jit(solution)/shard_map/all_to_all | solution.py:1268
  640.5 114.5 %copy-start.108 = (f32[96]{0:T(128)S(1)}, f32[96]{0:T(128)}, u32[]{:S(2)}) copy-start(f32[96]{0:T(128)} %copy-done.107) | copy-start | bytes 1156
  640.5 114.5 %copy-start.109 = (f32[96]{0:T(128)S(1)}, f32[96]{0:T(128)}, u32[]{:S(2)}) copy-start(f32[96]{0:T(128)} %get-tuple-element.221) | copy-start | bytes 1156
  (112 other events, 497.1 us)
Sparse Core Ops, SparseCore 0:
  206.3 64.4 all-gather.2
  273.1 53.9 all-gather.4
  374.4 78.1 reduce-scatter.2
  523.3 117.1 reduce-scatter.4

commit v3 on v2

--- a/solution.py
+++ b/solution.py
@@ -18,6 +18,7 @@
 STATS = 16
 PAIR = 2 * HD
 PAIRS = HEADS // 2
+HALF = D // 2
 
 EPSILON = 1e-06
 PRECISE = lax.Precision.HIGHEST
@@ -25,6 +26,9 @@
 NEGATIVE = -1e30
 FAR = 1 << 20
 KEYS = 128
+GROUP = 12
+GROUP_BACK = 12
+CROSS_ROWS = 384
 VMEM = 56 * 1024 * 1024
 bf16 = jnp.bfloat16
 f32 = jnp.float32
@@ -99,6 +103,7 @@
     peak_ref[...] = jnp.full(peak_ref.shape, NEGATIVE, f32)
     total_ref[...] = jnp.zeros_like(total_ref)
     row_mark = row_ref[0]
+    scale = jnp.asarray(0.125, bf16)
 
     def body(key_block, unused):
         keys = pl.ds(pl.multiple_of(key_block * KEYS, KEYS), KEYS)
@@ -106,30 +111,33 @@
         allowed = (key_mark <= row_mark) if causal else (key_mark == row_mark)
         if with_bias:
             biased = pl.ds(pl.multiple_of(bias_slot(key_block, block) * KEYS, KEYS), KEYS)
-        for pair in range(PAIRS):
-            lanes = slice(pair * PAIR, (pair + 1) * PAIR)
-            k_pair = k_ref[keys, lanes]
-            v_pair = v_ref[keys, lanes]
-            q_pair = q_ref[:, lanes]
-            for half in range(2):
-                head = pair * 2 + half
-                scores = dot_nt(k_pair, head_mask(q_pair, half)) * 0.125
-                if with_bias:
-                    scores = scores + bias_ref[head, biased, :]
-                scores = jnp.where(allowed, scores, NEGATIVE)
-                old = peak_ref[head : head + 1, :]
-                peak = jnp.maximum(old, jnp.max(scores, axis=0, keepdims=True))
-                rescale = jnp.exp(old - peak)
-                weights = jnp.exp(scores - peak)
-                peak_ref[head : head + 1, :] = peak
-                total_ref[head : head + 1, :] = total_ref[
-                    head : head + 1, :
-                ] * rescale + jnp.sum(weights, axis=0, keepdims=True)
-                mixed = dot_tn(v_pair, weights.astype(bf16))
+        for first in range(0, HEADS, GROUP):
+            heads = range(first, first + GROUP)
+            scores = []
+            for head in heads:
+                lanes = slice(head // 2 * PAIR, (head // 2 + 1) * PAIR)
+                query = head_mask(q_ref[:, lanes] * scale, head % 2)
+                scores.append(dot_nt(k_ref[keys, lanes], query))
+            if with_bias:
+                scores = [s + bias_ref[h, biased, :] for s, h in zip(scores, heads)]
+            scores = [jnp.where(allowed, s, NEGATIVE) for s in scores]
+            olds = [peak_ref[h : h + 1, :] for h in heads]
+            peaks = [
+                jnp.maximum(old, jnp.max(s, axis=0, keepdims=True)) for s, old in zip(scores, olds)
+            ]
+            rescales = [jnp.exp(old - peak) for old, peak in zip(olds, peaks)]
+            weights = [jnp.exp(s - peak) for s, peak in zip(scores, peaks)]
+            sums = [jnp.sum(w, axis=0, keepdims=True) for w in weights]
+            mixed = []
+            for head, weight in zip(heads, weights):
+                lanes = slice(head // 2 * PAIR, (head // 2 + 1) * PAIR)
+                mixed.append(dot_tn(v_ref[keys, lanes], weight.astype(bf16)))
+            for n, head in enumerate(heads):
+                total_ref[head : head + 1, :] = total_ref[head : head + 1, :] * rescales[n] + sums[n]
+                peak_ref[head : head + 1, :] = peaks[n]
                 rows = slice(head * HD, (head + 1) * HD)
-                acc_ref[rows, :] = (
-                    acc_ref[rows, :] * rescale + mixed[half * HD : (half + 1) * HD, :]
-                )
+                half = slice(head % 2 * HD, (head % 2 + 1) * HD)
+                acc_ref[rows, :] = acc_ref[rows, :] * rescales[n] + mixed[n][half, :]
         return 0
 
     lax.fori_loop(spans_ref[2 * block], spans_ref[2 * block + 1], body, 0)
@@ -207,9 +215,9 @@
     *rest,
 ):
     if with_bias:
-        bias_ref, dq_ref, dk_ref, dv_ref, dbias_ref, dqt_ref, dk_acc, dv_acc = rest
+        bias_ref, dq_ref, dkv_ref, dbias_ref, dqt_ref, dk_acc, dv_acc = rest
     else:
-        dq_ref, dk_ref, dv_ref, dqt_ref, dk_acc, dv_acc = rest
+        dq_ref, dkv_ref, dqt_ref, dk_acc, dv_acc = rest
     block = pl.program_id(0)
 
     @pl.when(block == 0)
@@ -221,6 +229,7 @@
 
     dqt_ref[...] = jnp.zeros_like(dqt_ref)
     row_mark = row_ref[0]
+    scale = jnp.asarray(0.125, bf16)
 
     def body(key_block, unused):
         keys = pl.ds(pl.multiple_of(key_block * KEYS, KEYS), KEYS)
@@ -228,37 +237,38 @@
         allowed = (key_mark <= row_mark) if causal else (key_mark == row_mark)
         if with_bias:
             biased = pl.ds(pl.multiple_of(bias_slot(key_block, block) * KEYS, KEYS), KEYS)
-        for pair in range(PAIRS):
-            lanes = slice(pair * PAIR, (pair + 1) * PAIR)
-            k_pair = k_ref[keys, lanes]
-            v_pair = v_ref[keys, lanes]
-            q_pair = q_ref[:, lanes]
-            do_pair = do_ref[:, lanes]
-            dk_add = None
-            dv_add = None
-            for half in range(2):
-                head = pair * 2 + half
-                q_half = head_mask(q_pair, half)
-                do_half = head_mask(do_pair, half)
-                scores = dot_nt(k_pair, q_half) * 0.125
+        for first in range(0, HEADS, GROUP_BACK):
+            heads = range(first, first + GROUP_BACK)
+            slices = [slice(h // 2 * PAIR, (h // 2 + 1) * PAIR) for h in heads]
+            queries = [head_mask(q_ref[:, lanes] * scale, h % 2) for lanes, h in zip(slices, heads)]
+            grads = [head_mask(do_ref[:, lanes], h % 2) for lanes, h in zip(slices, heads)]
+            scores = [dot_nt(k_ref[keys, lanes], q) for lanes, q in zip(slices, queries)]
+            passed = [dot_nt(v_ref[keys, lanes], g) for lanes, g in zip(slices, grads)]
+            if with_bias:
+                scores = [s + bias_ref[h, biased, :] for s, h in zip(scores, heads)]
+            scores = [jnp.where(allowed, s, NEGATIVE) for s in scores]
+            weights = [jnp.exp(s - stat_ref[h : h + 1, :]) for s, h in zip(scores, heads)]
+            grad_scores = [
+                w * (p - dot_ref[h : h + 1, :]) for w, p, h in zip(weights, passed, heads)
+            ]
+            rounded = [g.astype(bf16) for g in grad_scores]
+            values = [
+                jnp.dot(w.astype(bf16), g, preferred_element_type=f32)
+                for w, g in zip(weights, grads)
+            ]
+            key_parts = [
+                jnp.dot(r, q, preferred_element_type=f32) for r, q in zip(rounded, queries)
+            ]
+            mixed = [dot_tn(k_ref[keys, lanes], r) for lanes, r in zip(slices, rounded)]
+            for n, head in enumerate(heads):
                 if with_bias:
-                    scores = scores + bias_ref[head, biased, :]
-                scores = jnp.where(allowed, scores, NEGATIVE)
-                weights = jnp.exp(scores - stat_ref[head : head + 1, :])
-                grad_weights = dot_nt(v_pair, do_half)
-                grad_scores = weights * (grad_weights - dot_ref[head : head + 1, :])
-                if with_bias:
-                    dbias_ref[head, biased, :] += grad_scores
-                rounded = grad_scores.astype(bf16)
-                dv_part = jnp.dot(weights.astype(bf16), do_half, preferred_element_type=f32)
-                dk_part = jnp.dot(rounded, q_half, preferred_element_type=f32)
-                dv_add = dv_part if dv_add is None else dv_add + dv_part
-                dk_add = dk_part if dk_add is None else dk_add + dk_part
-                mixed = dot_tn(k_pair, rounded)
+                    dbias_ref[head, biased, :] += grad_scores[n]
                 rows = slice(head * HD, (head + 1) * HD)
-                dqt_ref[rows, :] += mixed[half * HD : (half + 1) * HD, :]
-            dk_acc[keys, lanes] += dk_add
-            dv_acc[keys, lanes] += dv_add
+                half = slice(head % 2 * HD, (head % 2 + 1) * HD)
+                dqt_ref[rows, :] += mixed[n][half, :]
+                if head % 2:
+                    dk_acc[keys, slices[n]] += key_parts[n - 1] + key_parts[n]
+                    dv_acc[keys, slices[n]] += values[n - 1] + values[n]
         return 0
 
     lax.fori_loop(spans_ref[2 * block], spans_ref[2 * block + 1], body, 0)
@@ -268,8 +278,8 @@
 
     @pl.when(block == pl.num_programs(0) - 1)
     def finish():
-        dk_ref[...] = (dk_acc[...] * 0.125).astype(dk_ref.dtype)
-        dv_ref[...] = dv_acc[...].astype(dv_ref.dtype)
+        dkv_ref[:, :D] = dk_acc[...].astype(dkv_ref.dtype)
+        dkv_ref[:, D:] = dv_acc[...].astype(dkv_ref.dtype)
 
 
 def attend_back(
@@ -292,13 +302,11 @@
     operands += [do, stat, dot]
     out_specs = [
         pl.BlockSpec((rows, D), lambda i, s: (i, 0)),
-        pl.BlockSpec((span, D), lambda i, s: (0, 0)),
-        pl.BlockSpec((span, D), lambda i, s: (0, 0)),
+        pl.BlockSpec((span, 2 * D), lambda i, s: (0, 0)),
     ]
     out_shape = [
         jax.ShapeDtypeStruct((count, D), bf16),
-        jax.ShapeDtypeStruct((span, D), bf16),
-        jax.ShapeDtypeStruct((span, D), bf16),
+        jax.ShapeDtypeStruct((span, 2 * D), bf16),
     ]
     if bias is not None:
         specs.append(pl.BlockSpec(bias.shape, lambda i, s: (0, 0, 0)))
@@ -328,7 +336,8 @@
 
 CORE, ROW, LOW, HIGH, COLUMN = 1, 2, 4, 8, 16
 ORDERS = ((COLUMN, ROW, LOW, HIGH), (ROW, COLUMN, LOW, HIGH), (LOW, HIGH, ROW, COLUMN))
-LAGS = (0, 4, 9, 13, 16)
+LAGS = (-1.5, 0, 4, 9, 13, 16)
+RING = 3
 SMALL = 16
 EVERYONE = (CORE, ROW, LOW, HIGH, COLUMN)
 
@@ -352,6 +361,9 @@
         elif columns in (2 * D, 3 * D):
             for first in range(0, columns, D):
                 chunks.append((source, 0, rows, first, D // 2))
+        elif columns > 3 * D:
+            for first in range(0, rows, 16):
+                chunks.append((source, first, 16, 0, columns // 2))
         else:
             chunks.append((source, 0, rows, 0, columns // 2))
     return chunks
@@ -383,24 +395,44 @@
     return bit_of, partner
 
 
-def meet(partner):
+def meet(partner, neighbours=False):
     barrier = pltpu.get_barrier_semaphore()
     for axis in EVERYONE:
         pl.semaphore_signal(
             barrier, inc=1, device_id=partner(axis), device_id_type=pl.DeviceIdType.MESH
         )
-    pl.semaphore_wait(barrier, len(EVERYONE))
-
-
-def spread_kernel(plan, count, late, *refs):
+    if neighbours:
+        dp = lax.axis_index("dp")
+        seq = lax.axis_index("seq")
+        last = lax.axis_size("seq") - 1
+        for step, there in ((-1, seq > 0), (1, seq < last)):
+
+            @pl.when(there)
+            def greet(step=step):
+                pl.semaphore_signal(
+                    barrier,
+                    inc=1,
+                    device_id=(dp, seq + step),
+                    device_id_type=pl.DeviceIdType.MESH,
+                )
+
+        peers = len(EVERYONE) + (seq > 0).astype(jnp.int32) + (seq < last).astype(jnp.int32)
+        pl.semaphore_wait(barrier, peers)
+    else:
+        pl.semaphore_wait(barrier, len(EVERYONE))
+
+
+def spread_kernel(plan, count, late, near, *refs):
     shards = refs[:count]
     late_shards = refs[count : count + late]
-    refs = refs[count + late :]
+    near_own = refs[count + late] if near else None
+    refs = refs[count + late + near :]
     wholes = refs[:count]
     late_rows = refs[count : count + late]
-    send_sem, recv_sem, own_sem = refs[count + late :]
+    near_all = refs[count + late] if near else None
+    send_sem, recv_sem, own_sem = refs[count + late + near :]
     bit_of, partner = position()
-    meet(partner)
+    meet(partner, bool(near))
 
     def region(item, known, other=None):
         source, row, rows, column, half, order = plan[item]
@@ -408,8 +440,9 @@
         def bit(axis):
             return 1 - bit_of(axis) if axis == other else bit_of(axis)
 
-        at = [slice(None) if axis in known else bit(axis) for axis in (HIGH, LOW, ROW, CORE)]
-        if COLUMN in known or len(order) == 3:
+        axes = (LOW, ROW, CORE) if len(order) == 2 else SLOT_AXES
+        at = [slice(None) if axis in known else bit(axis) for axis in axes]
+        if COLUMN in known or len(order) < 4:
             lanes = pl.ds(column, 2 * half)
         else:
             lanes = pl.ds(pl.multiple_of(column + bit(COLUMN) * half, 128), half)
@@ -417,7 +450,7 @@
 
     def own_part(item):
         source, row, rows, column, half, order = plan[item]
-        if len(order) == 3:
+        if len(order) < 4:
             return shards[source].at[pl.ds(row, rows), pl.ds(column, 2 * half)]
         return shards[source].at[pl.ds(row, rows), pl.ds(column // 2, half)]
 
@@ -458,6 +491,32 @@
 
     def late_copy(item):
         return remote(late_shards[item], late_part(item), len(plan) + item, 0, COLUMN)
+
+    dp = lax.axis_index("dp")
+    seq = lax.axis_index("seq")
+    marks = len(plan) + late
+
+    def near_copy(step):
+        return pltpu.make_async_remote_copy(
+            src_ref=near_own,
+            dst_ref=near_all.at[1 - step],
+            send_sem=send_sem.at[marks, 1 + step],
+            recv_sem=recv_sem.at[marks, 1 + step],
+            device_id=(dp, seq + step),
+            device_id_type=pl.DeviceIdType.MESH,
+        )
+
+    def near_mine():
+        return pltpu.make_async_copy(near_own, near_all.at[1], own_sem.at[marks])
+
+    steps = ((-1, seq > 0), (1, seq < lax.axis_size("seq") - 1))
+    if near:
+        near_mine().start()
+        for step, there in steps:
+
+            @pl.when(there)
+            def send(step=step):
+                near_copy(step).start()
 
     for item in range(late):
         late_own(item).start()
@@ -487,29 +546,42 @@
     for item in range(late):
         late_own(item).wait()
         late_copy(item).wait()
-
-
-def spread(shards, late, rows, collective_id):
+    if near:
+        near_mine().wait()
+        for step, there in steps:
+
+            @pl.when(there)
+            def finish(step=step):
+                near_copy(step).wait_send()
+                near_copy(-step).wait_recv()
+
+
+def spread(shards, late, rows, row_orders, near, collective_id):
     shapes = [(shard.shape[0], 2 * shard.shape[1]) for shard in shards]
     late_shapes = [(shard.shape[0], 2 * shard.shape[1]) for shard in late]
-    marks = len(late)
+    more = [] if near is None else [near]
+    marks = len(late) + len(more)
     plan = ordered(chunks_of(shapes), SPREAD, SPREAD_SHARES)
     if rows is not None:
         count, columns = rows.shape
-        for half, order in enumerate(SHARE):
+        for half, order in enumerate(row_orders):
             first = half * columns // 2
             plan.insert(half, (len(shards), 0, count, first, columns // 4, order))
         shards = shards + [rows]
         shapes.append(rows.shape)
+    leads = [4] * len(shapes)
+    if rows is not None:
+        leads[-1] = len(row_orders[0]) + 1
     space = pl.BlockSpec(memory_space=pl.ANY)
     results = pl.pallas_call(
-        functools.partial(spread_kernel, plan, len(shards), len(late)),
-        in_specs=[space] * (len(shards) + len(late)),
-        out_specs=[space] * (len(shards) + len(late)),
+        functools.partial(spread_kernel, plan, len(shards), len(late), len(more)),
+        in_specs=[space] * (len(shards) + marks),
+        out_specs=[space] * (len(shards) + marks),
         out_shape=[
-            jax.ShapeDtypeStruct((2, 2, 2, 2, rows, columns), bf16) for rows, columns in shapes
+            jax.ShapeDtypeStruct((2,) * lead + shape, bf16) for lead, shape in zip(leads, shapes)
         ]
-        + [jax.ShapeDtypeStruct(shape, bf16) for shape in late_shapes],
+        + [jax.ShapeDtypeStruct(shape, bf16) for shape in late_shapes]
+        + [jax.ShapeDtypeStruct((3,) + block.shape, bf16) for block in more],
         scratch_shapes=[
             pltpu.SemaphoreType.DMA((len(plan) + marks, 9)),
             pltpu.SemaphoreType.DMA((len(plan) + marks, 9)),
@@ -524,9 +596,10 @@
             transcendentals=0,
         ),
         name="spread",
-    )(*shards, *late)
+    )(*shards, *late, *more)
     return [
-        result.reshape(16 * rows, columns) for result, (rows, columns) in zip(results, shapes)
+        result.reshape((1 << lead) * shape[0], shape[1])
+        for result, lead, shape in zip(results, leads, shapes)
     ], results[len(shards) :]
 
 
@@ -550,7 +623,19 @@
 
 
 def reduce_plan(shapes):
-    return ordered(chunks_of(shapes), ORDERS, (0.39, 0.39, 0.22))
+    chunks = []
+    for source, (rows, columns) in enumerate(shapes):
+        half = columns // 2
+        if rows > 48:
+            for first in range(0, half, 128):
+                chunks.append((source, first, rows, (first, half + first), 128))
+        elif columns > 3 * D:
+            for first in range(0, half, HALF):
+                chunks.append((source, first, rows, (first, half + first), HALF))
+        else:
+            for first in range(0, half, HALF):
+                chunks.append((source, first, rows, (2 * first, 2 * first + HALF), HALF))
+    return ordered(chunks, ORDERS, (0.39, 0.39, 0.22))
 
 
 def stage_shapes(chunk):
@@ -573,19 +658,23 @@
 
 
 def reduce_kernel(plan, count, late, *refs):
-    sources = refs[:count]
-    late_rows = refs[count : count + late]
-    small_in = refs[count + late]
-    refs = refs[count + late + 1 :]
+    lefts = refs[:count]
+    rights = refs[count : 2 * count]
+    late_rows = refs[2 * count : 2 * count + late]
+    small_in, rows_in = refs[2 * count + late : 2 * count + late + 2]
+    refs = refs[2 * count + late + 2 :]
     outs = refs[:count]
     late_outs = refs[count : count + late]
-    small_out = refs[count + late]
-    scratch = list(refs[count + late + 1 :])
-    send_sem, recv_sem, own_sem, small_acc, small_recv = scratch[:5]
-    late_recv = scratch[5 : 5 + late]
-    scratch = scratch[5 + late :]
-    own = scratch[: len(plan)]
-    held = [scratch[len(plan) + 5 * i : len(plan) + 5 * i + 5] for i in range(len(plan))]
+    small_out, rows_out = refs[count + late : count + late + 2]
+    scratch = list(refs[count + late + 2 :])
+    send_sem, recv_sem, small_acc, small_recv, ring_low, ring_tall = scratch[:6]
+    rows_held = [rows_in] + scratch[6:9]
+    late_recv = scratch[9 : 9 + late]
+    scratch = scratch[9 + late :]
+    held = [scratch[5 * i : 5 * i + 5] for i in range(len(plan))]
+    turns = []
+    for item, chunk in enumerate(plan):
+        turns.append(sum(1 for other in plan[:item] if other[2] == chunk[2]))
 
     bit_of, partner = position()
     meet(partner)
@@ -600,19 +689,34 @@
             device_id_type=pl.DeviceIdType.MESH,
         )
 
+    def ring(item):
+        return (ring_low if plan[item][2] == 48 else ring_tall).at[turns[item] % RING]
+
     def core_copy(item):
-        source, row, rows, column, half, order = plan[item]
-        block = sources[source].at[
-            :, :, :, 1 - bit_of(CORE), pl.ds(row, rows), pl.ds(column, 2 * half)
-        ]
-        return remote(block, held[item][0], item, 0, CORE)
-
-    def own_copy(item):
-        source, row, rows, column, half, order = plan[item]
-        block = sources[source].at[
-            :, :, :, bit_of(CORE), pl.ds(row, rows), pl.ds(column, 2 * half)
-        ]
-        return pltpu.make_async_copy(block, own[item], own_sem.at[item])
+        return remote(ring(item).at[:, :, :, 1 - bit_of(CORE)], held[item][0], item, 0, CORE)
+
+    def produce(item):
+        source, column, rows, firsts, half, order = plan[item]
+        for before in range(item):
+            if plan[before][2] == rows and turns[before] == turns[item] - RING:
+                core_copy(before).wait_send()
+        target = ring(item)
+        block = 8 * 48
+        groups = block // (2 * rows)
+
+        def body(i, unused):
+            left = lefts[source][:, pl.ds(pl.multiple_of(i * block, 128), block)]
+            for n, first in enumerate(firsts):
+                grad = dot_tn(left, rights[source][:, first : first + half]).astype(bf16)
+                lanes = slice(n * half, (n + 1) * half)
+                if groups == 4:
+                    target[i, :, :, :, :, lanes] = grad.reshape(2, 2, 2, rows, half)
+                else:
+                    at = (i // 4, i // 2 % 2, i % 2)
+                    target[at + (slice(None), slice(None), lanes)] = grad.reshape(2, rows, half)
+            return 0
+
+        lax.fori_loop(0, 8 // groups, body, 0)
 
     def view(item, stage, mine):
         chunk = plan[item]
@@ -638,9 +742,11 @@
         return remote(source, small_recv.at[stage], len(plan), stage, EVERYONE[stage])
 
     def core_add(item):
+        own = ring(item)
+
         def body(i, unused):
             at = (i // 4, i // 2 % 2, i % 2)
-            held[item][0][at] = held[item][0][at] + own[item][at]
+            held[item][0][at] = held[item][0][at] + own[at + (bit_of(CORE),)]
             return 0
 
         lax.fori_loop(0, 8, body, 0)
@@ -659,10 +765,7 @@
                 kept = held[item][stage - 1][index[:at] + (bit,) + index[at:]]
             if stage == 4:
                 out = outs[chunk[0]]
-                first = chunk[3] // 2
-                out[pl.ds(chunk[1], chunk[2]), pl.ds(first, chunk[4])] = kept.astype(
-                    f32
-                ) + target[...].astype(f32)
+                out[:, pl.ds(chunk[1], chunk[4])] = kept.astype(f32) + target[...].astype(f32)
             else:
                 target[index] = kept + target[index]
             return 0
@@ -672,6 +775,28 @@
         else:
             body(0, 0)
 
+    rows_axes = (CORE, ROW, LOW)
+
+    def rows_copy(stage):
+        axis = rows_axes[stage]
+        block = rows_held[stage].at[(slice(None),) * (2 - stage) + (1 - bit_of(axis),)]
+        return remote(block, rows_held[stage + 1], len(plan) + 1 + late, stage, axis)
+
+    def rows_add(stage):
+        def body(i, unused):
+            index = tuple(i // (1 << (1 - stage - n)) % 2 for n in range(2 - stage))
+            kept = rows_held[stage][index + (bit_of(rows_axes[stage]),)]
+            if stage == 2:
+                rows_out[...] = kept.astype(f32) + rows_held[3][...].astype(f32)
+            else:
+                rows_held[stage + 1][index] = kept + rows_held[stage + 1][index]
+            return 0
+
+        if stage == 2:
+            body(0, 0)
+        else:
+            lax.fori_loop(0, 1 << (2 - stage), body, 0)
+
     def late_lanes(item, mine):
         half = late_recv[item].shape[1]
         bit = bit_of(COLUMN) if mine else 1 - bit_of(COLUMN)
@@ -681,25 +806,31 @@
         block = late_rows[item].at[:, late_lanes(item, False)]
         return remote(block, late_recv[item], len(plan) + 1 + item, 0, COLUMN)
 
-    for item in range(len(plan)):
-        core_copy(item).start()
-        own_copy(item).start()
     small_copy(0).start()
+    rows_copy(0).start()
     for item in range(late):
         late_copy(item).start()
     events = sorted(
-        (item + LAGS[stage], stage, item) for item in range(len(plan)) for stage in range(5)
+        (item + LAGS[stage + 1], stage, item) for item in range(len(plan)) for stage in range(-1, 5)
     )
     for unused, stage, item in events:
+        if stage < 0:
+            produce(item)
+            core_copy(item).start()
+            continue
         if stage == 0:
             core_copy(item).wait_recv()
-            own_copy(item).wait()
             core_add(item)
         else:
             stage_copy(item, stage).wait_recv()
             stage_add(item, stage)
         if stage < 4:
             stage_copy(item, stage + 1).start()
+        if item == 0 and stage < 3:
+            rows_copy(stage).wait()
+            rows_add(stage)
+            if stage < 2:
+                rows_copy(stage + 1).start()
         if item == 0:
             small_copy(stage).wait()
             before = small_in[...] if stage == 0 else small_acc[stage - 1]
@@ -715,52 +846,54 @@
             f32
         ) + late_recv[item][...].astype(f32)
     for item in range(len(plan)):
-        core_copy(item).wait_send()
+        same = [other for other in plan[item:] if other[2] == plan[item][2]]
+        if len(same) <= RING:
+            core_copy(item).wait_send()
         for stage in range(1, 5):
             stage_copy(item, stage).wait_send()
 
 
-def reduce_all(grads, late, small):
-    shapes = [(grad.shape[0] // 16, grad.shape[1]) for grad in grads]
+def reduce_all(factors, late, small, rows):
+    lefts = [left for left, right in factors]
+    rights = [right for left, right in factors]
+    shapes = [(left.shape[1] // 16, right.shape[1]) for left, right in factors]
     plan = reduce_plan(shapes)
     scratch = [
-        pltpu.SemaphoreType.DMA((len(plan) + 1 + len(late), 5)),
-        pltpu.SemaphoreType.DMA((len(plan) + 1 + len(late), 5)),
-        pltpu.SemaphoreType.DMA((len(plan),)),
+        pltpu.SemaphoreType.DMA((len(plan) + 2 + len(late), 5)),
+        pltpu.SemaphoreType.DMA((len(plan) + 2 + len(late), 5)),
         pltpu.VMEM((4, SMALL, D), f32),
         pltpu.VMEM((5, SMALL, D), f32),
+        pltpu.VMEM((RING, 2, 2, 2, 2, 48, D), bf16),
+        pltpu.VMEM((RING, 2, 2, 2, 2, 192, 256), bf16),
     ]
+    own_rows = rows.shape[0] // 8
+    scratch += [pltpu.VMEM((2,) * n + (own_rows, D), bf16) for n in (2, 1, 0)]
     late_shapes = [(rows.shape[0], rows.shape[1] // 2) for rows in late]
     scratch += [pltpu.VMEM(shape, bf16) for shape in late_shapes]
-    scratch += [pltpu.VMEM(buffer_shape(c, stage_shapes(c)[0]), bf16) for c in plan]
     for chunk in plan:
         shapes_held = stage_shapes(chunk)
         scratch += [pltpu.VMEM(buffer_shape(chunk, h), bf16) for h in shapes_held]
-    operands = [
-        grad.reshape(2, 2, 2, 2, rows, columns) for grad, (rows, columns) in zip(grads, shapes)
-    ]
-    space = pl.BlockSpec(memory_space=pl.ANY)
     near = pl.BlockSpec(memory_space=pltpu.VMEM)
     results = pl.pallas_call(
-        functools.partial(reduce_kernel, plan, len(grads), len(late)),
-        in_specs=[space] * len(grads) + [near] * (len(late) + 1),
-        out_specs=[near] * (len(grads) + len(late) + 1),
+        functools.partial(reduce_kernel, plan, len(factors), len(late)),
+        in_specs=[near] * (2 * len(factors) + len(late) + 2),
+        out_specs=[near] * (len(factors) + len(late) + 2),
         out_shape=[jax.ShapeDtypeStruct((rows, columns // 2), f32) for rows, columns in shapes]
         + [jax.ShapeDtypeStruct(shape, f32) for shape in late_shapes]
-        + [jax.ShapeDtypeStruct((SMALL, D), f32)],
+        + [jax.ShapeDtypeStruct((SMALL, D), f32), jax.ShapeDtypeStruct((own_rows, D), f32)],
         scratch_shapes=scratch,
         compiler_params=pltpu.CompilerParams(
             collective_id=1, has_side_effects=True, vmem_limit_bytes=60 * 1024 * 1024
         ),
         name="reduce_all",
-    )(*operands, *late, small)
-    return results[: len(grads)], results[len(grads) : -1], results[-1]
+    )(*lefts, *rights, *late, small, rows.reshape(2, 2, 2, own_rows, D))
+    return results[: len(factors)], results[len(factors) : -2], results[-2], results[-1]
 
 
 MERGE = ((CORE, ROW, LOW, HIGH), (CORE, LOW, HIGH, ROW))
 SHARE = ((HIGH, LOW, ROW), (ROW, HIGH, LOW))
+GROUP_SHARE = ((LOW, ROW), (ROW, LOW))
 SLOT_AXES = (HIGH, LOW, ROW, CORE)
-HALF = D // 2
 HALF_HEADS = HEADS // 2
 HALF_STATS = STATS // 2
 
@@ -1067,6 +1200,13 @@
     dp_count = lax.axis_size("dp")
     part = D // seq_count
     wide = D // dp_count
+    row_count = enc_input.shape[1]
+    dec_rows = dec_input.shape[1]
+    group_size = TGT // dec_rows
+    groups = [
+        list(range(first, first + group_size)) for first in range(0, seq_count, group_size)
+    ]
+    here = dp_count == 2 and seq_count == 16 and group_size == 8 and row_count == PASS
 
     def flat(master):
         shard = master.astype(bf16)
@@ -1074,26 +1214,38 @@
             shard = shard.transpose(1, 0, 2).reshape(part, -1)
         return shard
 
-    here = dp_count == 2 and seq_count == 16
-
-    def gathered(masters, late, rows, collective_id):
+
+    def gathered(masters, late, rows, row_groups, near, collective_id):
         shards = [flat(master) for master in masters]
         late = [flat(master) for master in late]
         if here:
-            return spread(shards, late, rows, collective_id)
+            row_orders = SHARE if row_groups is None else GROUP_SHARE
+            return spread(shards, late, rows, row_orders, near, collective_id)
         weights, late = spread_plainly(shards, late)
         if rows is not None:
-            weights.append(lax.all_gather(rows, "seq", axis=0, tiled=True))
+            weights.append(
+                lax.all_gather(rows, "seq", axis=0, tiled=True, axis_index_groups=row_groups)
+            )
+        if near is not None:
+            forward = [(i, i + 1) for i in range(seq_count - 1)]
+            low = lax.ppermute(near[row_count - PASS :], "seq", forward)
+            high = lax.ppermute(near[:PASS], "seq", [(i + 1, i) for i in range(seq_count - 1)])
+            late.append(jnp.concatenate([low, near, high], axis=0))
         return weights, late
 
-    (self_qkv_w, enc_qkv_w, self_out_w, cross_q_w), unused = gathered(
-        (self_qkv, enc_qkv, self_out, cross_qkv[0]), (), None, 2
-    )
+    weights, unused = gathered(
+        (self_qkv[1:], self_qkv[0], enc_qkv, self_out, cross_qkv[0]),
+        (),
+        dec_input[0],
+        groups,
+        None,
+        2,
+    )
+    self_kv_w, self_q_w, enc_qkv_w, self_out_w, cross_q_w, group_input = weights
 
     enc_gains_w = enc_gains.astype(bf16).astype(f32)
     dec_gains_w = dec_gains.astype(bf16).astype(f32)
     tokens = enc_input[0].astype(f32)
-    row_count = tokens.shape[0]
     key_span = row_count + 2 * PASS
     passage = passage_ids[0]
     lengths = target_lengths[0]
@@ -1121,17 +1273,12 @@
     ).reshape(HEADS, 5 * KEYS, KEYS)
 
     dec_tokens = dec_input[0].astype(f32)
-    dec_rows = dec_tokens.shape[0]
     dec_total = dec_rows * seq_count
     slot_first = seq_index * dec_rows
     my_query = slot_first // TGT
     my_place = slot_first % TGT + jnp.arange(dec_rows, dtype=jnp.int32)
     my_length = lax.dynamic_index_in_dim(lengths, my_query, 0, keepdims=False)
     valid_rows = (my_place < my_length).astype(f32)[:, None]
-    group_size = TGT // dec_rows
-    groups = [
-        list(range(first, first + group_size)) for first in range(0, seq_count, group_size)
-    ]
     group_place = jnp.arange(TGT, dtype=jnp.int32)
     self_marks = jnp.where(group_place < my_length, group_place, FAR)
     self_spans = jnp.stack(
@@ -1139,15 +1286,11 @@
     ).astype(jnp.int32)
 
     dec_normed_one = norm_apply(dec_tokens, dec_gains_w[0]).astype(bf16)
-    self_proj = matmul(dec_normed_one, self_qkv_w).astype(bf16)
-    if here:
-        (self_near,) = share_all((self_proj[:, D:],), ((LOW, ROW), (ROW, LOW)), 6)
-        self_near = self_near.reshape(TGT, 2 * D)
-    else:
-        self_near = lax.all_gather(
-            self_proj[:, D:], "seq", axis=0, tiled=True, axis_index_groups=groups
-        )
-    self_args = (self_proj, 0, self_near, 0, 1, my_place, self_marks, self_spans, None)
+    group_tokens = group_input.astype(f32)
+    group_normed = norm_apply(group_tokens, dec_gains_w[0]).astype(bf16)
+    self_queries = matmul(dec_normed_one, self_q_w).astype(bf16)
+    self_kv = matmul(group_normed, self_kv_w).astype(bf16)
+    self_args = (self_queries, 0, self_kv, 0, 1, my_place, self_marks, self_spans, None)
     self_mix_b, self_stat = attend(*self_args, dec_rows, True)
     dec_hidden = dec_tokens + matmul(self_mix_b, self_out_w)
     dec_normed_two = norm_apply(dec_hidden, dec_gains_w[1]).astype(bf16)
@@ -1155,27 +1298,21 @@
 
     normed_one = norm_apply(tokens, enc_gains_w[0]).astype(bf16)
     enc_proj = matmul(normed_one, enc_qkv_w).astype(bf16)
-    cross_queries, enc_proj = lax.optimization_barrier((cross_queries, enc_proj))
-    (enc_out_w, cross_kv_w, enc_up_w, enc_down_w, cross_out_w, all_queries), late_rows = gathered(
+    weights, late_rows = gathered(
         (enc_out, cross_qkv[1:], enc_up, enc_down, cross_out),
         (dec_up, dec_down),
         cross_queries,
+        None,
+        enc_proj[:, D:],
         3,
     )
+    enc_out_w, cross_kv_w, enc_up_w, enc_down_w, cross_out_w, all_queries = weights
+    enc_near = late_rows[2].reshape(key_span, 2 * D)
     dec_up_w, dec_down_w = [
-        lax.all_gather(rows, "seq", axis=0, tiled=True) for rows in late_rows
+        lax.all_gather(rows, "seq", axis=0, tiled=True) for rows in late_rows[:2]
     ]
     forward = [(i, i + 1) for i in range(seq_count - 1)]
     backward = [(i + 1, i) for i in range(seq_count - 1)]
-    own_kv = enc_proj[:, D:]
-    enc_near = jnp.concatenate(
-        [
-            lax.ppermute(own_kv[row_count - PASS :], "seq", forward),
-            own_kv,
-            lax.ppermute(own_kv[:PASS], "seq", backward),
-        ],
-        axis=0,
-    )
     enc_args = (enc_proj, 0, enc_near, 0, 1, row_ids, key_ids, enc_spans, band)
     enc_mixed_b, enc_stat = attend(*enc_args, KEYS, False)
     enc_hidden = tokens + matmul(enc_mixed_b, enc_out_w)
@@ -1186,7 +1323,7 @@
     cross_kv = matmul(encoded_b, cross_kv_w).astype(bf16)
 
     key_owner = row_ids // PASS_N
-    cross_rows = 256
+    cross_rows = CROSS_ROWS
     block_query = jnp.arange(dec_total // cross_rows, dtype=jnp.int32) * cross_rows // TGT
     own_first = jnp.sum(key_owner[None, :] < block_query[:, None], axis=1)
     own_last = jnp.sum(key_owner[None, :] <= block_query[:, None], axis=1)
@@ -1226,7 +1363,6 @@
     )
     grad_hidden_two = grad_hidden_two + grad_final
     grad_cross_b = grad_hidden_two.astype(bf16)
-    grad_cross_out = grad_of(cross_mix_b, grad_cross_b)
     late = [
         lax.psum_scatter(grad.astype(bf16), "seq", scatter_dimension=0, tiled=True)
         for grad in (grad_dec_up, grad_dec_down)
@@ -1245,56 +1381,42 @@
         all_stats = lax.all_gather(
             jnp.concatenate([cross_stat, cross_dot], axis=0).T, "seq", axis=0, tiled=True
         ).T
-    part_dq, cross_dk, cross_dv = attend_back(
+    part_dq, cross_kv_grad = attend_back(
         *cross_args, cross_rows, False, all_grads, all_stats[:STATS], all_stats[STATS:]
     )
     came_dq = lax.all_to_all(part_dq, "seq", 0, 0, tiled=True).reshape(seq_count, dec_rows, D)
     grad_cross_q_b = jnp.sum(came_dq.astype(f32), axis=0).astype(bf16)
-    grad_cross_qw = grad_of(dec_normed_two, grad_cross_q_b)
     grad_hidden, grad_gain_two = norm_back(
         dec_hidden, dec_gains_w[1], back_of(grad_cross_q_b, cross_q_w)
     )
     grad_hidden = grad_hidden + grad_hidden_two
-    cross_kv_grad = jnp.concatenate([cross_dk, cross_dv], axis=1)
-    grad_cross_kvw = grad_of(encoded_b, cross_kv_grad)
     grad_encoded = back_of(cross_kv_grad, cross_kv_w)
     grad_self_b = grad_hidden.astype(bf16)
-    grad_self_out = grad_of(self_mix_b, grad_self_b)
     grad_self_mix = back_of(grad_self_b, self_out_w).astype(bf16)
     self_dot = per_head_dot(grad_self_mix, self_mix_b)
-    self_dq, self_dk, self_dv = attend_back(
+    self_dq, self_dkv = attend_back(
         *self_args, dec_rows, True, grad_self_mix, self_stat, self_dot
     )
-    came_dkv = lax.all_to_all(
-        jnp.concatenate([self_dk, self_dv], axis=1),
-        "seq",
-        0,
-        0,
-        tiled=True,
-        axis_index_groups=groups,
-    ).reshape(group_size, dec_rows, 2 * D)
-    self_dkv = jnp.sum(came_dkv.astype(f32), axis=0).astype(bf16)
-    self_grad_b = jnp.concatenate([self_dq, self_dkv], axis=1)
-    grad_self_qkv = grad_of(dec_normed_one, self_grad_b)
-    grad_dec_in, grad_gain_one = norm_back(
-        dec_tokens, dec_gains_w[0], back_of(self_grad_b, self_qkv_w)
-    )
-    grad_dec_in = grad_dec_in + grad_hidden
+    group_scale = lax.rsqrt(jnp.mean(group_tokens * group_tokens, axis=-1, keepdims=True) + EPSILON)
+    dec_scale = lax.rsqrt(jnp.mean(dec_tokens * dec_tokens, axis=-1, keepdims=True) + EPSILON)
+    grad_group = back_of(self_dkv, self_kv_w)
+    grad_own = back_of(self_dq, self_q_w)
+    grad_gain_one = jnp.sum(grad_group * (group_tokens * group_scale), axis=0) + jnp.sum(
+        grad_own * (dec_tokens * dec_scale), axis=0
+    )
+    grad_group_b = grad_group.astype(bf16)
     grad_dec_gains = jnp.stack([grad_gain_one, grad_gain_two, grad_gain_three])
 
     grad_encoded_b = grad_encoded.astype(bf16)
-    grad_enc_down = grad_of(enc_active, grad_encoded_b)
     grad_enc_inner = gelu_back(enc_inner, back_of(grad_encoded_b, enc_down_w)).astype(bf16)
-    grad_enc_up = grad_of(normed_two, grad_enc_inner)
     grad_enc_hidden, grad_enc_gain_two = norm_back(
         enc_hidden, enc_gains_w[1], back_of(grad_enc_inner, enc_up_w)
     )
     grad_enc_hidden = grad_enc_hidden + grad_encoded
     grad_attn_b = grad_enc_hidden.astype(bf16)
-    grad_enc_out = grad_of(enc_mixed_b, grad_attn_b)
     grad_enc_mix = back_of(grad_attn_b, enc_out_w).astype(bf16)
     enc_dot = per_head_dot(grad_enc_mix, enc_mixed_b)
-    enc_dq, enc_dk, enc_dv, grad_band = attend_back(
+    enc_dq, near_grad, grad_band = attend_back(
         *enc_args, KEYS, False, grad_enc_mix, enc_stat, enc_dot
     )
     table_part = lax.dot_general(
@@ -1304,42 +1426,45 @@
         precision=PRECISE,
         preferred_element_type=f32,
     )
-    near_grad = jnp.concatenate([enc_dk, enc_dv], axis=1)
     from_higher = lax.ppermute(near_grad[:PASS], "seq", backward)
     from_lower = lax.ppermute(near_grad[key_span - PASS :], "seq", forward)
     own_grad = near_grad[PASS : PASS + row_count].astype(f32)
     own_grad = own_grad.at[row_count - PASS :].add(from_higher.astype(f32))
     own_grad = own_grad.at[:PASS].add(from_lower.astype(f32))
     enc_grad_b = jnp.concatenate([enc_dq, own_grad.astype(bf16)], axis=1)
-    grad_enc_qkv = grad_of(normed_one, enc_grad_b)
     grad_enc_in, grad_enc_gain_one = norm_back(
         tokens, enc_gains_w[0], back_of(enc_grad_b, enc_qkv_w)
     )
     grad_enc_in = grad_enc_in + grad_enc_hidden
     grad_enc_gains = jnp.stack([grad_enc_gain_one, grad_enc_gain_two])
-    grads = (
-        grad_cross_out,
-        grad_cross_kvw,
-        grad_cross_qw,
-        grad_self_out,
-        grad_self_qkv,
-        grad_enc_down,
-        grad_enc_up,
-        grad_enc_out,
-        grad_enc_qkv,
-    )
-    grads = [grad.astype(bf16) for grad in grads]
+    factors = (
+        (cross_mix_b, grad_cross_b),
+        (encoded_b, cross_kv_grad),
+        (dec_normed_two, grad_cross_q_b),
+        (self_mix_b, grad_self_b),
+        (group_normed, self_dkv),
+        (dec_normed_one, self_dq),
+        (enc_active, grad_encoded_b),
+        (normed_two, grad_enc_inner),
+        (enc_mixed_b, grad_attn_b),
+        (normed_one, enc_grad_b),
+    )
     gains_part = jnp.concatenate([grad_enc_gains, grad_dec_gains], axis=0)
     if here:
         table_row = jnp.pad(table_part.reshape(1, -1), ((0, 0), (0, D - BUCKETS * HEADS)))
         small = jnp.concatenate([gains_part, table_row], axis=0)
         small = jnp.pad(small, ((0, SMALL - small.shape[0]), (0, 0)))
-        sums, late, small = reduce_all(grads, late, small)
+        sums, late, small, grad_normed = reduce_all(factors, late, small, grad_group_b)
         gains_total = small[:5]
         table_grad = small[5, : BUCKETS * HEADS].reshape(BUCKETS, HEADS)
     else:
         gains_total, table_grad = lax.psum((gains_part, table_part), ("dp", "seq"))
-        sums, late = reduce_plainly(grads, late)
+        sums, late = reduce_plainly([grad_of(*pair).astype(bf16) for pair in factors], late)
+        grad_normed = lax.psum_scatter(
+            grad_group_b, "seq", scatter_dimension=0, tiled=True, axis_index_groups=groups
+        ).astype(f32)
+    grad_dec_in, unused = norm_back(dec_tokens, dec_gains_w[0], grad_normed + grad_own)
+    grad_dec_in = grad_dec_in + grad_hidden
 
     def threes(rows):
         return rows.reshape(part, -1, wide).transpose(1, 0, 2)
@@ -1349,13 +1474,13 @@
         grad_enc_in[None],
         grad_dec_in[None],
         gains_total[:2],
-        threes(sums[8]),
+        threes(sums[9]),
+        sums[8],
+        table_grad,
         sums[7],
-        table_grad,
         sums[6],
-        sums[5],
         gains_total[2:],
-        threes(sums[4]),
+        jnp.concatenate([sums[5][None], threes(sums[4])], axis=0),
         sums[3],
         jnp.concatenate([sums[2][None], threes(sums[1])], axis=0),
         sums[0],

time: 779 us -> 682 us (0.88)
  starting transfers between devices: 48.6 us -> 12.9 us
  Pallas kernels: 486 us -> 460 us
  matrix products: 106 us -> 89.1 us
  local copies, waits for them, and re-layouts: 68.9 us -> 57.2 us
    pallas_call x1, Pallas kernels: 111 us -> 151 us  [reduce_all(): pl.pallas_call(functools.partial(reduce_kernel, plan, len(factors), len(l...]
    dot_general x11 -> x2, matrix products: 37.1 us -> 7.38 us  [grad_of(): lax.dot_general(left_side, right_side, (((0,), (0,)), ((), ())), preferre...]
    all_to_all x1 -> x0, starting transfers between devices: 27.1 us -> none  [per_device(): lax.all_to_all(jnp.concatenate([self_dk, self_dv], axis=1), 'seq', 0, 0,...]
    pallas_call x3, Pallas kernels: 65.7 us -> 45 us  [attend_back(): pl.pallas_call(functools.partial(attend_back_kernel, causal, bias is not...]
    pallas_call x3, Pallas kernels: 48.5 us -> 29.2 us  [attend(): pl.pallas_call(functools.partial(attend_kernel, causal, bias is not None)...]
    pallas_call x2 -> x1, Pallas kernels: 47.5 us -> 30.5 us  [share_all(): pl.pallas_call(functools.partial(share_kernel, orders, axes, kinds), in_s...]
    pallas_call x1, Pallas kernels: 65.8 us -> 54.7 us  [merge_all(): pl.pallas_call(merge_kernel, in_specs=[near] * 2, out_specs=[near] * 2, o...]
    dot_general x11 -> x12, matrix products: 32.8 us -> 41.9 us  [back_of(): lax.dot_general(gradient, weight, (((1,), (1,)), ((), ())), preferred_ele...]
  transfers between devices with their start and end apart: 10 -> 7, of which waited for: 2 -> 3; matrix products, arithmetic and copies ran while one was open for 19% -> 17% of each run, Pallas kernels for 26% -> 23%
where the time goes in v3:
time: 682 us; the launch traced here: 674 us
  Pallas kernels  460 us (67%)
  matrix products  89.1 us (13%)
  local copies, waits for them, and re-layouts  57.2 us (8%)
  other arithmetic  27.9 us (4%)
  between operations  15.7 us (2%)
  starting transfers between devices  12.9 us (2%)
  waiting for transfers between devices  11.3 us (2%)
    pallas_call x1, Pallas kernels, reduce_all(): pl.pallas_call(functools.partial(reduce_kernel, plan, len(factors), len(l...  151 us
    pallas_call x2, Pallas kernels, spread(): pl.pallas_call(functools.partial(spread_kernel, plan, len(shards), len(la...  150 us
    pallas_call x1, Pallas kernels, merge_all(): pl.pallas_call(merge_kernel, in_specs=[near] * 2, out_specs=[near] * 2, o...  54.7 us
    pallas_call x3, Pallas kernels, attend_back(): pl.pallas_call(functools.partial(attend_back_kernel, causal, bias is not...  45 us
    dot_general x12, matrix products, back_of(): lax.dot_general(gradient, weight, (((1,), (1,)), ((), ())), preferred_ele...  41.9 us
    unnamed x262, local copies, waits for them, and re-layouts  36.8 us
    dot_general x12, matrix products, matmul(): return jnp.dot(left_side, right_side, preferred_element_type=f32)  30.9 us
    pallas_call x1, Pallas kernels, share_all(): pl.pallas_call(functools.partial(share_kernel, orders, axes, kinds), in_s...  30.5 us
  transfers between devices with their start and end apart: 7, of which 3 were waited for; matrix products, arithmetic and copies ran while one was open for 17% of the time, Pallas kernels for 23%

profile of v3, /device:TPU:0, one launch (start us, length us, event | category | flops | bytes accessed | tf_op | source)
XLA Modules:
  0.0 673.7 jit_solution(1035729116388232144)
XLA Ops:
  10.8 54.6 %spread.2 = (bf16[2,2,2,2,48,1536]{5,4,3,2,1,0:T(8,128)(2,1)S(1)}, bf16[2,2,2,2,48,768]{5,4,3,2,1,0:T(8,128)(2,1)S(1)}, bf16[2,2,2,2,48,2304]{5,4,3,2,1,0:T(8,12...) custom-call(bf16[48,768]{1,0:T(8,128)(2,1)S(1)} %bitcast.284, ...), custom_call_target="tpu_custom_call" | custom-call | flops 134400000000 | tf_op jit(solution)/shard_map/spread/pallas_call | solution.py:576
  80.0 4.5 shard_map.307
  91.3 95.0 %spread.3 = (bf16[2,2,2,2,48,768]{5,4,3,2,1,0:T(8,128)(2,1)S(1)}, bf16[2,2,2,2,48,1536]{5,4,3,2,1,0:T(8,128)(2,1)S(1)}, bf16[2,2,2,2,48,3072]{5,4,3,2,1,0:T(8,12...) custom-call(bf16[48,384]{1,0:T(8,128)(2,1)S(1)} %convert_element_typ, ...), custom_call_target="tpu_custom_call" | custom-call | flops 192000000000 | tf_op jit(solution)/shard_map/spread/pallas_call | solution.py:576
  207.5 11.7 %shard_map.308 = (bf16[384,768]{1,0:T(8,128)(2,1)}, f32[16,384]{1,0:T(8,128)}) custom-call(s32[6]{0:T(128)} %reshape.790.spans_ref, bf16[384,2304]{1,0:T(8,128)(2,1)} %copy-done.28, bf16[1152,1536]{1,0:T(8,128)(2,1)} %bitcast.261, bf16[1152,1536]{1,0:T(8,128)(2,1)} %bitcast.262, s32[3,1,128]{2,1,0:T(1,128)} %get-tuple-element.250.row_ref, ...), custom_call_target="tpu_custom_call" | custom-call | flops 452984832 | bytes 7077888 | tf_op jit(solution)/shard_map/pallas_call | solution.py:176
  222.6 8.2 %multiply_convert_fusion = (bf16[384,3072]{1,0:T(8,128)(2,1)S(1)}, f32[384,3072]{1,0:T(8,128)}) fusion(bf16[384,768]{1,0:T(8,128)(2,1)S(1)} %multiply_convert_fusion.4.refs_7_, bf16[768,3072]{1,0:T(8,128)(2,1)} %bitcast.285), kind=kOutput, calls=%fused_computation.16 | convolution fusion | flops 1822556160 | bytes 12386304 | tf_op jit(solution)/shard_map/dot_general | solution.py:63
  235.5 13.0 %shard_map.309 = (bf16[1536,768]{1,0:T(8,128)(2,1)}, f32[16,1536]{1,0:T(8,128)}) custom-call(s32[8]{0:T(128)} %reshape.784.spans_ref, bf16[1536,768]{1,0:T(8,128)(2,1)} %bitcast.265, bf16[384,1536]{1,0:T(8,128)(2,1)} %convolution_convert_fusion.4.k_ref.v_ref, bf16[384,1536]{1,0:T(8,128)(2,1)} %convolution_convert_fusion.4.k_ref.v_ref, ...), custom_call_target="tpu_custom_call" | custom-call | flops 603979776 | bytes 2359296 | tf_op jit(solution)/shard_map/pallas_call | solution.py:176
  251.3 54.7 %merge_all.1 = (f32[96,768]{1,0:T(8,128)S(1)}, f32[2,8,96]{2,1,0:T(8,128)S(1)}) custom-call(bf16[2,2,2,2,96,768]{5,4,3,2,1,0:T(8,128)(2,1)S(1)} %bitcast.278, f32[2,2,2,2,2,8,96]{6,5,4,3,2,1,0:T(8,128)S(1)} %bitcast.280), custom_call_target="tpu_custom_call" | custom-call | tf_op jit(solution)/shard_map/merge_all/pallas_call | solution.py:1011
  308.3 4.4 fusion.75
  313.3 4.5 fusion.31
  322.9 4.8 multiply_reduce_fusion.5
  329.5 30.5 %share_all.1 = (bf16[2,2,2,2,96,768]{5,4,3,2,1,0:T(8,128)(2,1)S(1)}, f32[2,2,2,2,2,16,96]{6,5,4,3,2,1,0:T(8,128)S(1)}) custom-call(bf16[96,768]{1,0:T(8,128)(2,1)S(1)} %get-tuple-element.264.refs_0_, f32[2,16,96]{2,1,0:T(8,128)S(1)} %select_maximum_fusion.refs_1_), custom_call_target="tpu_custom_call" | custom-call | tf_op jit(solution)/shard_map/share_all/pallas_call | solution.py:1112
  363.1 20.0 %shard_map.310 = (bf16[1536,768]{1,0:T(8,128)(2,1)}, bf16[384,1536]{1,0:T(8,128)(2,1)}) custom-call(s32[8]{0:T(128)} %reshape.784.spans_ref, bf16[1536,768]{1,0:T(8,128)(2,1)} %bitcast.266, bf16[384,1536]{1,0:T(8,128)(2,1)} %convolution_convert_fusion.4.k_ref.v_ref, bf16[384,1536]{1,0:T(8,128)(2,1)} %convolution_convert_fusion.4.k_ref.v_ref, ...), custom_call_target="tpu_custom_call" | custom-call | flops 1509949440 | bytes 4718592 | tf_op jit(solution)/shard_map/pallas_call | solution.py:316
  386.6 3.7 convolution_convert_fusion
  390.4 8.9 %fusion.10.refs_17_ = bf16[384,3072]{1,0:T(8,128)(2,1)} fusion(f32[384,3072]{1,0:T(8,128)} %get-tuple-element.259, bf16[384,768]{1,0:T(8,128)(2,1)S(1)} %get-tuple-element.265.refs_16_, bf16[3072,768]{1,0:T(8,128)(2,1)} %bitcast.287), kind=kOutput, calls=%fused_computation.15 | convolution fusion | flops 1835532288 | bytes 12386304 | tf_op jit(solution)/shard_map/dot_general | solution.py:73
  400.5 6.8 %multiply_reduce_fusion.2 = (f32[768]{0:T(1024)}, f32[384]{0:T(512)}, f32[384,768]{1,0:T(8,128)}) fusion(f32[384,768]{1,0:T(8,128)S(1)} %copy-done.30, f32[384]{0:T(512)S(1)} %copy-done.96, f32[768]{0:T(1024)S(1)} %copy-done.88, bf16[384,3072]{1,0:T(8,128)(2,1)} %fusion.10.refs_17_, bf16[768,3072]{1,0:T(8,128)(2,1)} %bitcast.286), kind=kOutput, calls=%fused_computation.59 | convolution fusion | flops 1813707648 | bytes 9446400 | tf_op jit(solution)/shard_map/dot_general | solution.py:73
  407.3 7.4 %all-to-all-start = ((bf16[16,96,768]{2,1,0:T(8,128)(2,1)}), bf16[16,96,768]{2,1,0:T(8,128)(2,1)}, u32[]{:S(2)}, u32[]{:S(2)}) async-start(bf16[16,96,768]{2,1,0:T(8,128)(2,1)} %bitcast.302), calls=%async_computation | async-start | bytes 4718592 | tf_op jit(solution)/shard_map/all_to_all | solution.py:1387
  421.2 19.1 %shard_map.311 = (bf16[384,768]{1,0:T(8,128)(2,1)}, bf16[1152,1536]{1,0:T(8,128)(2,1)}, f32[12,640,128]{2,1,0:T(8,128)}) custom-call(s32[6]{0:T(128)} %reshape.790.spans_ref, bf16[384,2304]{1,0:T(8,128)(2,1)} %copy-done.28, bf16[1152,1536]{1,0:T(8,128)(2,1)} %bitcast.263, bf16[1152,1536]{1,0:T(8,128)(2,1)} %bitcast.264, ...), custom_call_target="tpu_custom_call" | custom-call | flops 1132462080 | bytes 14155776 | tf_op jit(solution)/shard_map/pallas_call | solution.py:316
  454.4 5.4 fusion
  460.0 4.1 fusion.37
  472.6 6.2 all-to-all-done
  484.3 5.9 shard_map.312
  492.4 5.1 fusion.84
  498.2 3.7 reduce-scatter.5.cloned.1.call-done.refs_21_
  501.9 150.7 %reduce_all.1 = (f32[48,384]{1,0:T(8,128)}, f32[48,768]{1,0:T(8,128)}, f32[48,384]{1,0:T(8,128)}, f32[48,384]{1,0:T(8,128)}, f32[48,768]{1,0:T(8,128)}, /*index=...) custom-call(bf16[96,768]{1,0:T(8,128)(2,1)} %copy-done.48, ...), custom_call_target="tpu_custom_call" | custom-call | tf_op jit(solution)/shard_map/reduce_all/pallas_call | solution.py:877
  (411 shorter events, 125.1 us)
Async XLA Ops:
  7.2 193.3 %copy-start = (f32[32,12]{0,1:T(8,128)S(1)}, f32[32,12]{0,1:T(8,128)}, u32[]{:S(2)}) copy-start(f32[32,12]{0,1:T(8,128)} %param.34) | copy-start | bytes 4612
  7.2 301.0 %all-gather.3.cloned.1.call-start = ((), (), s32[]{:S(2)}) async-start(), calls=%async_computation.3 | async-start | bytes 5013504 | tf_op jit(solution)/shard_map/all_gather | solution.py:1312
  10.6 64.6 %copy-start.72 = (f32[768]{0:T(1024)}, f32[768]{0:T(1024)S(1)}, u32[]{:S(2)}) copy-start(f32[768]{0:T(1024)S(1)} %get-tuple-element.222) | copy-start | bytes 9220
  10.6 79.6 %copy-start.83 = (f32[768]{0:T(1024)}, f32[768]{0:T(1024)S(1)}, u32[]{:S(2)}) copy-start(f32[768]{0:T(1024)S(1)} %get-tuple-element.221) | copy-start | bytes 9220
  10.7 54.6 %copy-start.115 = (f32[96]{0:T(128)}, f32[96]{0:T(128)S(1)}, u32[]{:S(2)}) copy-start(f32[96]{0:T(128)S(1)} %fusion.53) | copy-start | bytes 1156
  10.8 64.5 %copy-start.107 = (f32[96]{0:T(128)}, f32[96]{0:T(128)S(1)}, u32[]{:S(2)}) copy-start(f32[96]{0:T(128)S(1)} %fusion.70) | copy-start | bytes 1156
  91.3 105.0 %copy-start.90 = (s32[1,6144]{1,0:T(1,128)S(1)}, s32[1,6144]{1,0:T(1,128)}, u32[]{:S(2)}) copy-start(s32[1,6144]{1,0:T(1,128)} %param.28) | copy-start | bytes 73732
  195.2 118.1 %all-gather.5.cloned.1.call-start = ((), (), s32[]{:S(2)}) async-start(), calls=%async_computation.4 | async-start | bytes 5013504 | tf_op jit(solution)/shard_map/all_gather | solution.py:1312
  195.9 302.3 %reduce-scatter.3.cloned.1.call-start = ((), (), s32[]{:S(2)}) async-start(), calls=%async_computation.5 | async-start | bytes 5013504 | tf_op jit(solution)/shard_map/reduce_scatter | solution.py:1367
  207.5 12.3 %copy-start.40 = (bf16[1,384,768]{2,1,0:T(8,128)(2,1)S(1)}, bf16[1,384,768]{2,1,0:T(8,128)(2,1)}, u32[]{:S(2)}) copy-start(bf16[1,384,768]{2,1,0:T(8,128)(2,1)} %param.26) | copy-start | bytes 1769476
  221.6 9.3 %copy-start.29 = (f32[384,768]{1,0:T(8,128)}, f32[384,768]{1,0:T(8,128)S(1)}, u32[]{:S(2)}) copy-start(f32[384,768]{1,0:T(8,128)S(1)} %get-tuple-element.257) | copy-start | bytes 3538948
  222.4 8.4 %slice-start = ((s8[4718592]{0:T(1024)(128)(4,1)}), s8[4194304]{0:T(1024)(128)(4,1)S(1)}, s32[]{:S(2)}) async-start(s8[4718592]{0:T(1024)(128)(4,1)} %bitcast.288), calls=%async_computation.7 | async-start | bytes 8388608
  222.6 8.3 %copy-start.46 = (bf16[384,768]{1,0:T(8,128)(2,1)}, bf16[384,768]{1,0:T(8,128)(2,1)S(1)}, u32[]{:S(2)}) copy-start(bf16[384,768]{1,0:T(8,128)(2,1)S(1)} %multiply_convert_fusion.4.refs_7_) | copy-start | bytes 1769476
  251.3 56.0 %copy-start.35 = (f32[96,768]{1,0:T(8,128)S(1)}, f32[96,768]{1,0:T(8,128)}, u32[]{:S(2)}) copy-start(f32[96,768]{1,0:T(8,128)} %copy-done.34) | copy-start | bytes 884740
  307.7 19.9 %copy-start.32 = (f32[96,768]{1,0:T(8,128)}, f32[96,768]{1,0:T(8,128)S(1)}, u32[]{:S(2)}) copy-start(f32[96,768]{1,0:T(8,128)S(1)} %get-tuple-element.261) | copy-start | bytes 884740
  321.5 180.4 %reduce-scatter.5.cloned.1.call-start = ((), (), s32[]{:S(2)}) async-start(), calls=%async_computation.6 | async-start | bytes 5013504 | tf_op jit(solution)/shard_map/reduce_scatter | solution.py:1367
  363.1 20.0 %copy-start.27 = (bf16[2,2,2,2,48,1536]{5,4,3,2,1,0:T(8,128)(2,1)S(1)}, bf16[2,2,2,2,48,1536]{5,4,3,2,1,0:T(8,128)(2,1)}, u32[]{:S(2)}) copy-start(bf16[2,2,2,2,48,1536]{5,4,3,2,1,0:T(8,128)(2,1)} %copy-done.25) | copy-start | bytes 7077892
  407.3 71.5 %all-to-all-start = ((bf16[16,96,768]{2,1,0:T(8,128)(2,1)}), bf16[16,96,768]{2,1,0:T(8,128)(2,1)}, u32[]{:S(2)}, u32[]{:S(2)}) async-start(bf16[16,96,768]{2,1,0:T(8,128)(2,1)} %bitcast.302), calls=%async_computation | async-start | bytes 4718592 | tf_op jit(solution)/shard_map/all_to_all | solution.py:1387
  440.2 8.3 %copy-start.86 = (f32[2,2,2,96]{3,2,1,0:T(2,128)S(1)}, f32[2,2,2,96]{3,2,1,0:T(2,128)}, u32[]{:S(2)}) copy-start(f32[2,2,2,96]{3,2,1,0:T(2,128)} %copy-done.85) | copy-start | bytes 9220
  440.3 8.4 %copy-start.111 = (f32[768]{0:T(1024)S(1)}, f32[768]{0:T(1024)}, u32[]{:S(2)}) copy-start(f32[768]{0:T(1024)} %get-tuple-element.212) | copy-start | bytes 9220
  440.3 8.4 %copy-start.97 = (f32[768]{0:T(1024)S(1)}, f32[768]{0:T(1024)}, u32[]{:S(2)}) copy-start(f32[768]{0:T(1024)} %get-tuple-element.216) | copy-start | bytes 9220
  443.4 20.7 %collective-permute-start.1 = (bf16[384,1536]{1,0:T(8,128)(2,1)}, bf16[384,1536]{1,0:T(8,128)(2,1)S(1)}, u32[]{:S(2)}, u32[]{:S(2)}) collective-permute-start(bf16[384,1536]{1,0:T(8,128)(2,1)} %get-tuple-element.241), channel_id=1, source_target_pairs={{0,1},{1,2},{2,3},{3,4},{4,5},{5,6},{6,7},{7,8},{8,9},{9,10},{10,1... | collective-permute-start | bytes 3538952 | tf_op jit(solution)/shard_map/ppermute | solution.py:1430
  446.9 17.2 %collective-permute-start = (bf16[384,1536]{1,0:T(8,128)(2,1)}, bf16[384,1536]{1,0:T(8,128)(2,1)}, u32[]{:S(2)}, u32[]{:S(2)}) collective-permute-start(bf16[384,1536]{1,0:T(8,128)(2,1)} %get-tuple-element.240), channel_id=1, source_target_pairs={{1,0},{2,1},{3,2},{4,3},{5,4},{6,5},{7,6},{8,7},{9,8},{10,9},{11,1... | collective-permute-start | bytes 3538952 | tf_op jit(solution)/shard_map/ppermute | solution.py:1429
  501.9 155.3 %copy-start.116 = (f32[96]{0:T(128)S(1)}, f32[96]{0:T(128)}, u32[]{:S(2)}) copy-start(f32[96]{0:T(128)} %copy-done.115) | copy-start | bytes 1156
  (107 other events, 350.2 us)
Sparse Core Ops, SparseCore 0:
  195.3 54.3 all-gather.2
  252.0 61.2 all-gather.4
  321.6 73.5 reduce-scatter.2
  399.4 102.4 reduce-scatter.4

commit v4 on v3

--- a/solution.py
+++ b/solution.py
@@ -203,6 +203,7 @@
 def attend_back_kernel(
     causal,
     with_bias,
+    parts,
     spans_ref,
     q_ref,
     k_ref,
@@ -211,13 +212,13 @@
     key_ref,
     do_ref,
     stat_ref,
-    dot_ref,
+    given_ref,
     *rest,
 ):
     if with_bias:
-        bias_ref, dq_ref, dkv_ref, dbias_ref, dqt_ref, dk_acc, dv_acc = rest
+        bias_ref, dq_ref, *dkv_refs, dbias_ref, dot_ref, dqt_ref, dk_acc, dv_acc = rest
     else:
-        dq_ref, dkv_ref, dqt_ref, dk_acc, dv_acc = rest
+        dq_ref, *dkv_refs, dot_ref, dqt_ref, dk_acc, dv_acc = rest
     block = pl.program_id(0)
 
     @pl.when(block == 0)
@@ -227,6 +228,20 @@
         if with_bias:
             dbias_ref[...] = jnp.zeros_like(dbias_ref)
 
+    if given_ref.shape == dot_ref.shape:
+        dot_ref[...] = given_ref[...]
+    else:
+        product = do_ref[...].astype(f32) * given_ref[...].astype(f32)
+        head_at = lax.broadcasted_iota(jnp.int32, (STATS, D), 0)
+        column_at = lax.broadcasted_iota(jnp.int32, (STATS, D), 1)
+        chosen = (column_at // HD == head_at).astype(f32)
+        dot_ref[...] = lax.dot_general(
+            chosen,
+            product,
+            (((1,), (1,)), ((), ())),
+            precision=PRECISE,
+            preferred_element_type=f32,
+        )
     dqt_ref[...] = jnp.zeros_like(dqt_ref)
     row_mark = row_ref[0]
     scale = jnp.asarray(0.125, bf16)
@@ -278,12 +293,28 @@
 
     @pl.when(block == pl.num_programs(0) - 1)
     def finish():
-        dkv_ref[:, :D] = dk_acc[...].astype(dkv_ref.dtype)
-        dkv_ref[:, D:] = dv_acc[...].astype(dkv_ref.dtype)
+        for n, dkv_ref in enumerate(dkv_refs):
+            rows = slice(n * dkv_ref.shape[0], (n + 1) * dkv_ref.shape[0])
+            dkv_ref[:, :D] = dk_acc[rows, :].astype(dkv_ref.dtype)
+            dkv_ref[:, D:] = dv_acc[rows, :].astype(dkv_ref.dtype)
 
 
 def attend_back(
-    q_src, q_col, kv_src, k_col, v_col, row_mark, key_mark, spans, bias, rows, causal, do, stat, dot
+    q_src,
+    q_col,
+    kv_src,
+    k_col,
+    v_col,
+    row_mark,
+    key_mark,
+    spans,
+    bias,
+    rows,
+    causal,
+    do,
+    stat,
+    given,
+    parts=1,
 ):
     count = q_src.shape[0]
     blocks = count // rows
@@ -296,31 +327,35 @@
         pl.BlockSpec((span, 1), lambda i, s: (0, 0)),
         pl.BlockSpec((rows, D), lambda i, s: (i, 0)),
         pl.BlockSpec((STATS, rows), lambda i, s: (0, i)),
-        pl.BlockSpec((STATS, rows), lambda i, s: (0, i)),
     ]
+    if given.shape == stat.shape:
+        specs.append(pl.BlockSpec((STATS, rows), lambda i, s: (0, i)))
+    else:
+        specs.append(pl.BlockSpec((rows, D), lambda i, s: (i, 0)))
     operands = [q_src, kv_src, kv_src, row_mark.reshape(blocks, 1, rows), key_mark[:, None]]
-    operands += [do, stat, dot]
+    operands += [do, stat, given]
     out_specs = [
         pl.BlockSpec((rows, D), lambda i, s: (i, 0)),
-        pl.BlockSpec((span, 2 * D), lambda i, s: (0, 0)),
     ]
+    out_specs += [pl.BlockSpec((span // parts, 2 * D), lambda i, s: (0, 0))] * parts
     out_shape = [
         jax.ShapeDtypeStruct((count, D), bf16),
-        jax.ShapeDtypeStruct((span, 2 * D), bf16),
     ]
+    out_shape += [jax.ShapeDtypeStruct((span // parts, 2 * D), bf16)] * parts
     if bias is not None:
         specs.append(pl.BlockSpec(bias.shape, lambda i, s: (0, 0, 0)))
         operands.append(bias)
         out_specs.append(pl.BlockSpec(bias.shape, lambda i, s: (0, 0, 0)))
         out_shape.append(jax.ShapeDtypeStruct(bias.shape, f32))
     return pl.pallas_call(
-        functools.partial(attend_back_kernel, causal, bias is not None),
+        functools.partial(attend_back_kernel, causal, bias is not None, parts),
         grid_spec=pltpu.PrefetchScalarGridSpec(
             num_scalar_prefetch=1,
             grid=(blocks,),
             in_specs=specs,
             out_specs=out_specs,
             scratch_shapes=[
+                pltpu.VMEM((STATS, rows), f32),
                 pltpu.VMEM((D, rows), f32),
                 pltpu.VMEM((span, D), f32),
                 pltpu.VMEM((span, D), f32),
@@ -350,6 +385,15 @@
 )
 SPREAD_SHARES = (0.39, 0.39, 0.11, 0.11)
 SPREAD_LAGS = (-6, 0, 4, 8, 14)
+SPREAD_STAGES = (-1000, 0, 100, 200, 300)
+
+
+LATE = ((0, 0, 0, 0, FF // 2),) + tuple((1, 48 * n, 48, D * n, D // 2) for n in range(4))
+
+
+EARLY = 128
+LATE_SUMS = LATE[:1] + tuple((1, 48 * n, 0, FF + 2 * EARLY * n, EARLY) for n in range(4))
+LATE_WIDE = FF + 8 * EARLY
 
 
 def chunks_of(shapes):
@@ -422,15 +466,18 @@
         pl.semaphore_wait(barrier, len(EVERYONE))
 
 
-def spread_kernel(plan, count, late, near, *refs):
+def spread_kernel(plan, count, late, near, banded, *refs):
     shards = refs[:count]
     late_shards = refs[count : count + late]
     near_own = refs[count + late] if near else None
-    refs = refs[count + late + near :]
+    table = refs[count + late + near] if banded else None
+    refs = refs[count + late + near + banded :]
     wholes = refs[:count]
-    late_rows = refs[count : count + late]
-    near_all = refs[count + late] if near else None
-    send_sem, recv_sem, own_sem = refs[count + late + near :]
+    packs = 1 if late else 0
+    late_rows = refs[count : count + packs]
+    near_all = refs[count + packs] if near else None
+    band = refs[count + packs + near] if banded else None
+    send_sem, recv_sem, own_sem, *band_bucket = refs[count + packs + near + banded :]
     bit_of, partner = position()
     meet(partner, bool(near))
 
@@ -479,22 +526,28 @@
         held = region(item, order[: stage - 1], order[stage - 1])
         return remote(held, held, item, 4 + stage, CORE)
 
+    pieces = LATE if late else ()
+
     def late_part(item):
-        half = late_shards[item].shape[1]
-        lanes = pl.ds(pl.multiple_of(bit_of(COLUMN) * half, 128), half)
-        return late_rows[item].at[:, lanes]
+        array, row, to_row, to_column, half = LATE[item]
+        lanes = pl.ds(pl.multiple_of(to_column + bit_of(COLUMN) * half, 128), half)
+        return late_rows[0].at[pl.ds(to_row, 48), lanes]
+
+    def late_shard(item):
+        return late_shards[LATE[item][0]].at[pl.ds(LATE[item][1], 48)]
 
     def late_own(item):
         return pltpu.make_async_copy(
-            late_shards[item], late_part(item), own_sem.at[len(plan) + item]
+            late_shard(item), late_part(item), own_sem.at[len(plan) + item]
         )
 
     def late_copy(item):
-        return remote(late_shards[item], late_part(item), len(plan) + item, 0, COLUMN)
+        return remote(late_shard(item), late_part(item), len(plan) + item, 0, COLUMN)
 
     dp = lax.axis_index("dp")
     seq = lax.axis_index("seq")
-    marks = len(plan) + late
+    marks = len(plan) + len(pieces)
+    lags = SPREAD_STAGES if near else SPREAD_LAGS
 
     def near_copy(step):
         return pltpu.make_async_remote_copy(
@@ -518,20 +571,38 @@
             def send(step=step):
                 near_copy(step).start()
 
-    for item in range(late):
+    for item in range(len(pieces)):
         late_own(item).start()
         late_copy(item).start()
+    if banded:
+        shape = (3 * KEYS, KEYS)
+        key_at = lax.broadcasted_iota(jnp.int32, shape, 0) - KEYS
+        band_bucket[0][...] = bucket_of(key_at - lax.broadcasted_iota(jnp.int32, shape, 1))
+
+    def band_of(head):
+        def body(i, values):
+            return jnp.where(band_bucket[0][...] == i, table[i, head], values)
+
+        values = lax.fori_loop(0, BUCKETS, body, jnp.zeros((3 * KEYS, KEYS), f32))
+        band[head, KEYS : 4 * KEYS, :] = values
+        band[head, :KEYS, :] = jnp.full((KEYS, KEYS), table[BUCKETS // 2 - 1, head], f32)
+        band[head, 4 * KEYS :, :] = jnp.full((KEYS, KEYS), table[BUCKETS - 1, head], f32)
+
     events = sorted(
-        (item + SPREAD_LAGS[stage + 1], stage, item)
+        (item + lags[stage + 1], stage, item)
         for item in range(len(plan))
         for stage in range(-1, len(plan[item][5]))
     )
-    for unused, stage, item in events:
+    heads_done = 0
+    for turn, (unused, stage, item) in enumerate(events):
         if stage < 0:
             stage_copy(item, 0).start()
             own_copy(item).start()
             core_copy(item, 0).start()
             continue
+        if banded and turn % 2 and heads_done < HEADS:
+            band_of(heads_done)
+            heads_done += 1
         if stage == 0:
             own_copy(item).wait()
         stage_copy(item, stage).wait_recv()
@@ -543,7 +614,10 @@
             stage_copy(item, stage).wait_send()
             core_copy(item, stage).wait()
         core_copy(item, len(plan[item][5])).wait()
-    for item in range(late):
+    if banded:
+        for head in range(heads_done, HEADS):
+            band_of(head)
+    for item in range(len(pieces)):
         late_own(item).wait()
         late_copy(item).wait()
     if near:
@@ -556,11 +630,12 @@
                 near_copy(-step).wait_recv()
 
 
-def spread(shards, late, rows, row_orders, near, collective_id):
+def spread(shards, late, rows, row_orders, near, table, collective_id):
     shapes = [(shard.shape[0], 2 * shard.shape[1]) for shard in shards]
-    late_shapes = [(shard.shape[0], 2 * shard.shape[1]) for shard in late]
+    late_shapes = [(2 * 48, FF)] if late else []
     more = [] if near is None else [near]
-    marks = len(late) + len(more)
+    tables = [] if table is None else [table]
+    marks = len(LATE) + len(more)
     plan = ordered(chunks_of(shapes), SPREAD, SPREAD_SHARES)
     if rows is not None:
         count, columns = rows.shape
@@ -574,19 +649,25 @@
         leads[-1] = len(row_orders[0]) + 1
     space = pl.BlockSpec(memory_space=pl.ANY)
     results = pl.pallas_call(
-        functools.partial(spread_kernel, plan, len(shards), len(late), len(more)),
-        in_specs=[space] * (len(shards) + marks),
-        out_specs=[space] * (len(shards) + marks),
+        functools.partial(
+            spread_kernel, plan, len(shards), len(late), len(more), len(tables)
+        ),
+        in_specs=[space] * (len(shards) + len(late) + len(more))
+        + [pl.BlockSpec(memory_space=pltpu.SMEM) for table in tables],
+        out_specs=[space] * (len(shards) + len(late_shapes) + len(more))
+        + [pl.BlockSpec(memory_space=pltpu.VMEM) for table in tables],
         out_shape=[
             jax.ShapeDtypeStruct((2,) * lead + shape, bf16) for lead, shape in zip(leads, shapes)
         ]
         + [jax.ShapeDtypeStruct(shape, bf16) for shape in late_shapes]
-        + [jax.ShapeDtypeStruct((3,) + block.shape, bf16) for block in more],
+        + [jax.ShapeDtypeStruct((3,) + block.shape, bf16) for block in more]
+        + [jax.ShapeDtypeStruct((HEADS, 5 * KEYS, KEYS), f32) for table in tables],
         scratch_shapes=[
             pltpu.SemaphoreType.DMA((len(plan) + marks, 9)),
             pltpu.SemaphoreType.DMA((len(plan) + marks, 9)),
             pltpu.SemaphoreType.DMA((len(plan) + marks,)),
-        ],
+        ]
+        + [pltpu.VMEM((3 * KEYS, KEYS), jnp.int32) for table in tables],
         compiler_params=pltpu.CompilerParams(
             collective_id=collective_id, has_side_effects=True, vmem_limit_bytes=16 * 1024 * 1024
         ),
@@ -596,7 +677,7 @@
             transcendentals=0,
         ),
         name="spread",
-    )(*shards, *late, *more)
+    )(*shards, *late, *more, *tables)
     return [
         result.reshape((1 << lead) * shape[0], shape[1])
         for result, lead, shape in zip(results, leads, shapes)
@@ -657,20 +738,20 @@
     return (2,) * len(left) + (chunk[2], width)
 
 
-def reduce_kernel(plan, count, late, *refs):
+def reduce_kernel(plan, count, *refs):
     lefts = refs[:count]
     rights = refs[count : 2 * count]
-    late_rows = refs[2 * count : 2 * count + late]
-    small_in, rows_in = refs[2 * count + late : 2 * count + late + 2]
-    refs = refs[2 * count + late + 2 :]
+    late_rows, small_in, rows_in = refs[2 * count : 2 * count + 3]
+    refs = refs[2 * count + 3 :]
     outs = refs[:count]
-    late_outs = refs[count : count + late]
-    small_out, rows_out = refs[count + late : count + late + 2]
-    scratch = list(refs[count + late + 2 :])
+    late_outs = refs[count : count + 2]
+    small_out, rows_out = refs[count + 2 : count + 4]
+    scratch = list(refs[count + 4 :])
+    late = len(LATE_SUMS)
     send_sem, recv_sem, small_acc, small_recv, ring_low, ring_tall = scratch[:6]
     rows_held = [rows_in] + scratch[6:9]
-    late_recv = scratch[9 : 9 + late]
-    scratch = scratch[9 + late :]
+    late_recv = scratch[9]
+    scratch = scratch[10:]
     held = [scratch[5 * i : 5 * i + 5] for i in range(len(plan))]
     turns = []
     for item, chunk in enumerate(plan):
@@ -797,14 +878,18 @@
         else:
             lax.fori_loop(0, 1 << (2 - stage), body, 0)
 
-    def late_lanes(item, mine):
-        half = late_recv[item].shape[1]
+    def late_part(item, mine):
+        array, row, to_row, to_column, half = LATE_SUMS[item]
         bit = bit_of(COLUMN) if mine else 1 - bit_of(COLUMN)
-        return pl.ds(pl.multiple_of(bit * half, 128), half)
+        lanes = pl.ds(pl.multiple_of(to_column + bit * half, 128), half)
+        return late_rows.at[pl.ds(to_row, 48), lanes]
+
+    def late_came(item):
+        array, row, to_row, to_column, half = LATE_SUMS[item]
+        return late_recv.at[pl.ds(to_row, 48), pl.ds(to_column // 2, half)]
 
     def late_copy(item):
-        block = late_rows[item].at[:, late_lanes(item, False)]
-        return remote(block, late_recv[item], len(plan) + 1 + item, 0, COLUMN)
+        return remote(late_part(item, False), late_came(item), len(plan) + 1 + item, 0, COLUMN)
 
     small_copy(0).start()
     rows_copy(0).start()
@@ -842,9 +927,10 @@
                 small_out[...] = summed
     for item in range(late):
         late_copy(item).wait()
-        late_outs[item][...] = late_rows[item][:, late_lanes(item, True)].astype(
+        array, row = LATE_SUMS[item][:2]
+        late_outs[array][row : row + 48, :] = late_part(item, True)[...].astype(
             f32
-        ) + late_recv[item][...].astype(f32)
+        ) + late_came(item)[...].astype(f32)
     for item in range(len(plan)):
         same = [other for other in plan[item:] if other[2] == plan[item][2]]
         if len(same) <= RING:
@@ -859,8 +945,8 @@
     shapes = [(left.shape[1] // 16, right.shape[1]) for left, right in factors]
     plan = reduce_plan(shapes)
     scratch = [
-        pltpu.SemaphoreType.DMA((len(plan) + 2 + len(late), 5)),
-        pltpu.SemaphoreType.DMA((len(plan) + 2 + len(late), 5)),
+        pltpu.SemaphoreType.DMA((len(plan) + 2 + len(LATE_SUMS), 5)),
+        pltpu.SemaphoreType.DMA((len(plan) + 2 + len(LATE_SUMS), 5)),
         pltpu.VMEM((4, SMALL, D), f32),
         pltpu.VMEM((5, SMALL, D), f32),
         pltpu.VMEM((RING, 2, 2, 2, 2, 48, D), bf16),
@@ -868,16 +954,16 @@
     ]
     own_rows = rows.shape[0] // 8
     scratch += [pltpu.VMEM((2,) * n + (own_rows, D), bf16) for n in (2, 1, 0)]
-    late_shapes = [(rows.shape[0], rows.shape[1] // 2) for rows in late]
-    scratch += [pltpu.VMEM(shape, bf16) for shape in late_shapes]
+    late_shapes = [(48, FF // 2), (4 * 48, EARLY)]
+    scratch.append(pltpu.VMEM((48, LATE_WIDE // 2), bf16))
     for chunk in plan:
         shapes_held = stage_shapes(chunk)
         scratch += [pltpu.VMEM(buffer_shape(chunk, h), bf16) for h in shapes_held]
     near = pl.BlockSpec(memory_space=pltpu.VMEM)
     results = pl.pallas_call(
-        functools.partial(reduce_kernel, plan, len(factors), len(late)),
-        in_specs=[near] * (2 * len(factors) + len(late) + 2),
-        out_specs=[near] * (len(factors) + len(late) + 2),
+        functools.partial(reduce_kernel, plan, len(factors)),
+        in_specs=[near] * (2 * len(factors) + 3),
+        out_specs=[near] * (len(factors) + 4),
         out_shape=[jax.ShapeDtypeStruct((rows, columns // 2), f32) for rows, columns in shapes]
         + [jax.ShapeDtypeStruct(shape, f32) for shape in late_shapes]
         + [jax.ShapeDtypeStruct((SMALL, D), f32), jax.ShapeDtypeStruct((own_rows, D), f32)],
@@ -886,7 +972,7 @@
             collective_id=1, has_side_effects=True, vmem_limit_bytes=60 * 1024 * 1024
         ),
         name="reduce_all",
-    )(*lefts, *rights, *late, small, rows.reshape(2, 2, 2, own_rows, D))
+    )(*lefts, *rights, late, small, rows.reshape(2, 2, 2, own_rows, D))
     return results[: len(factors)], results[len(factors) : -2], results[-2], results[-1]
 
 
@@ -999,6 +1085,61 @@
                 copy.wait_send()
 
 
+def pair_kernel(half_ref, broad_ref, tall_ref, late_send, late_recv, late_own):
+    bit_of, partner = position()
+    barrier = pltpu.get_barrier_semaphore()
+    pl.semaphore_signal(
+        barrier, inc=1, device_id=partner(CORE), device_id_type=pl.DeviceIdType.MESH
+    )
+    pl.semaphore_wait(barrier, 1)
+    wholes = (broad_ref, tall_ref)
+
+    def late_ends(item):
+        array, row, from_row, column, half = LATE[item]
+        source = half_ref.at[:, pl.ds(from_row, 48), pl.ds(column, 2 * half)]
+        return source, wholes[array].at[:, bit_of(CORE), pl.ds(row, 48)]
+
+    def late_mine(item):
+        return pltpu.make_async_copy(*late_ends(item), late_own.at[item])
+
+    def late_copy(item):
+        source, target = late_ends(item)
+        return pltpu.make_async_remote_copy(
+            src_ref=source,
+            dst_ref=target,
+            send_sem=late_send.at[item],
+            recv_sem=late_recv.at[item],
+            device_id=partner(CORE),
+            device_id_type=pl.DeviceIdType.MESH,
+        )
+
+    for item in range(len(LATE)):
+        late_copy(item).start()
+        late_mine(item).start()
+    for item in range(len(LATE)):
+        late_copy(item).wait()
+        late_mine(item).wait()
+
+
+def pair_all(late):
+    space = pl.BlockSpec(memory_space=pl.ANY)
+    broad, tall = pl.pallas_call(
+        pair_kernel,
+        in_specs=[space],
+        out_specs=[space, space],
+        out_shape=[
+            jax.ShapeDtypeStruct((8, 2, 48, FF), bf16),
+            jax.ShapeDtypeStruct((8, 2, 4 * 48, D), bf16),
+        ],
+        scratch_shapes=[pltpu.SemaphoreType.DMA((len(LATE),))] * 3,
+        compiler_params=pltpu.CompilerParams(
+            collective_id=6, has_side_effects=True, vmem_limit_bytes=16 * 1024 * 1024
+        ),
+        name="pair_all",
+    )(late.reshape(8, 2 * 48, FF))
+    return broad.reshape(D, FF), tall.reshape(FF, D)
+
+
 def merge_all(mix, stat):
     rows = mix.shape[0] // 16
     near = pl.BlockSpec(memory_space=pltpu.VMEM)
@@ -1010,8 +1151,8 @@
             scratch.append(pltpu.VMEM(lead + (HALF_STATS, rows), f32))
     return pl.pallas_call(
         merge_kernel,
-        in_specs=[near] * 2,
-        out_specs=[near] * 2,
+        in_specs=[near, near],
+        out_specs=[near, near],
         out_shape=[
             jax.ShapeDtypeStruct((rows, D), f32),
             jax.ShapeDtypeStruct((2, HALF_STATS, rows), f32),
@@ -1021,13 +1162,18 @@
             collective_id=4, has_side_effects=True, vmem_limit_bytes=32 * 1024 * 1024
         ),
         name="merge_all",
-    )(mix.reshape(2, 2, 2, 2, rows, D), stat.reshape(2, 2, 2, 2, 2, HALF_STATS, rows))
+    )(
+        mix.reshape(2, 2, 2, 2, rows, D),
+        stat.reshape(2, 2, 2, 2, 2, HALF_STATS, rows),
+    )
 
 
 def share_kernel(orders, axes, kinds, *refs):
     sources = refs[:kinds]
-    outs = refs[kinds : 2 * kinds]
-    send_sem, recv_sem, own_sem = refs[2 * kinds :]
+    late_left, late_right, tall_left, tall_right = refs[kinds : kinds + 4]
+    refs = refs[kinds + 4 :]
+    outs = refs[:kinds]
+    late_out, send_sem, recv_sem, own_sem, late_send, late_recv, full, got = refs[kinds:]
     bit_of, partner = position()
     meet(partner)
     depth = len(orders[0])
@@ -1079,10 +1225,53 @@
             for kind, (source, target) in enumerate(zip(part(item), region(item, ())))
         ]
 
+    def produce(kind):
+        def tall(i, unused):
+            left = tall_left[:, pl.ds(pl.multiple_of(i * 8 * 48, 128), 8 * 48)]
+            grad = dot_tn(left, tall_right[...]).astype(bf16).reshape(2, 4, 48, 2 * EARLY)
+            for n in range(4):
+                first = FF + 2 * EARLY * n
+                full[i, :, :, first : first + 2 * EARLY] = grad[:, n]
+            return 0
+
+        def body(i, unused):
+            left = late_left[:, pl.ds(pl.multiple_of(i * 8 * 48, 128), 8 * 48)]
+            for n in range(4):
+                lanes = slice(n * D, (n + 1) * D)
+                grad = dot_tn(left, late_right[:, lanes]).astype(bf16)
+                full[pl.ds(4 * i, 4), :, :, lanes] = grad.reshape(4, 2, 48, D)
+            return 0
+
+        if kind == 0:
+            lax.fori_loop(0, 2, body, 0)
+        else:
+            lax.fori_loop(0, 8, tall, 0)
+
+    def late_copy(kind):
+        lanes = (pl.ds(0, FF), pl.ds(FF, LATE_WIDE - FF))[kind]
+        return pltpu.make_async_remote_copy(
+            src_ref=full.at[:, 1 - bit_of(CORE), :, lanes],
+            dst_ref=got.at[:, :, lanes],
+            send_sem=late_send.at[kind],
+            recv_sem=late_recv.at[kind],
+            device_id=partner(CORE),
+            device_id_type=pl.DeviceIdType.MESH,
+        )
+
+    def late_add():
+        def body(i, unused):
+            late_out[i] = full[i, bit_of(CORE)] + got[i]
+            return 0
+
+        lax.fori_loop(0, 8, body, 0)
+
     for item in range(2):
         for copy in stage_copies(item, 0) + core_copies(item, 0) + own_copies(item):
             copy.start()
     for stage in range(depth):
+        if stage < 2:
+            produce(stage)
+            late_copy(stage).start()
         for item in range(2):
             if stage == 0:
                 for copy in own_copies(item):
@@ -1101,9 +1290,12 @@
         for stage in range(depth + 1):
             for copy in core_copies(item, stage):
                 copy.wait()
-
-
-def share_all(arrays, orders, collective_id):
+    late_copy(0).wait()
+    late_copy(1).wait()
+    late_add()
+
+
+def share_all(arrays, factors, orders, collective_id):
     kinds = len(arrays)
     near = pl.BlockSpec(memory_space=pltpu.VMEM)
     axes = tuple(axis for axis in SLOT_AXES if axis == CORE or axis in orders[0])
@@ -1111,16 +1303,26 @@
     lead = (2,) * len(axes)
     outs = pl.pallas_call(
         functools.partial(share_kernel, orders, axes, kinds),
-        in_specs=[near] * kinds,
-        out_specs=[near] * kinds,
-        out_shape=[jax.ShapeDtypeStruct(lead + array.shape, array.dtype) for array in arrays],
-        scratch_shapes=[sems, sems, pltpu.SemaphoreType.DMA((2, 2))],
+        in_specs=[near] * (kinds + 4),
+        out_specs=[near] * (kinds + 1),
+        out_shape=[jax.ShapeDtypeStruct(lead + array.shape, array.dtype) for array in arrays]
+        + [jax.ShapeDtypeStruct((8, 48, LATE_WIDE), bf16)],
+        scratch_shapes=[
+            sems,
+            sems,
+            pltpu.SemaphoreType.DMA((2, 2)),
+            pltpu.SemaphoreType.DMA((2,)),
+            pltpu.SemaphoreType.DMA((2,)),
+            pltpu.VMEM((8, 2, 48, LATE_WIDE), bf16),
+            pltpu.VMEM((8, 48, LATE_WIDE), bf16),
+        ],
         compiler_params=pltpu.CompilerParams(
-            collective_id=collective_id, has_side_effects=True, vmem_limit_bytes=32 * 1024 * 1024
+            collective_id=collective_id, has_side_effects=True, vmem_limit_bytes=48 * 1024 * 1024
         ),
         name="share_all",
-    )(*arrays)
-    return [out.reshape((1 << len(axes),) + array.shape) for out, array in zip(outs, arrays)]
+    )(*arrays, *factors[0], *factors[1])
+    shared = [out.reshape((1 << len(axes),) + array.shape) for out, array in zip(outs, arrays)]
+    return shared, outs[-1].reshape(8 * 48, LATE_WIDE)
 
 
 def halves_of(stat):
@@ -1215,12 +1417,12 @@
         return shard
 
 
-    def gathered(masters, late, rows, row_groups, near, collective_id):
+    def gathered(masters, late, rows, row_groups, near, table, collective_id):
         shards = [flat(master) for master in masters]
         late = [flat(master) for master in late]
         if here:
             row_orders = SHARE if row_groups is None else GROUP_SHARE
-            return spread(shards, late, rows, row_orders, near, collective_id)
+            return spread(shards, late, rows, row_orders, near, table, collective_id)
         weights, late = spread_plainly(shards, late)
         if rows is not None:
             weights.append(
@@ -1231,14 +1433,28 @@
             low = lax.ppermute(near[row_count - PASS :], "seq", forward)
             high = lax.ppermute(near[:PASS], "seq", [(i + 1, i) for i in range(seq_count - 1)])
             late.append(jnp.concatenate([low, near, high], axis=0))
+        if table is not None:
+            late.append(
+                lax.dot_general(
+                    table,
+                    band_onehot,
+                    (((0,), (0,)), ((), ())),
+                    precision=PRECISE,
+                    preferred_element_type=f32,
+                ).reshape(HEADS, 5 * KEYS, KEYS)
+            )
         return weights, late
 
-    weights, unused = gathered(
+    band_onehot = (
+        jnp.arange(BUCKETS, dtype=jnp.int32)[:, None] == bias_bands()[None, :]
+    ).astype(f32)
+    weights, (band,) = gathered(
         (self_qkv[1:], self_qkv[0], enc_qkv, self_out, cross_qkv[0]),
         (),
         dec_input[0],
         groups,
         None,
+        rel_table,
         2,
     )
     self_kv_w, self_q_w, enc_qkv_w, self_out_w, cross_q_w, group_input = weights
@@ -1262,15 +1478,6 @@
         jnp.where(key_ids[None, :] == enc_blocks[:, KEYS - 1 :], places[None, :], 0), axis=1
     )
     enc_spans = jnp.stack([low_at // KEYS, high_at // KEYS + 1], axis=1).reshape(-1)
-
-    band_bucket = bias_bands()
-    band_onehot = (
-        jnp.arange(BUCKETS, dtype=jnp.int32)[:, None] == band_bucket[None, :]
-    ).astype(f32)
-    band = lax.dot_general(
-        rel_table, band_onehot, (((0,), (0,)), ((), ())), precision=PRECISE,
-        preferred_element_type=f32,
-    ).reshape(HEADS, 5 * KEYS, KEYS)
 
     dec_tokens = dec_input[0].astype(f32)
     dec_total = dec_rows * seq_count
@@ -1304,13 +1511,20 @@
         cross_queries,
         None,
         enc_proj[:, D:],
+        None,
         3,
     )
     enc_out_w, cross_kv_w, enc_up_w, enc_down_w, cross_out_w, all_queries = weights
-    enc_near = late_rows[2].reshape(key_span, 2 * D)
-    dec_up_w, dec_down_w = [
-        lax.all_gather(rows, "seq", axis=0, tiled=True) for rows in late_rows[:2]
-    ]
+    enc_near = late_rows[-1].reshape(key_span, 2 * D)
+    parities = [list(range(core, seq_count, 2)) for core in range(2)]
+    if here:
+        late_half = lax.all_gather(
+            late_rows[0], "seq", axis=0, tiled=True, axis_index_groups=parities
+        )
+    else:
+        dec_up_w, dec_down_w = [
+            lax.all_gather(rows, "seq", axis=0, tiled=True) for rows in late_rows[:2]
+        ]
     forward = [(i, i + 1) for i in range(seq_count - 1)]
     backward = [(i + 1, i) for i in range(seq_count - 1)]
     enc_args = (enc_proj, 0, enc_near, 0, 1, row_ids, key_ids, enc_spans, band)
@@ -1319,6 +1533,7 @@
     normed_two = norm_apply(enc_hidden, enc_gains_w[1]).astype(bf16)
     enc_inner = matmul(normed_two, enc_up_w)
     enc_active = jax.nn.gelu(enc_inner).astype(bf16)
+    enc_slope = lax.optimization_barrier(gelu_back(enc_inner, jnp.ones_like(enc_inner)))
     encoded_b = (enc_hidden + matmul(enc_active, enc_down_w)).astype(bf16)
     cross_kv = matmul(encoded_b, cross_kv_w).astype(bf16)
 
@@ -1340,6 +1555,8 @@
     if here:
         stat_slots = halves_of(part_stat).reshape(2, HALF_STATS, seq_count, dec_rows)
         cross_mix, cross_stat = merge_all(part_mix, stat_slots.transpose(2, 0, 1, 3))
+        cross_mix, late_half = lax.optimization_barrier((cross_mix, late_half))
+        dec_up_w, dec_down_w = pair_all(late_half)
         cross_stat = heads_from(cross_stat)
     else:
         came_mix = lax.all_to_all(part_mix, "seq", 0, 0, tiled=True)
@@ -1355,28 +1572,39 @@
 
     grad_final = cotangent[0].astype(f32) * valid_rows
     grad_final_b = grad_final.astype(bf16)
-    grad_dec_down = grad_of(dec_active, grad_final_b)
     grad_dec_inner = gelu_back(dec_inner, back_of(grad_final_b, dec_down_w)).astype(bf16)
-    grad_dec_up = grad_of(dec_normed_three, grad_dec_inner)
     grad_hidden_two, grad_gain_three = norm_back(
         dec_hidden_two, dec_gains_w[2], back_of(grad_dec_inner, dec_up_w)
     )
     grad_hidden_two = grad_hidden_two + grad_final
     grad_cross_b = grad_hidden_two.astype(bf16)
-    late = [
-        lax.psum_scatter(grad.astype(bf16), "seq", scatter_dimension=0, tiled=True)
-        for grad in (grad_dec_up, grad_dec_down)
-    ]
+    late_factor = (dec_normed_three, grad_dec_inner)
+
+    def columns_of(first, last):
+        halves = [grad_final_b[:, first:last], grad_final_b[:, wide + first : wide + last]]
+        return jnp.concatenate(halves, axis=1)
+
     grad_cross_mix = back_of(grad_cross_b, cross_out_w).astype(bf16)
     cross_dot = per_head_dot(grad_cross_mix, cross_mix)
     if here:
         both = jnp.concatenate([halves_of(cross_stat), halves_of(cross_dot)], axis=1)
-        all_grads, all_stats = share_all((grad_cross_mix, both), SHARE, 5)
+        (all_grads, all_stats), late = share_all(
+            (grad_cross_mix, both),
+            (late_factor, (dec_active, columns_of(0, EARLY))),
+            SHARE,
+            5,
+        )
+        late = lax.psum_scatter(
+            late, "seq", scatter_dimension=0, tiled=True, axis_index_groups=parities
+        )
         all_grads = all_grads.reshape(dec_total, D)
         all_stats = all_stats.reshape(seq_count, 2, 2, HALF_STATS, dec_rows)
         all_stats = heads_from(all_stats.transpose(2, 0, 1, 3, 4)).transpose(0, 2, 1, 3)
         all_stats = all_stats.reshape(2 * STATS, dec_total)
     else:
+        late = lax.psum_scatter(
+            grad_of(*late_factor).astype(bf16), "seq", scatter_dimension=0, tiled=True
+        )
         all_grads = lax.all_gather(grad_cross_mix, "seq", axis=0, tiled=True)
         all_stats = lax.all_gather(
             jnp.concatenate([cross_stat, cross_dot], axis=0).T, "seq", axis=0, tiled=True
@@ -1385,17 +1613,38 @@
         *cross_args, cross_rows, False, all_grads, all_stats[:STATS], all_stats[STATS:]
     )
     came_dq = lax.all_to_all(part_dq, "seq", 0, 0, tiled=True).reshape(seq_count, dec_rows, D)
+    grad_encoded = back_of(cross_kv_grad, cross_kv_w)
+    grad_encoded_b = grad_encoded.astype(bf16)
+    grad_enc_inner = (back_of(grad_encoded_b, enc_down_w) * enc_slope).astype(bf16)
+    grad_enc_hidden, grad_enc_gain_two = norm_back(
+        enc_hidden, enc_gains_w[1], back_of(grad_enc_inner, enc_up_w)
+    )
+    grad_enc_hidden = grad_enc_hidden + grad_encoded
+    grad_attn_b = grad_enc_hidden.astype(bf16)
+    grad_enc_mix = back_of(grad_attn_b, enc_out_w).astype(bf16)
+    enc_dq, low_grad, own_grad, high_grad, grad_band = attend_back(
+        *enc_args, KEYS, False, grad_enc_mix, enc_stat, enc_mixed_b, key_span // PASS
+    )
+    table_part = lax.dot_general(
+        band_onehot,
+        grad_band.reshape(HEADS, -1),
+        (((1,), (1,)), ((), ())),
+        precision=PRECISE,
+        preferred_element_type=f32,
+    )
+    from_higher = lax.ppermute(low_grad, "seq", backward)
+    from_lower = lax.ppermute(high_grad, "seq", forward)
+    own_grad = own_grad.astype(f32) + from_higher.astype(f32) + from_lower.astype(f32)
+    own_grad, came_dq, late = lax.optimization_barrier((own_grad, came_dq, late))
     grad_cross_q_b = jnp.sum(came_dq.astype(f32), axis=0).astype(bf16)
     grad_hidden, grad_gain_two = norm_back(
         dec_hidden, dec_gains_w[1], back_of(grad_cross_q_b, cross_q_w)
     )
     grad_hidden = grad_hidden + grad_hidden_two
-    grad_encoded = back_of(cross_kv_grad, cross_kv_w)
     grad_self_b = grad_hidden.astype(bf16)
     grad_self_mix = back_of(grad_self_b, self_out_w).astype(bf16)
-    self_dot = per_head_dot(grad_self_mix, self_mix_b)
     self_dq, self_dkv = attend_back(
-        *self_args, dec_rows, True, grad_self_mix, self_stat, self_dot
+        *self_args, dec_rows, True, grad_self_mix, self_stat, self_mix_b
     )
     group_scale = lax.rsqrt(jnp.mean(group_tokens * group_tokens, axis=-1, keepdims=True) + EPSILON)
     dec_scale = lax.rsqrt(jnp.mean(dec_tokens * dec_tokens, axis=-1, keepdims=True) + EPSILON)
@@ -1407,30 +1656,6 @@
     grad_group_b = grad_group.astype(bf16)
     grad_dec_gains = jnp.stack([grad_gain_one, grad_gain_two, grad_gain_three])
 
-    grad_encoded_b = grad_encoded.astype(bf16)
-    grad_enc_inner = gelu_back(enc_inner, back_of(grad_encoded_b, enc_down_w)).astype(bf16)
-    grad_enc_hidden, grad_enc_gain_two = norm_back(
-        enc_hidden, enc_gains_w[1], back_of(grad_enc_inner, enc_up_w)
-    )
-    grad_enc_hidden = grad_enc_hidden + grad_encoded
-    grad_attn_b = grad_enc_hidden.astype(bf16)
-    grad_enc_mix = back_of(grad_attn_b, enc_out_w).astype(bf16)
-    enc_dot = per_head_dot(grad_enc_mix, enc_mixed_b)
-    enc_dq, near_grad, grad_band = attend_back(
-        *enc_args, KEYS, False, grad_enc_mix, enc_stat, enc_dot
-    )
-    table_part = lax.dot_general(
-        band_onehot,
-        grad_band.reshape(HEADS, -1),
-        (((1,), (1,)), ((), ())),
-        precision=PRECISE,
-        preferred_element_type=f32,
-    )
-    from_higher = lax.ppermute(near_grad[:PASS], "seq", backward)
-    from_lower = lax.ppermute(near_grad[key_span - PASS :], "seq", forward)
-    own_grad = near_grad[PASS : PASS + row_count].astype(f32)
-    own_grad = own_grad.at[row_count - PASS :].add(from_higher.astype(f32))
-    own_grad = own_grad.at[:PASS].add(from_lower.astype(f32))
     enc_grad_b = jnp.concatenate([enc_dq, own_grad.astype(bf16)], axis=1)
     grad_enc_in, grad_enc_gain_one = norm_back(
         tokens, enc_gains_w[0], back_of(enc_grad_b, enc_qkv_w)
@@ -1448,6 +1673,7 @@
         (normed_two, grad_enc_inner),
         (enc_mixed_b, grad_attn_b),
         (normed_one, enc_grad_b),
+        (dec_active, columns_of(EARLY, wide) if here else grad_final_b),
     )
     gains_part = jnp.concatenate([grad_enc_gains, grad_dec_gains], axis=0)
     if here:
@@ -1459,7 +1685,7 @@
         table_grad = small[5, : BUCKETS * HEADS].reshape(BUCKETS, HEADS)
     else:
         gains_total, table_grad = lax.psum((gains_part, table_part), ("dp", "seq"))
-        sums, late = reduce_plainly([grad_of(*pair).astype(bf16) for pair in factors], late)
+        sums, late = reduce_plainly([grad_of(*pair).astype(bf16) for pair in factors], [late])
         grad_normed = lax.psum_scatter(
             grad_group_b, "seq", scatter_dimension=0, tiled=True, axis_index_groups=groups
         ).astype(f32)
@@ -1485,7 +1711,7 @@
         jnp.concatenate([sums[2][None], threes(sums[1])], axis=0),
         sums[0],
         late[0],
-        late[1],
+        jnp.concatenate([late[1], sums[10]], axis=1) if here else sums[10],
     )
 
 

time: 682 us -> 650 us (0.953)
  matrix products: 89.1 us -> 65.9 us
  waiting for transfers between devices: 11.3 us -> 3.74 us
    dot_general x3 -> x0, matrix products: 10.9 us -> none  [the longest x2 7.38 us: grad_of(): lax.dot_general(left_side, right_side, (((0,), (0,)), ((), ())), preferre...]
    dot_general x12, matrix products: 41.9 us -> 32.1 us  [back_of(): lax.dot_general(gradient, weight, (((1,), (1,)), ((), ())), preferred_ele...]
    pallas_call x2 -> x3, Pallas kernels: 205 us -> 201 us  [the longest x1 149 us: reduce_all(): pl.pallas_call(functools.partial(reduce_kernel, plan, len(factors)), in_s...]
    unnamed x262 -> x271, local copies, waits for them, and re-layouts: 36.8 us -> 40.3 us
  transfers between devices with their start and end apart: 7 -> 5, of which waited for: 3 -> 1; matrix products, arithmetic and copies ran while one was open for 17% -> 9% of each run, Pallas kernels for 23% -> 18%
where the time goes in v4:
time: 650 us; the launch traced here: 641 us
  Pallas kernels  462 us (71%)
  matrix products  65.9 us (10%)
  local copies, waits for them, and re-layouts  57.5 us (9%)
  other arithmetic  25.6 us (4%)
  between operations  16.2 us (2%)
  starting transfers between devices  10.6 us (2%)
    pallas_call x2, Pallas kernels, spread(): pl.pallas_call(functools.partial(spread_kernel, plan, len(shards), len(la...  151 us
    pallas_call x1, Pallas kernels, reduce_all(): pl.pallas_call(functools.partial(reduce_kernel, plan, len(factors)), in_s...  149 us
    pallas_call x3, Pallas kernels, attend_back(): pl.pallas_call(functools.partial(attend_back_kernel, causal, bias is not...  50.4 us
    pallas_call x1, Pallas kernels, merge_all(): pl.pallas_call(merge_kernel, in_specs=[near, near], out_specs=[near, near...  43.5 us
    unnamed x271, local copies, waits for them, and re-layouts  40.3 us
    dot_general x12, matrix products, back_of(): lax.dot_general(gradient, weight, (((1,), (1,)), ((), ())), preferred_ele...  32.1 us
    pallas_call x3, Pallas kernels, attend(): pl.pallas_call(functools.partial(attend_kernel, causal, bias is not None)...  31.5 us
    dot_general x12, matrix products, matmul(): return jnp.dot(left_side, right_side, preferred_element_type=f32)  28.4 us
  transfers between devices with their start and end apart: 5, of which 1 were waited for; matrix products, arithmetic and copies ran while one was open for 9% of the time, Pallas kernels for 18%

profile of v4, /device:TPU:0, one launch (start us, length us, event | category | flops | bytes accessed | tf_op | source)
XLA Modules:
  0.0 641.2 jit_solution(1437111037621226227)
XLA Ops:
  12.3 55.7 %spread.2 = (bf16[2,2,2,2,48,1536]{5,4,3,2,1,0:T(8,128)(2,1)S(1)}, bf16[2,2,2,2,48,768]{5,4,3,2,1,0:T(8,128)(2,1)S(1)}, bf16[2,2,2,2,48,2304]{5,4,3,2,1,0:T(8,12...) custom-call(bf16[48,768]{1,0:T(8,128)(2,1)S(1)} %bitcast.292, ...), custom_call_target="tpu_custom_call" | custom-call | flops 134400000000 | tf_op jit(solution)/shard_map/spread/pallas_call | solution.py:651
  78.8 3.4 convolution_convert_fusion.1.k_ref.v_ref
  83.3 4.5 shard_map.297
  95.1 94.9 %spread.3 = (bf16[2,2,2,2,48,768]{5,4,3,2,1,0:T(8,128)(2,1)S(1)}, bf16[2,2,2,2,48,1536]{5,4,3,2,1,0:T(8,128)(2,1)S(1)}, bf16[2,2,2,2,48,3072]{5,4,3,2,1,0:T(8,12...) custom-call(bf16[48,384]{1,0:T(8,128)(2,1)S(1)} %convert_element_typ, ...), custom_call_target="tpu_custom_call" | custom-call | flops 192000000000 | tf_op jit(solution)/shard_map/spread/pallas_call | solution.py:651
  203.6 13.9 %shard_map.298 = (bf16[384,768]{1,0:T(8,128)(2,1)}, f32[16,384]{1,0:T(8,128)}) custom-call(s32[6]{0:T(128)} %reshape.751.spans_ref, bf16[384,2304]{1,0:T(8,128)(2,1)} %copy-done.36, bf16[1152,1536]{1,0:T(8,128)(2,1)} %bitcast.260, bf16[1152,1536]{1,0:T(8,128)(2,1)} %bitcast.261, s32[3,1,128]{2,1,0:T(1,128)} %get-tuple-element.237.row_ref, ...), custom_call_target="tpu_custom_call" | custom-call | flops 452984832 | bytes 7077888 | tf_op jit(solution)/shard_map/pallas_call | solution.py:176
  221.0 8.9 %fusion.7 = (f32[384,3072]{1,0:T(8,128)}, bf16[384,3072]{1,0:T(8,128)(2,1)S(1)}) fusion(bf16[384,768]{1,0:T(8,128)(2,1)S(1)} %multiply_convert_fusion.5.refs_7_, bf16[768,3072]{1,0:T(8,128)(2,1)} %bitcast.293), kind=kOutput, calls=%fused_computation.10 | convolution fusion | flops 1834352640 | bytes 12386304 | tf_op jit(solution)/shard_map/dot_general | solution.py:63
  234.6 13.1 %shard_map.299 = (bf16[1536,768]{1,0:T(8,128)(2,1)}, f32[16,1536]{1,0:T(8,128)}) custom-call(s32[8]{0:T(128)} %reshape.745.spans_ref, bf16[1536,768]{1,0:T(8,128)(2,1)} %bitcast.266, bf16[384,1536]{1,0:T(8,128)(2,1)} %convolution_convert_fusion.2.k_ref.v_ref, bf16[384,1536]{1,0:T(8,128)(2,1)} %convolution_convert_fusion.2.k_ref.v_ref, ...), custom_call_target="tpu_custom_call" | custom-call | flops 603979776 | bytes 2359296 | tf_op jit(solution)/shard_map/pallas_call | solution.py:176
  250.5 43.5 %merge_all.1 = (f32[96,768]{1,0:T(8,128)S(1)}, f32[2,8,96]{2,1,0:T(8,128)S(1)}) custom-call(bf16[2,2,2,2,96,768]{5,4,3,2,1,0:T(8,128)(2,1)S(1)} %bitcast.284, f32[2,2,2,2,2,8,96]{6,5,4,3,2,1,0:T(8,128)S(1)} %bitcast.288), custom_call_target="tpu_custom_call" | custom-call | tf_op jit(solution)/shard_map/merge_all/pallas_call | solution.py:1152
  297.7 8.0 %pair_all.1 = (bf16[8,2,48,3072]{3,2,1,0:T(8,128)(2,1)S(1)}, bf16[8,2,192,768]{3,2,1,0:T(8,128)(2,1)S(1)}) custom-call(bf16[8,96,3072]{2,1,0:T(8,128)(2,1)S(1)} %bitcast.275), custom_call_target="tpu_custom_call" | custom-call | tf_op jit(solution)/shard_map/pair_all/pallas_call | solution.py:1126
  315.3 28.3 %share_all.1 = (bf16[2,2,2,2,96,768]{5,4,3,2,1,0:T(8,128)(2,1)S(1)}, f32[2,2,2,2,2,16,96]{6,5,4,3,2,1,0:T(8,128)S(1)}, bf16[8,48,4096]{2,1,0:T(8,128)(2,1)}) custom-call(bf16[96,768]{1,0:T(8,128)(2,1)S(1)} %get-tuple-element.251.refs_0_, f32[2,16,96]{2,1,0:T(8,128)S(1)} %select_maximum_fusion.refs_1_, bf16[96,768]{1,0:T(8,128)(2,1)S(1)} %multiply_convert_fusion.6.refs_2_, ...), custom_call_target="tpu_custom_call" | custom-call | tf_op jit(solution)/shard_map/share_all/pallas_call | solution.py:1304
  346.7 20.5 %shard_map.300 = (bf16[1536,768]{1,0:T(8,128)(2,1)}, bf16[384,1536]{1,0:T(8,128)(2,1)}) custom-call(s32[8]{0:T(128)} %reshape.745.spans_ref, bf16[1536,768]{1,0:T(8,128)(2,1)} %bitcast.267, bf16[384,1536]{1,0:T(8,128)(2,1)} %convolution_convert_fusion.2.k_ref.v_ref, bf16[384,1536]{1,0:T(8,128)(2,1)} %convolution_convert_fusion.2.k_ref.v_ref, ...), custom_call_target="tpu_custom_call" | custom-call | flops 1509949440 | bytes 4718592 | tf_op jit(solution)/shard_map/pallas_call | solution.py:350
  367.2 3.5 fusion.86
  370.7 4.8 all-to-all-start
  375.5 6.2 multiply_convert_fusion.refs_18_
  386.9 23.7 %shard_map.301 = (bf16[384,768]{1,0:T(8,128)(2,1)}, bf16[384,1536]{1,0:T(8,128)(2,1)}, bf16[384,1536]{1,0:T(8,128)(2,1)}, bf16[384,1536]{1,0:T(8,128)(2,1)}, f32[12,640,128]{2,1,0:T(8,128)}) custom-call(s32[6]{0:T(128)} %reshape.751.spans_ref, bf16[384,2304]{1,0:T(8,128)(2,1)} %copy-done.36, bf16[1152,1536]{1,0:T(8,128)(2,1)} %bitcast.262, ...), custom_call_target="tpu_custom_call" | custom-call | flops 1132462080 | bytes 14155776 | tf_op jit(solution)/shard_map/pallas_call | solution.py:350
  411.9 4.2 collective-permute-start.1
  423.0 5.4 fusion
  429.8 4.0 fusion.34
  434.8 3.3 convert_add_fusion
  438.2 3.7 reduce-scatter.2.cloned.1.call-done.refs_22_
  441.9 5.2 fusion.17
  453.5 6.2 shard_map.302
  461.9 5.2 fusion.82
  467.9 149.4 %reduce_all.1 = (f32[48,384]{1,0:T(8,128)}, f32[48,768]{1,0:T(8,128)}, f32[48,384]{1,0:T(8,128)}, f32[48,384]{1,0:T(8,128)}, f32[48,768]{1,0:T(8,128)}, /*index=...) custom-call(bf16[96,768]{1,0:T(8,128)(2,1)} %copy-done.52, ...), custom_call_target="tpu_custom_call" | custom-call | tf_op jit(solution)/shard_map/reduce_all/pallas_call | solution.py:963
  (411 shorter events, 105.4 us)
Async XLA Ops:
  7.2 288.1 %all-gather.2.cloned.1.call-start = ((), (), s32[]{:S(2)}) async-start(), calls=%async_computation.2 | async-start | bytes 5308416 | tf_op jit(solution)/shard_map/all_gather | solution.py:1521
  12.3 64.2 %copy-start.120 = (f32[96]{0:T(128)}, f32[96]{0:T(128)S(1)}, u32[]{:S(2)}) copy-start(f32[96]{0:T(128)S(1)} %fusion.53) | copy-start | bytes 1156
  76.5 17.6 %copy-start.87 = (f32[768]{0:T(1024)}, f32[768]{0:T(1024)S(1)}, u32[]{:S(2)}) copy-start(f32[768]{0:T(1024)S(1)} %get-tuple-element.203) | copy-start | bytes 9220
  95.1 104.3 %copy-start.93 = (s32[1,6144]{1,0:T(1,128)S(1)}, s32[1,6144]{1,0:T(1,128)}, u32[]{:S(2)}) copy-start(s32[1,6144]{1,0:T(1,128)} %param.20) | copy-start | bytes 73732
  199.1 19.1 %copy-start.23 = (bf16[2,2,2,2,48,768]{5,4,3,2,1,0:T(8,128)(2,1)}, bf16[2,2,2,2,48,768]{5,4,3,2,1,0:T(8,128)(2,1)S(1)}, u32[]{:S(2)}) copy-start(bf16[2,2,2,2,48,768]{5,4,3,2,1,0:T(8,128)(2,1)S(1)} %get-tuple-element.84) | copy-start | bytes 3538948
  199.1 242.8 %reduce-scatter.2.cloned.1.call-start = ((), (), s32[]{:S(2)}) async-start(), calls=%async_computation.3 | async-start | bytes 3538944 | tf_op jit(solution)/shard_map/reduce_scatter | solution.py:1597
  203.6 14.6 %copy-start.43 = (bf16[1,384,768]{2,1,0:T(8,128)(2,1)S(1)}, bf16[1,384,768]{2,1,0:T(8,128)(2,1)}, u32[]{:S(2)}) copy-start(bf16[1,384,768]{2,1,0:T(8,128)(2,1)} %param.18) | copy-start | bytes 1769476
  220.0 10.0 %copy-start.96 = (f32[384]{0:T(512)}, f32[384]{0:T(512)S(1)}, u32[]{:S(2)}) copy-start(f32[384]{0:T(512)S(1)} %get-tuple-element.243) | copy-start | bytes 4612
  220.0 10.0 %copy-start.37 = (f32[384,768]{1,0:T(8,128)}, f32[384,768]{1,0:T(8,128)S(1)}, u32[]{:S(2)}) copy-start(f32[384,768]{1,0:T(8,128)S(1)} %get-tuple-element.244) | copy-start | bytes 3538948
  220.8 9.2 %slice-start = ((s8[4718592]{0:T(1024)(128)(4,1)}), s8[4194304]{0:T(1024)(128)(4,1)S(1)}, s32[]{:S(2)}) async-start(s8[4718592]{0:T(1024)(128)(4,1)} %bitcast.270), calls=%async_computation.4 | async-start | bytes 8388608
  221.0 9.0 %copy-start.49 = (bf16[384,768]{1,0:T(8,128)(2,1)}, bf16[384,768]{1,0:T(8,128)(2,1)S(1)}, u32[]{:S(2)}) copy-start(bf16[384,768]{1,0:T(8,128)(2,1)S(1)} %multiply_convert_fusion.5.refs_7_) | copy-start | bytes 1769476
  221.0 9.0 %slice-start.1 = ((s8[4718592]{0:T(1024)(128)(4,1)}), s8[524288]{0:T(1024)(128)(4,1)S(1)}, s32[]{:S(2)}) async-start(s8[4718592]{0:T(1024)(128)(4,1)} %bitcast.270), calls=%async_computation.5 | async-start | bytes 1048576
  250.5 44.8 %copy-start.122 = (pred[8]{0:T(512)(128)(4,1)S(1)}, pred[8]{0:T(512)(128)(4,1)}, u32[]{:S(2)}) copy-start(pred[8]{0:T(512)(128)(4,1)} %constant.189.clone.1) | copy-start | bytes 28
  294.7 17.5 %copy-start.117 = (f32[96]{0:T(128)}, f32[96]{0:T(128)S(1)}, u32[]{:S(2)}) copy-start(f32[96]{0:T(128)S(1)} %compare_convert_fusion) | copy-start | bytes 1156
  297.7 8.1 %copy-start.40 = (f32[96,768]{1,0:T(8,128)S(1)}, f32[96,768]{1,0:T(8,128)}, u32[]{:S(2)}) copy-start(f32[96,768]{1,0:T(8,128)} %copy-done.39) | copy-start | bytes 884740
  308.2 121.6 %copy-start.5 = (bf16[96,3072]{1,0:T(8,128)(2,1)}, bf16[96,3072]{1,0:T(8,128)(2,1)S(1)}, u32[]{:S(2)}) copy-start(bf16[96,3072]{1,0:T(8,128)(2,1)S(1)} %get-tuple-element.247.refs_4_.refs_10_) | copy-start | bytes 1769476
  346.7 20.5 %copy-start.34 = (bf16[2,2,2,2,48,1536]{5,4,3,2,1,0:T(8,128)(2,1)S(1)}, bf16[2,2,2,2,48,1536]{5,4,3,2,1,0:T(8,128)(2,1)}, u32[]{:S(2)}) copy-start(bf16[2,2,2,2,48,1536]{5,4,3,2,1,0:T(8,128)(2,1)} %copy-done.32) | copy-start | bytes 7077892
  370.7 11.0 %slice-start.2 = ((s8[4718592]{0:T(1024)(128)(4,1)}), s8[524288]{0:T(1024)(128)(4,1)S(1)}, s32[]{:S(2)}) async-start(s8[4718592]{0:T(1024)(128)(4,1)} %bitcast.294), calls=%async_computation.6 | async-start | bytes 1048576
  370.7 67.5 %all-to-all-start = ((bf16[16,96,768]{2,1,0:T(8,128)(2,1)}), bf16[16,96,768]{2,1,0:T(8,128)(2,1)}, u32[]{:S(2)}, u32[]{:S(2)}) async-start(bf16[16,96,768]{2,1,0:T(8,128)(2,1)} %bitcast.306), calls=%async_computation | async-start | bytes 4718592 | tf_op jit(solution)/shard_map/all_to_all | solution.py:1615
  386.9 29.3 %copy-start.101 = (s32[640]{0:T(1024)S(1)}, s32[640]{0:T(1024)}, u32[]{:S(2)}) copy-start(s32[640]{0:T(1024)} %iota_add_fusion) | copy-start | bytes 7684
  386.9 29.7 %copy-start.91 = (f32[2,2,2,96]{3,2,1,0:T(2,128)S(1)}, f32[2,2,2,96]{3,2,1,0:T(2,128)}, u32[]{:S(2)}) copy-start(f32[2,2,2,96]{3,2,1,0:T(2,128)} %copy-done.90) | copy-start | bytes 9220
  410.6 23.1 %collective-permute-start = (bf16[384,1536]{1,0:T(8,128)(2,1)}, bf16[384,1536]{1,0:T(8,128)(2,1)S(1)}, u32[]{:S(2)}, u32[]{:S(2)}) collective-permute-start(bf16[384,1536]{1,0:T(8,128)(2,1)} %get-tuple-element.104), channel_id=1, source_target_pairs={{1,0},{2,1},{3,2},{4,3},{5,4},{6,5},{7,6},{8,7},{9,8},{10,9},{11,1... | collective-permute-start | bytes 3538952 | tf_op jit(solution)/shard_map/ppermute | solution.py:1635
  411.9 21.9 %collective-permute-start.1 = (bf16[384,1536]{1,0:T(8,128)(2,1)}, bf16[384,1536]{1,0:T(8,128)(2,1)}, u32[]{:S(2)}, u32[]{:S(2)}) collective-permute-start(bf16[384,1536]{1,0:T(8,128)(2,1)} %get-tuple-element.105), channel_id=1, source_target_pairs={{0,1},{1,2},{2,3},{3,4},{4,5},{5,6},{6,7},{7,8},{8,9},{9,10},{10,1... | collective-permute-start | bytes 3538952 | tf_op jit(solution)/shard_map/ppermute | solution.py:1636
  453.5 8.4 %copy-start.31 = (bf16[2,2,2,2,48,1536]{5,4,3,2,1,0:T(8,128)(2,1)S(1)}, bf16[2,2,2,2,48,1536]{5,4,3,2,1,0:T(8,128)(2,1)}, u32[]{:S(2)}) copy-start(bf16[2,2,2,2,48,1536]{5,4,3,2,1,0:T(8,128)(2,1)} %copy-done.29) | copy-start | bytes 7077892
  (110 other events, 348.0 us)
Sparse Core Ops, SparseCore 0:
  199.2 94.2 all-gather.1
  346.8 95.0 reduce-scatter.1

commit v5 on v4

--- a/solution.py
+++ b/solution.py
@@ -738,15 +738,16 @@
     return (2,) * len(left) + (chunk[2], width)
 
 
-def reduce_kernel(plan, count, *refs):
+def reduce_kernel(plan, count, places, *refs):
     lefts = refs[:count]
     rights = refs[count : 2 * count]
     late_rows, small_in, rows_in = refs[2 * count : 2 * count + 3]
     refs = refs[2 * count + 3 :]
-    outs = refs[:count]
-    late_outs = refs[count : count + 2]
-    small_out, rows_out = refs[count + 2 : count + 4]
-    scratch = list(refs[count + 4 :])
+    made = 1 + max(place for place, lead in places)
+    outs = refs[:made]
+    late_outs = refs[made : made + 2]
+    small_out, rows_out = refs[made + 2 : made + 4]
+    scratch = list(refs[made + 4 :])
     late = len(LATE_SUMS)
     send_sem, recv_sem, small_acc, small_recv, ring_low, ring_tall = scratch[:6]
     rows_held = [rows_in] + scratch[6:9]
@@ -845,8 +846,12 @@
             else:
                 kept = held[item][stage - 1][index[:at] + (bit,) + index[at:]]
             if stage == 4:
-                out = outs[chunk[0]]
-                out[:, pl.ds(chunk[1], chunk[4])] = kept.astype(f32) + target[...].astype(f32)
+                place, lead = places[chunk[0]]
+                total = kept.astype(f32) + target[...].astype(f32)
+                if lead is None:
+                    outs[place][:, pl.ds(chunk[1], chunk[4])] = total
+                else:
+                    outs[place][lead + chunk[1] // HALF] = total
             else:
                 target[index] = kept + target[index]
             return 0
@@ -939,11 +944,15 @@
             stage_copy(item, stage).wait_send()
 
 
-def reduce_all(factors, late, small, rows):
+def reduce_all(factors, places, late, small, rows):
     lefts = [left for left, right in factors]
     rights = [right for left, right in factors]
     shapes = [(left.shape[1] // 16, right.shape[1]) for left, right in factors]
     plan = reduce_plan(shapes)
+    made = {}
+    for (place, lead), (part, columns) in zip(places, shapes):
+        made[place] = (part, columns // 2) if lead is None else (3, part, HALF)
+    made = [made[place] for place in range(len(made))]
     scratch = [
         pltpu.SemaphoreType.DMA((len(plan) + 2 + len(LATE_SUMS), 5)),
         pltpu.SemaphoreType.DMA((len(plan) + 2 + len(LATE_SUMS), 5)),
@@ -961,10 +970,10 @@
         scratch += [pltpu.VMEM(buffer_shape(chunk, h), bf16) for h in shapes_held]
     near = pl.BlockSpec(memory_space=pltpu.VMEM)
     results = pl.pallas_call(
-        functools.partial(reduce_kernel, plan, len(factors)),
+        functools.partial(reduce_kernel, plan, len(factors), places),
         in_specs=[near] * (2 * len(factors) + 3),
-        out_specs=[near] * (len(factors) + 4),
-        out_shape=[jax.ShapeDtypeStruct((rows, columns // 2), f32) for rows, columns in shapes]
+        out_specs=[near] * (len(made) + 4),
+        out_shape=[jax.ShapeDtypeStruct(shape, f32) for shape in made]
         + [jax.ShapeDtypeStruct(shape, f32) for shape in late_shapes]
         + [jax.ShapeDtypeStruct((SMALL, D), f32), jax.ShapeDtypeStruct((own_rows, D), f32)],
         scratch_shapes=scratch,
@@ -973,7 +982,7 @@
         ),
         name="reduce_all",
     )(*lefts, *rights, late, small, rows.reshape(2, 2, 2, own_rows, D))
-    return results[: len(factors)], results[len(factors) : -2], results[-2], results[-1]
+    return results[: len(made)], results[len(made) : -2], results[-2], results[-1]
 
 
 MERGE = ((CORE, ROW, LOW, HIGH), (CORE, LOW, HIGH, ROW))
@@ -1675,12 +1684,14 @@
         (normed_one, enc_grad_b),
         (dec_active, columns_of(EARLY, wide) if here else grad_final_b),
     )
+    places = ((0, None), (1, 1), (1, 0), (2, None), (3, 1), (3, 0))
+    places = places + ((4, None), (5, None), (6, None), (7, 0), (8, None))
     gains_part = jnp.concatenate([grad_enc_gains, grad_dec_gains], axis=0)
     if here:
         table_row = jnp.pad(table_part.reshape(1, -1), ((0, 0), (0, D - BUCKETS * HEADS)))
         small = jnp.concatenate([gains_part, table_row], axis=0)
         small = jnp.pad(small, ((0, SMALL - small.shape[0]), (0, 0)))
-        sums, late, small, grad_normed = reduce_all(factors, late, small, grad_group_b)
+        sums, late, small, grad_normed = reduce_all(factors, places, late, small, grad_group_b)
         gains_total = small[:5]
         table_grad = small[5, : BUCKETS * HEADS].reshape(BUCKETS, HEADS)
     else:
@@ -1695,23 +1706,28 @@
     def threes(rows):
         return rows.reshape(part, -1, wide).transpose(1, 0, 2)
 
+    if not here:
+        cross = jnp.concatenate([sums[2][None], threes(sums[1])], axis=0)
+        own = jnp.concatenate([sums[5][None], threes(sums[4])], axis=0)
+        sums = [sums[0], cross, sums[3], own, *sums[6:9], threes(sums[9]), sums[10]]
+
     return (
         dec_output[None],
         grad_enc_in[None],
         grad_dec_in[None],
         gains_total[:2],
-        threes(sums[9]),
-        sums[8],
-        table_grad,
         sums[7],
         sums[6],
+        table_grad,
+        sums[5],
+        sums[4],
         gains_total[2:],
-        jnp.concatenate([sums[5][None], threes(sums[4])], axis=0),
         sums[3],
-        jnp.concatenate([sums[2][None], threes(sums[1])], axis=0),
+        sums[2],
+        sums[1],
         sums[0],
         late[0],
-        jnp.concatenate([late[1], sums[10]], axis=1) if here else sums[10],
+        jnp.concatenate([late[1], sums[8]], axis=1) if here else sums[8],
     )
 
 

time: 650 us -> 650 us (level)
    unnamed x271 -> x269, local copies, waits for them, and re-layouts: 40.3 us -> 41.9 us
  transfers between devices with their start and end apart: 5 -> 5, of which waited for: 1 -> 1; matrix products, arithmetic and copies ran while one was open for 9% -> 9% of each run, Pallas kernels for 18% -> 17%
where the time goes in v5:
time: 650 us; the launch traced here: 641 us
  Pallas kernels  458 us (70%)
  matrix products  65.9 us (10%)
  local copies, waits for them, and re-layouts  56.1 us (9%)
  other arithmetic  27.5 us (4%)
  between operations  16.1 us (2%)
  starting transfers between devices  13 us (2%)
    pallas_call x2, Pallas kernels, spread(): pl.pallas_call(functools.partial(spread_kernel, plan, len(shards), len(la...  151 us
    pallas_call x1, Pallas kernels, reduce_all(): pl.pallas_call(functools.partial(reduce_kernel, plan, len(factors), place...  149 us
    pallas_call x3, Pallas kernels, attend_back(): pl.pallas_call(functools.partial(attend_back_kernel, causal, bias is not...  47.1 us
    pallas_call x1, Pallas kernels, merge_all(): pl.pallas_call(merge_kernel, in_specs=[near, near], out_specs=[near, near...  45.1 us
    unnamed x269, local copies, waits for them, and re-layouts  41.9 us
    dot_general x12, matrix products, back_of(): lax.dot_general(gradient, weight, (((1,), (1,)), ((), ())), preferred_ele...  32.1 us
    pallas_call x3, Pallas kernels, attend(): pl.pallas_call(functools.partial(attend_kernel, causal, bias is not None)...  29.8 us
    dot_general x12, matrix products, matmul(): return jnp.dot(left_side, right_side, preferred_element_type=f32)  28.4 us
  transfers between devices with their start and end apart: 5, of which 1 were waited for; matrix products, arithmetic and copies ran while one was open for 9% of the time, Pallas kernels for 17%

profile of v5, /device:TPU:0, one launch (start us, length us, event | category | flops | bytes accessed | tf_op | source)
XLA Modules:
  0.0 641.2 jit_solution(7118628707916825183)
XLA Ops:
  12.3 55.7 %spread.2 = (bf16[2,2,2,2,48,1536]{5,4,3,2,1,0:T(8,128)(2,1)S(1)}, bf16[2,2,2,2,48,768]{5,4,3,2,1,0:T(8,128)(2,1)S(1)}, bf16[2,2,2,2,48,2304]{5,4,3,2,1,0:T(8,12...) custom-call(bf16[48,768]{1,0:T(8,128)(2,1)S(1)} %bitcast.275, ...), custom_call_target="tpu_custom_call" | custom-call | flops 134400000000 | tf_op jit(solution)/shard_map/spread/pallas_call | solution.py:651
  78.9 3.4 convolution_convert_fusion.1.k_ref.v_ref
  83.3 4.5 shard_map.297
  95.2 94.9 %spread.3 = (bf16[2,2,2,2,48,768]{5,4,3,2,1,0:T(8,128)(2,1)S(1)}, bf16[2,2,2,2,48,1536]{5,4,3,2,1,0:T(8,128)(2,1)S(1)}, bf16[2,2,2,2,48,3072]{5,4,3,2,1,0:T(8,12...) custom-call(bf16[48,384]{1,0:T(8,128)(2,1)S(1)} %convert_element_typ, ...), custom_call_target="tpu_custom_call" | custom-call | flops 192000000000 | tf_op jit(solution)/shard_map/spread/pallas_call | solution.py:651
  203.7 12.0 %shard_map.298 = (bf16[384,768]{1,0:T(8,128)(2,1)}, f32[16,384]{1,0:T(8,128)}) custom-call(s32[6]{0:T(128)} %reshape.742.spans_ref, bf16[384,2304]{1,0:T(8,128)(2,1)} %copy-done.36, bf16[1152,1536]{1,0:T(8,128)(2,1)} %bitcast.243, bf16[1152,1536]{1,0:T(8,128)(2,1)} %bitcast.244, s32[3,1,128]{2,1,0:T(1,128)} %get-tuple-element.233.row_ref, ...), custom_call_target="tpu_custom_call" | custom-call | flops 452984832 | bytes 7077888 | tf_op jit(solution)/shard_map/pallas_call | solution.py:176
  219.1 8.9 %fusion.7 = (f32[384,3072]{1,0:T(8,128)}, bf16[384,3072]{1,0:T(8,128)(2,1)S(1)}) fusion(bf16[384,768]{1,0:T(8,128)(2,1)S(1)} %multiply_convert_fusion.5.refs_7_, bf16[768,3072]{1,0:T(8,128)(2,1)} %bitcast.276), kind=kOutput, calls=%fused_computation.10 | convolution fusion | flops 1834352640 | bytes 12386304 | tf_op jit(solution)/shard_map/dot_general | solution.py:63
  232.7 13.4 %shard_map.299 = (bf16[1536,768]{1,0:T(8,128)(2,1)}, f32[16,1536]{1,0:T(8,128)}) custom-call(s32[8]{0:T(128)} %reshape.736.spans_ref, bf16[1536,768]{1,0:T(8,128)(2,1)} %bitcast.249, bf16[384,1536]{1,0:T(8,128)(2,1)} %convolution_convert_fusion.2.k_ref.v_ref, bf16[384,1536]{1,0:T(8,128)(2,1)} %convolution_convert_fusion.2.k_ref.v_ref, ...), custom_call_target="tpu_custom_call" | custom-call | flops 603979776 | bytes 2359296 | tf_op jit(solution)/shard_map/pallas_call | solution.py:176
  248.8 45.1 %merge_all.1 = (f32[96,768]{1,0:T(8,128)S(1)}, f32[2,8,96]{2,1,0:T(8,128)S(1)}) custom-call(bf16[2,2,2,2,96,768]{5,4,3,2,1,0:T(8,128)(2,1)S(1)} %bitcast.267, f32[2,2,2,2,2,8,96]{6,5,4,3,2,1,0:T(8,128)S(1)} %bitcast.271), custom_call_target="tpu_custom_call" | custom-call | tf_op jit(solution)/shard_map/merge_all/pallas_call | solution.py:1161
  297.6 8.0 %pair_all.1 = (bf16[8,2,48,3072]{3,2,1,0:T(8,128)(2,1)S(1)}, bf16[8,2,192,768]{3,2,1,0:T(8,128)(2,1)S(1)}) custom-call(bf16[8,96,3072]{2,1,0:T(8,128)(2,1)S(1)} %bitcast.258), custom_call_target="tpu_custom_call" | custom-call | tf_op jit(solution)/shard_map/pair_all/pallas_call | solution.py:1135
  315.2 28.2 %share_all.1 = (bf16[2,2,2,2,96,768]{5,4,3,2,1,0:T(8,128)(2,1)S(1)}, f32[2,2,2,2,2,16,96]{6,5,4,3,2,1,0:T(8,128)S(1)}, bf16[8,48,4096]{2,1,0:T(8,128)(2,1)}) custom-call(bf16[96,768]{1,0:T(8,128)(2,1)S(1)} %get-tuple-element.247.refs_0_, f32[2,16,96]{2,1,0:T(8,128)S(1)} %select_maximum_fusion.refs_1_, bf16[96,768]{1,0:T(8,128)(2,1)S(1)} %multiply_convert_fusion.6.refs_2_, ...), custom_call_target="tpu_custom_call" | custom-call | tf_op jit(solution)/shard_map/share_all/pallas_call | solution.py:1313
  346.6 20.5 %shard_map.300 = (bf16[1536,768]{1,0:T(8,128)(2,1)}, bf16[384,1536]{1,0:T(8,128)(2,1)}) custom-call(s32[8]{0:T(128)} %reshape.736.spans_ref, bf16[1536,768]{1,0:T(8,128)(2,1)} %bitcast.250, bf16[384,1536]{1,0:T(8,128)(2,1)} %convolution_convert_fusion.2.k_ref.v_ref, bf16[384,1536]{1,0:T(8,128)(2,1)} %convolution_convert_fusion.2.k_ref.v_ref, ...), custom_call_target="tpu_custom_call" | custom-call | flops 1509949440 | bytes 4718592 | tf_op jit(solution)/shard_map/pallas_call | solution.py:350
  367.0 3.5 fusion.86
  370.5 4.8 all-to-all-start
  375.4 6.1 multiply_convert_fusion.refs_18_
  386.7 20.4 %shard_map.301 = (bf16[384,768]{1,0:T(8,128)(2,1)}, bf16[384,1536]{1,0:T(8,128)(2,1)}, bf16[384,1536]{1,0:T(8,128)(2,1)}, bf16[384,1536]{1,0:T(8,128)(2,1)}, f32[12,640,128]{2,1,0:T(8,128)}) custom-call(s32[6]{0:T(128)} %reshape.742.spans_ref, bf16[384,2304]{1,0:T(8,128)(2,1)} %copy-done.36, bf16[1152,1536]{1,0:T(8,128)(2,1)} %bitcast.245, ...), custom_call_target="tpu_custom_call" | custom-call | flops 1132462080 | bytes 14155776 | tf_op jit(solution)/shard_map/pallas_call | solution.py:350
  408.4 6.6 %collective-permute-start.1 = (bf16[384,1536]{1,0:T(8,128)(2,1)}, bf16[384,1536]{1,0:T(8,128)(2,1)}, u32[]{:S(2)}, u32[]{:S(2)}) collective-permute-start(bf16[384,1536]{1,0:T(8,128)(2,1)} %get-tuple-element.103), channel_id=1, source_target_pairs={{0,1},{1,2},{2,3},{3,4},{4,5},{5,6},{6,7},{7,8},{8,9},{9,10},{10,1... | collective-permute-start | bytes 3538952 | tf_op jit(solution)/shard_map/ppermute | solution.py:1645
  422.0 5.4 fusion
  428.8 4.0 fusion.34
  433.9 3.4 convert_add_fusion
  437.2 4.5 reduce-scatter.2.cloned.1.call-done.refs_22_
  441.8 5.2 fusion.17
  453.4 6.2 shard_map.302
  461.8 5.2 fusion.82
  467.8 149.2 %reduce_all.1 = (f32[48,384]{1,0:T(8,128)}, f32[3,48,384]{2,1,0:T(8,128)}, f32[48,384]{1,0:T(8,128)}, f32[3,48,384]{2,1,0:T(8,128)}, f32[192,384]{1,0:T(8,128)},...) custom-call(bf16[96,768]{1,0:T(8,128)(2,1)} %copy-done.52, ...), custom_call_target="tpu_custom_call" | custom-call | tf_op jit(solution)/shard_map/reduce_all/pallas_call | solution.py:972
  (404 shorter events, 105.9 us)
Async XLA Ops:
  7.2 288.0 %all-gather.2.cloned.1.call-start = ((), (), s32[]{:S(2)}) async-start(), calls=%async_computation.2 | async-start | bytes 5308416 | tf_op jit(solution)/shard_map/all_gather | solution.py:1530
  12.3 64.3 %copy-start.118 = (f32[96]{0:T(128)}, f32[96]{0:T(128)S(1)}, u32[]{:S(2)}) copy-start(f32[96]{0:T(128)S(1)} %fusion.53) | copy-start | bytes 1156
  76.5 17.7 %copy-start.85 = (f32[768]{0:T(1024)}, f32[768]{0:T(1024)S(1)}, u32[]{:S(2)}) copy-start(f32[768]{0:T(1024)S(1)} %get-tuple-element.199) | copy-start | bytes 9220
  95.2 104.3 %copy-start.91 = (s32[1,6144]{1,0:T(1,128)S(1)}, s32[1,6144]{1,0:T(1,128)}, u32[]{:S(2)}) copy-start(s32[1,6144]{1,0:T(1,128)} %param.20) | copy-start | bytes 73732
  199.2 17.0 %copy-start.23 = (bf16[2,2,2,2,48,768]{5,4,3,2,1,0:T(8,128)(2,1)}, bf16[2,2,2,2,48,768]{5,4,3,2,1,0:T(8,128)(2,1)S(1)}, u32[]{:S(2)}) copy-start(bf16[2,2,2,2,48,768]{5,4,3,2,1,0:T(8,128)(2,1)S(1)} %get-tuple-element.82) | copy-start | bytes 3538948
  199.2 242.5 %reduce-scatter.2.cloned.1.call-start = ((), (), s32[]{:S(2)}) async-start(), calls=%async_computation.3 | async-start | bytes 3538944 | tf_op jit(solution)/shard_map/reduce_scatter | solution.py:1606
  203.6 12.6 %copy-start.43 = (bf16[1,384,768]{2,1,0:T(8,128)(2,1)S(1)}, bf16[1,384,768]{2,1,0:T(8,128)(2,1)}, u32[]{:S(2)}) copy-start(bf16[1,384,768]{2,1,0:T(8,128)(2,1)} %param.18) | copy-start | bytes 1769476
  218.0 10.0 %copy-start.94 = (f32[384]{0:T(512)}, f32[384]{0:T(512)S(1)}, u32[]{:S(2)}) copy-start(f32[384]{0:T(512)S(1)} %get-tuple-element.239) | copy-start | bytes 4612
  218.0 10.0 %copy-start.37 = (f32[384,768]{1,0:T(8,128)}, f32[384,768]{1,0:T(8,128)S(1)}, u32[]{:S(2)}) copy-start(f32[384,768]{1,0:T(8,128)S(1)} %get-tuple-element.240) | copy-start | bytes 3538948
  218.9 9.2 %slice-start = ((s8[4718592]{0:T(1024)(128)(4,1)}), s8[4194304]{0:T(1024)(128)(4,1)S(1)}, s32[]{:S(2)}) async-start(s8[4718592]{0:T(1024)(128)(4,1)} %bitcast.253), calls=%async_computation.4 | async-start | bytes 8388608
  219.1 9.0 %slice-start.1 = ((s8[4718592]{0:T(1024)(128)(4,1)}), s8[524288]{0:T(1024)(128)(4,1)S(1)}, s32[]{:S(2)}) async-start(s8[4718592]{0:T(1024)(128)(4,1)} %bitcast.253), calls=%async_computation.5 | async-start | bytes 1048576
  248.8 46.4 %copy-start.120 = (pred[8]{0:T(512)(128)(4,1)S(1)}, pred[8]{0:T(512)(128)(4,1)}, u32[]{:S(2)}) copy-start(pred[8]{0:T(512)(128)(4,1)} %constant.189.clone.1) | copy-start | bytes 28
  294.6 17.5 %copy-start.115 = (f32[96]{0:T(128)}, f32[96]{0:T(128)S(1)}, u32[]{:S(2)}) copy-start(f32[96]{0:T(128)S(1)} %compare_convert_fusion) | copy-start | bytes 1156
  308.1 120.7 %copy-start.5 = (bf16[96,3072]{1,0:T(8,128)(2,1)}, bf16[96,3072]{1,0:T(8,128)(2,1)S(1)}, u32[]{:S(2)}) copy-start(bf16[96,3072]{1,0:T(8,128)(2,1)S(1)} %get-tuple-element.243.refs_4_.refs_10_) | copy-start | bytes 1769476
  346.6 20.5 %copy-start.34 = (bf16[2,2,2,2,48,1536]{5,4,3,2,1,0:T(8,128)(2,1)S(1)}, bf16[2,2,2,2,48,1536]{5,4,3,2,1,0:T(8,128)(2,1)}, u32[]{:S(2)}) copy-start(bf16[2,2,2,2,48,1536]{5,4,3,2,1,0:T(8,128)(2,1)} %copy-done.32) | copy-start | bytes 7077892
  370.5 11.0 %slice-start.2 = ((s8[4718592]{0:T(1024)(128)(4,1)}), s8[524288]{0:T(1024)(128)(4,1)S(1)}, s32[]{:S(2)}) async-start(s8[4718592]{0:T(1024)(128)(4,1)} %bitcast.277), calls=%async_computation.6 | async-start | bytes 1048576
  370.5 66.7 %all-to-all-start = ((bf16[16,96,768]{2,1,0:T(8,128)(2,1)}), bf16[16,96,768]{2,1,0:T(8,128)(2,1)}, u32[]{:S(2)}, u32[]{:S(2)}) async-start(bf16[16,96,768]{2,1,0:T(8,128)(2,1)} %bitcast.289), calls=%async_computation | async-start | bytes 4718592 | tf_op jit(solution)/shard_map/all_to_all | solution.py:1624
  386.7 28.3 %copy-start.99 = (s32[640]{0:T(1024)S(1)}, s32[640]{0:T(1024)}, u32[]{:S(2)}) copy-start(s32[640]{0:T(1024)} %iota_add_fusion) | copy-start | bytes 7684
  386.7 28.7 %copy-start.89 = (f32[2,2,2,96]{3,2,1,0:T(2,128)S(1)}, f32[2,2,2,96]{3,2,1,0:T(2,128)}, u32[]{:S(2)}) copy-start(f32[2,2,2,96]{3,2,1,0:T(2,128)} %copy-done.88) | copy-start | bytes 9220
  407.1 25.7 %collective-permute-start = (bf16[384,1536]{1,0:T(8,128)(2,1)}, bf16[384,1536]{1,0:T(8,128)(2,1)S(1)}, u32[]{:S(2)}, u32[]{:S(2)}) collective-permute-start(bf16[384,1536]{1,0:T(8,128)(2,1)} %get-tuple-element.102), channel_id=1, source_target_pairs={{1,0},{2,1},{3,2},{4,3},{5,4},{6,5},{7,6},{8,7},{9,8},{10,9},{11,1... | collective-permute-start | bytes 3538952 | tf_op jit(solution)/shard_map/ppermute | solution.py:1644
  408.4 24.4 %collective-permute-start.1 = (bf16[384,1536]{1,0:T(8,128)(2,1)}, bf16[384,1536]{1,0:T(8,128)(2,1)}, u32[]{:S(2)}, u32[]{:S(2)}) collective-permute-start(bf16[384,1536]{1,0:T(8,128)(2,1)} %get-tuple-element.103), channel_id=1, source_target_pairs={{0,1},{1,2},{2,3},{3,4},{4,5},{5,6},{6,7},{7,8},{8,9},{9,10},{10,1... | collective-permute-start | bytes 3538952 | tf_op jit(solution)/shard_map/ppermute | solution.py:1645
  467.8 153.8 %copy-start.119 = (f32[96]{0:T(128)S(1)}, f32[96]{0:T(128)}, u32[]{:S(2)}) copy-start(f32[96]{0:T(128)} %copy-done.118) | copy-start | bytes 1156
  467.8 154.7 %copy-start.93 = (f32[384]{0:T(512)S(1)}, f32[384]{0:T(512)}, u32[]{:S(2)}) copy-start(f32[384]{0:T(512)} %copy-done.92) | copy-start | bytes 4612
  467.8 154.7 %copy-start.117 = (f32[384]{0:T(512)S(1)}, f32[384]{0:T(512)}, u32[]{:S(2)}) copy-start(f32[384]{0:T(512)} %get-tuple-element.193) | copy-start | bytes 4612
  (108 other events, 362.6 us)
Sparse Core Ops, SparseCore 0:
  199.4 94.0 all-gather.1
  346.7 95.0 reduce-scatter.1
